TPU v7x, 512 devices: a whole 4x4x16 slice. The times are simulated.
512 devices in a mesh: row: 32 (over x_hi, z), col: 16 (over x_lo, y, core).
Axes of the slice: x: 4 (x_hi: 2, x_lo: 2; x = x_hi * 2 + x_lo), y: 4, z: 16, core: 2. Of those that a mesh axis runs over, the one named last changes fastest.
Arguments:
- start_block: float32 [1024, 32, 128], P(('col', 'row')), may hold values from -34 to 34
- tile_values: bfloat16 [32, 16, 48, 128, 128], P('row', 'col'), may hold values from -0.078125 to 0.078125
- tile_rows: int32 [32, 16, 48], P('row', 'col'), may hold values from 0 to 31, as said below
- tile_columns: int32 [32, 16, 48], P('row', 'col'), may hold values from 0 to 63, as said below
- diagonal_blocks: bfloat16 [1024, 128, 128], P(('col', 'row')), may hold values from -0.078125 to 0.078125
Outputs:
- basis_block: float32 [1024, 32, 128], P(('col', 'row'))
- alpha_blocks: float32 [2, 32, 32], replicated
- beta_blocks: float32 [2, 32, 32], replicated
Inputs may be any that keep to these rules, and one draw needn't show every extreme that they name: `tile_rows`: each grid position lists 48 distinct stored blocks, ordered by local block row and then local block column, and every local block row holds at least one. Write a block's global index as s * 2 + p with segment s and place p; a block of segments a != b and places p, q is stored exactly when (a < b) equals (p + q even); within one segment exactly when p < q. `tile_columns`: local block columns, obeying the storage rule stated for tile_rows.
All inputs are finite; a program needn't handle non-finite values.
Results may differ from a plain program's by a relative error of at most 0.006.
Values may be sent and summed in bfloat16 or wider, within the bound.
No kernel may reach another device: no remote copies, remote signals or barrier semaphores. Data moves between devices by JAX's collectives and lax.ppermute only.
A program may use at most 64 MiB of HBM per device.

v0:
```python
import math

import jax
import jax.numpy as jnp
from jax import lax
from jax.sharding import PartitionSpec as P

ITERS = 2


highest = lax.Precision.HIGHEST


def gram_of(left_side, right_side):
    return jnp.einsum("bkn,bln->kl", left_side, right_side, precision=highest)


def apply_inverse(factor, vectors):
    inverse = jax.scipy.linalg.solve_triangular(
        factor, jnp.eye(factor.shape[0], dtype=jnp.float32), lower=True
    )
    return jnp.einsum("kl,bln->bkn", inverse, vectors, precision=highest)


def block_sums(selected, products, row_count):
    targets = jnp.arange(row_count, dtype=jnp.int32)
    picker = (targets[:, None] == selected[None, :]).astype(jnp.float32)
    return jnp.dot(picker, products, precision=highest)


def apply_operator(vectors, tile_values, tile_rows, tile_columns, diagonal_blocks):
    narrow = vectors.astype(jnp.bfloat16)
    column_slab = lax.all_gather(narrow, "row", axis=0, tiled=True)
    row_slab = lax.all_gather(narrow, "col", axis=0, tiled=True)
    tile_set = tile_values[0, 0]
    row_list = tile_rows[0, 0]
    column_list = tile_columns[0, 0]
    count_tiles = tile_set.shape[0]
    own_blocks = narrow.shape[0]
    upper_part = jnp.einsum(
        "tkj,tij->tki", column_slab[column_list], tile_set, preferred_element_type=jnp.float32
    ).reshape(count_tiles, -1)
    from_rows = lax.psum_scatter(
        block_sums(row_list, upper_part, own_blocks * lax.axis_size("col")),
        "col",
        scatter_dimension=0,
        tiled=True,
    )
    lower_part = jnp.einsum(
        "tki,tij->tkj", row_slab[row_list], tile_set, preferred_element_type=jnp.float32
    ).reshape(count_tiles, -1)
    from_columns = lax.psum_scatter(
        block_sums(column_list, lower_part, own_blocks * lax.axis_size("row")),
        "row",
        scatter_dimension=0,
        tiled=True,
    )
    diagonal = 0.5 * (
        jnp.einsum("bkj,bij->bki", narrow, diagonal_blocks, preferred_element_type=jnp.float32)
        + jnp.einsum("bki,bij->bkj", narrow, diagonal_blocks, preferred_element_type=jnp.float32)
    )
    return (from_rows + from_columns).reshape(narrow.shape) + diagonal


def local(start_block, tile_values, tile_rows, tile_columns, diagonal_blocks):
    gram_sum = lax.psum(gram_of(start_block, start_block), ("row", "col"))
    factor = jnp.linalg.cholesky(gram_sum)
    current = apply_inverse(factor, start_block)
    previous = current
    alpha_list = []
    beta_list = []
    for iteration in range(ITERS):
        image_block = apply_operator(current, tile_values, tile_rows, tile_columns, diagonal_blocks)
        if iteration > 0:
            image_block = image_block - jnp.einsum(
                "lk,bln->bkn", factor, previous, precision=highest
            )
        projection = lax.psum(gram_of(current, image_block), ("row", "col"))
        residual = image_block - jnp.einsum("lk,bln->bkn", projection, current, precision=highest)
        gram_sum = lax.psum(gram_of(residual, residual), ("row", "col"))
        factor = jnp.linalg.cholesky(gram_sum)
        previous = current
        current = apply_inverse(factor, residual)
        alpha_list.append(projection)
        beta_list.append(factor)
    scaling = math.sqrt(
        current.shape[0] * current.shape[2] * lax.axis_size("row") * lax.axis_size("col")
    )
    return (current * scaling, jnp.stack(alpha_list), jnp.stack(beta_list))


def solution(mesh):
    placed = (
        P(("col", "row"), None, None),
        P("row", "col", None, None, None),
        P("row", "col", None),
        P("row", "col", None),
        P(("col", "row"), None, None),
    )
    return jax.shard_map(
        local,
        mesh=mesh,
        in_specs=placed,
        out_specs=(P(("col", "row"), None, None), P(), P()),
        check_vma=False,
    )
```

profile of v0, /device:TPU:1, one launch (start us, length us, event | category | flops | bytes accessed | tf_op | source)
XLA Modules:
  0.0 1589.4 jit_solution(11109363097400997131)
XLA Ops:
  7.2 1.0 convolution_bitcast_fusion.12
  8.3 111.1 %psum.35 = f32[32,32]{0,1:T(8,128)S(1)} all-reduce(f32[32,32]{0,1:T(8,128)S(1)} %convolution_bitcast_fusion.12), channel_id=1, replica_groups=mesh['row'=32,'col'=16] {'row','col'}, use_global_device_ids=true, to_apply=%region_0.0 | all-reduce | flops 1024 | bytes 8192 | tf_op jit(solution)/shard_map/psum | solution.py:66
  119.5 2.9 cholesky.59
  122.4 0.6 compare_reduce_fusion.2
  123.1 0.7 fusion.33
  123.7 2.4 custom-call.7
  126.4 0.9 fusion.56
  127.3 61.3 %all_gather.12 = bf16[64,32,128]{2,1,0:T(8,128)(2,1)S(1)} all-gather(bf16[2,32,128]{2,1,0:T(8,128)(2,1)S(1)} %get-tuple-element.9), channel_id=1, replica_groups=mesh['row'=32,'col'=16] {'row'}, dimensions={0}, use_global_device_ids=true | all-gather | bytes 540672 | tf_op jit(solution)/shard_map/all_gather | solution.py:33
  188.6 0.7 fusion.52
  189.3 0.6 gather_fusion
  189.9 0.9 fusion.6
  190.9 1.7 fusion.25
  192.7 31.9 %all_gather.13 = bf16[32,32,128]{2,1,0:T(8,128)(2,1)S(1)} all-gather(bf16[2,32,128]{2,1,0:T(8,128)(2,1)S(1)} %get-tuple-element.9), channel_id=1, replica_groups=mesh['row'=32,'col'=16] {'col'}, dimensions={0}, use_global_device_ids=true | all-gather | bytes 278528 | tf_op jit(solution)/shard_map/all_gather | solution.py:34
  224.5 0.6 gather_fusion.1
  225.2 0.5 fusion.4
  225.8 2.1 fusion.22
  228.0 1.3 dynamic-slice
  229.3 1.3 dynamic-slice.2
  232.0 96.1 %all-reduce.9.cloned.1.call-done = f32[32,4096]{1,0:T(8,128)} async-done(((f32[32,4096]{1,0:T(8,128)}), f32[32,4096]{1,0:T(8,128)}) %all-reduce.9.cloned.1.call-update) | async-done | bytes 524304
  328.2 285.2 %all-reduce.11.cloned.1.call-done = f32[64,4096]{1,0:T(8,128)} async-done(((f32[64,4096]{1,0:T(8,128)}), f32[64,4096]{1,0:T(8,128)}) %all-reduce.11.cloned.1.call-update) | async-done | bytes 1048592
  613.4 1.0 fusion.29
  614.7 122.1 %psum.36 = f32[32,32]{1,0:T(8,128)S(1)} all-reduce(f32[32,32]{1,0:T(8,128)S(1)} %convolution_bitcast_fusion.10), channel_id=1, replica_groups=mesh['row'=32,'col'=16] {'row','col'}, use_global_device_ids=true, to_apply=%region_5.0 | all-reduce | flops 1024 | bytes 8192 | tf_op jit(solution)/shard_map/psum | solution.py:78
  737.3 99.5 %psum.37 = f32[32,32]{0,1:T(8,128)S(1)} all-reduce(f32[32,32]{0,1:T(8,128)S(1)} %convolution_bitcast_fusion.9), channel_id=1, replica_groups=mesh['row'=32,'col'=16] {'row','col'}, use_global_device_ids=true, to_apply=%region_6.0 | all-reduce | flops 1024 | bytes 8192 | tf_op jit(solution)/shard_map/psum | solution.py:80
  836.8 2.9 cholesky.70
  839.8 0.6 compare_reduce_fusion.1
  840.4 0.7 fusion.46
  841.1 2.4 custom-call.8
  843.9 18.6 %all_gather.15 = bf16[32,32,128]{2,1,0:T(8,128)(2,1)S(1)} all-gather(bf16[2,32,128]{2,1,0:T(8,128)(2,1)S(1)} %get-tuple-element.11), channel_id=1, replica_groups=mesh['row'=32,'col'=16] {'col'}, dimensions={0}, use_global_device_ids=true | all-gather | bytes 278528 | tf_op jit(solution)/shard_map/all_gather | solution.py:34
  862.5 62.2 %all_gather.14 = bf16[64,32,128]{2,1,0:T(8,128)(2,1)S(1)} all-gather(bf16[2,32,128]{2,1,0:T(8,128)(2,1)S(1)} %get-tuple-element.11), channel_id=1, replica_groups=mesh['row'=32,'col'=16] {'row'}, dimensions={0}, use_global_device_ids=true | all-gather | bytes 540672 | tf_op jit(solution)/shard_map/all_gather | solution.py:33
  924.8 0.6 gather_fusion.3
  925.4 0.6 gather_fusion.2
  926.0 0.9 fusion.2
  926.9 1.7 fusion.19
  928.7 0.5 fusion
  929.3 2.1 fusion.16
  931.6 132.8 %all-reduce.13.cloned.1.call-done = f32[32,4096]{1,0:T(8,128)} async-done(((f32[32,4096]{1,0:T(8,128)}), f32[32,4096]{1,0:T(8,128)}) %all-reduce.13.cloned.1.call-update) | async-done | bytes 524304
  1064.3 285.1 %all-reduce.15.cloned.1.call-done = f32[64,4096]{1,0:T(8,128)} async-done(((f32[64,4096]{1,0:T(8,128)}), f32[64,4096]{1,0:T(8,128)}) %all-reduce.15.cloned.1.call-update) | async-done | bytes 1048592
  1349.4 1.0 fusion.28
  1350.6 0.9 fusion.10
  1351.6 122.3 %psum.38 = f32[32,32]{1,0:T(8,128)S(1)} all-reduce(f32[32,32]{1,0:T(8,128)S(1)} %convolution_bitcast_fusion.7), channel_id=1, replica_groups=mesh['row'=32,'col'=16] {'row','col'}, use_global_device_ids=true, to_apply=%region_9.12 | all-reduce | flops 1024 | bytes 8192 | tf_op jit(solution)/shard_map/psum | solution.py:78
  1474.3 99.5 %psum.39 = f32[32,32]{0,1:T(8,128)S(1)} all-reduce(f32[32,32]{0,1:T(8,128)S(1)} %convolution_bitcast_fusion.6), channel_id=1, replica_groups=mesh['row'=32,'col'=16] {'row','col'}, use_global_device_ids=true, to_apply=%region_10.13 | all-reduce | flops 1024 | bytes 8192 | tf_op jit(solution)/shard_map/psum | solution.py:80
  1573.9 2.9 cholesky.81
  1576.8 0.6 compare_reduce_fusion
  1577.5 0.7 fusion.45
  1578.1 2.4 custom-call.9
  1580.8 0.8 fusion.8
  1581.6 0.6 pad_maximum_fusion.1
  1582.2 0.6 pad_maximum_fusion
  (42 shorter events, 3.2 us)
Async XLA Ops:
  7.2 182.8 %copy-start = (bf16[1,1,48,128,128]{4,3,2,1,0:T(8,128)(2,1)S(1)}, bf16[1,1,48,128,128]{4,3,2,1,0:T(8,128)(2,1)}, u32[]{:S(2)}) copy-start(bf16[1,1,48,128,128]{4,3,2,1,0:T(8,128)(2,1)} %param.9) | copy-start | bytes 4718596
  7.2 321.0 %all-reduce.9.cloned.1.call-start = ((), (), s32[]{:S(2)}) async-start(), calls=%async_computation | async-start | bytes 1048576
  189.9 0.9 copy-start.2
  192.6 420.8 %all-reduce.11.cloned.1.call-start = ((), (), s32[]{:S(2)}) async-start(), calls=%async_computation.1 | async-start | bytes 2097152
  225.2 0.7 copy-start.3
  225.7 6.2 copy-start.1
  228.0 836.3 %all-reduce.13.cloned.1.call-start = ((), (), s32[]{:S(2)}) async-start(), calls=%async_computation.2 | async-start | bytes 1048576
  928.7 420.7 %all-reduce.15.cloned.1.call-start = ((), (), s32[]{:S(2)}) async-start(), calls=%async_computation.3 | async-start | bytes 2097152
Sparse Core Ops, SparseCore 0:
  192.7 135.3 all-reduce.8
  331.3 282.0 all-reduce.10
  928.8 135.4 all-reduce.12
  1067.3 282.0 all-reduce.14
where the time goes:
time: 1590 us
  waiting for transfers between devices  799 us (50%)
  blocking collectives  729 us (46%)
  other arithmetic  24 us (2%)
  matrix products  16.7 us (1%)
    unnamed x8, waiting for transfers between devices  799 us
    psum x2, blocking collectives, local(): projection = lax.psum(gram_of(current, image_block), ('row', 'col'))  244 us
    psum x2, blocking collectives, local(): gram_sum = lax.psum(gram_of(residual, residual), ('row', 'col'))  199 us
    all_gather x2, blocking collectives, apply_operator(): column_slab = lax.all_gather(narrow, 'row', axis=0, tiled=True)  124 us
    psum x1, blocking collectives, local(): gram_sum = lax.psum(gram_of(start_block, start_block), ('row', 'col'))  111 us
    all_gather x2, blocking collectives, apply_operator(): row_slab = lax.all_gather(narrow, 'col', axis=0, tiled=True)  50.5 us
  transfers between devices with their start and end apart: 4, of which 4 were waited for; matrix products, arithmetic and copies ran while one was open for 1% of the time, Pallas kernels for 0%

commit v1 on v0

v1 whole, which is shorter than its diff:
```python
import math

import jax
import jax.numpy as jnp
from jax import lax
from jax.sharding import PartitionSpec as P

highest = lax.Precision.HIGHEST


def gram_of(left_side, right_side):
    return jnp.einsum("bkn,bln->kl", left_side, right_side, precision=highest)


def mix(matrix, vectors):
    return jnp.einsum("kl,bln->bkn", matrix, vectors, precision=highest)


def dot(left_side, right_side):
    return jnp.dot(left_side, right_side, precision=highest)


def swap(parts, axis):
    return lax.all_to_all(parts, axis, 0, 0, tiled=True)


def gather(block, axis):
    size = lax.axis_size(axis)
    slab = jnp.broadcast_to(block[None], (size, *block.shape))
    return swap(slab, axis)


def sum_all(stacked):
    partial = jnp.sum(gather(stacked, "col"), axis=0)
    return jnp.sum(gather(partial, "row"), axis=0)


def block_sums(selected, products, row_count):
    targets = jnp.arange(row_count, dtype=jnp.int32)
    picker = (targets[:, None] == selected[None, :]).astype(jnp.float32)
    return jnp.dot(picker, products, precision=highest)


def scatter(sums, axis, shape):
    parts = sums.astype(jnp.bfloat16).reshape(lax.axis_size(axis), *shape)
    return jnp.sum(swap(parts, axis).astype(jnp.float32), axis=0)


def apply_operator(vectors, tile_set, row_list, column_list, diagonal_blocks):
    narrow = vectors.astype(jnp.bfloat16)
    shape = narrow.shape
    own_blocks = shape[0]
    count_tiles = tile_set.shape[0]
    column_slab = gather(narrow, "row").reshape(-1, *shape[1:])
    row_slab = gather(narrow, "col").reshape(-1, *shape[1:])
    lower_part = jnp.einsum(
        "tki,tij->tkj", row_slab[row_list], tile_set, preferred_element_type=jnp.float32
    ).reshape(count_tiles, -1)
    from_columns = scatter(
        block_sums(column_list, lower_part, own_blocks * lax.axis_size("row")), "row", shape
    )
    upper_part = jnp.einsum(
        "tkj,tij->tki", column_slab[column_list], tile_set, preferred_element_type=jnp.float32
    ).reshape(count_tiles, -1)
    from_rows = scatter(
        block_sums(row_list, upper_part, own_blocks * lax.axis_size("col")), "col", shape
    )
    diagonal = 0.5 * (
        jnp.einsum("bkj,bij->bki", narrow, diagonal_blocks, preferred_element_type=jnp.float32)
        + jnp.einsum("bki,bij->bkj", narrow, diagonal_blocks, preferred_element_type=jnp.float32)
    )
    return from_rows + from_columns + diagonal


def factor_of(gram):
    factor = jnp.linalg.cholesky(gram)
    inverse = jax.scipy.linalg.solve_triangular(
        factor, jnp.eye(factor.shape[0], dtype=jnp.float32), lower=True
    )
    return factor, inverse


def local(start_block, tile_values, tile_rows, tile_columns, diagonal_blocks):
    matrix = (tile_values[0, 0], tile_rows[0, 0], tile_columns[0, 0], diagonal_blocks)
    first = apply_operator(start_block, *matrix)
    sums = sum_all(
        jnp.stack(
            [gram_of(start_block, start_block), gram_of(start_block, first), gram_of(first, first)]
        )
    )
    second = apply_operator(first, *matrix)
    _, inverse_start = factor_of(sums[0])
    alpha_first = dot(dot(inverse_start, sums[1]), inverse_start.T)
    image_gram = dot(dot(inverse_start, sums[2]), inverse_start.T)
    beta_first, inverse_first = factor_of(image_gram - dot(alpha_first.T, alpha_first))
    basis_start = mix(inverse_start, start_block)
    image_start = mix(inverse_start, first)
    basis_first = mix(inverse_first, image_start - mix(alpha_first.T, basis_start))
    moved = mix(inverse_start, second) - mix(alpha_first.T, image_start)
    image_first = mix(inverse_first, moved) - mix(beta_first.T, basis_start)
    last = sum_all(jnp.stack([gram_of(basis_first, image_first), gram_of(image_first, image_first)]))
    alpha_last = last[0]
    beta_last, inverse_last = factor_of(last[1] - dot(alpha_last.T, alpha_last))
    basis_last = mix(inverse_last, image_first - mix(alpha_last.T, basis_first))
    scaling = math.sqrt(
        start_block.shape[0] * start_block.shape[2] * lax.axis_size("row") * lax.axis_size("col")
    )
    return (
        basis_last * scaling,
        jnp.stack([alpha_first, alpha_last]),
        jnp.stack([beta_first, beta_last]),
    )


def solution(mesh):
    placed = (
        P(("col", "row"), None, None),
        P("row", "col", None, None, None),
        P("row", "col", None),
        P("row", "col", None),
        P(("col", "row"), None, None),
    )
    return jax.shard_map(
        local,
        mesh=mesh,
        in_specs=placed,
        out_specs=(P(("col", "row"), None, None), P(), P()),
        check_vma=False,
    )
```

time: 1590 us -> 312 us (0.20)
  blocking collectives: 729 us -> 62.3 us
  waiting for transfers between devices: 799 us -> 137 us
  starting transfers between devices: 0.16 us -> 53.8 us
    unnamed x8 -> x0, waiting for transfers between devices: 799 us -> none
    psum x5 -> x0, blocking collectives: 555 us -> none  [the longest x2 244 us: local(): projection = lax.psum(gram_of(current, image_block), ('row', 'col'))]
    all_gather x4 -> x0, blocking collectives: 174 us -> none  [the longest x2 124 us: apply_operator(): column_slab = lax.all_gather(narrow, 'row', axis=0, tiled=True)]
    all_to_all x0 -> x8, waiting for transfers between devices: none -> 137 us  [swap(): return lax.all_to_all(parts, axis, 0, 0, tiled=True)]
    all_to_all x0 -> x4, blocking collectives: none -> 62.3 us  [swap(): return lax.all_to_all(parts, axis, 0, 0, tiled=True)]
    all_to_all x0 -> x8, starting transfers between devices: none -> 53.8 us  [swap(): return lax.all_to_all(parts, axis, 0, 0, tiled=True)]
  transfers between devices with their start and end apart: 4 -> 8, of which waited for: 4 -> 8; matrix products, arithmetic and copies ran while one was open for 1% -> 12% of each run, Pallas kernels for 0% -> 0%
where the time goes in v1:
time: 312 us; the launch traced here: 310 us
  waiting for transfers between devices  137 us (44%)
  blocking collectives  62.3 us (20%)
  starting transfers between devices  53.8 us (17%)
  other arithmetic  27.1 us (9%)
  local copies, waits for them, and re-layouts  15 us (5%)
  matrix products  13.7 us (4%)
    all_to_all x8, waiting for transfers between devices, swap(): return lax.all_to_all(parts, axis, 0, 0, tiled=True)  137 us
    all_to_all x4, blocking collectives, swap(): return lax.all_to_all(parts, axis, 0, 0, tiled=True)  62.3 us
    all_to_all x8, starting transfers between devices, swap(): return lax.all_to_all(parts, axis, 0, 0, tiled=True)  53.8 us
    another operation x9, other arithmetic, factor_of(): factor = jnp.linalg.cholesky(gram)  10.9 us
    another operation x4, other arithmetic, factor_of(): jax.scipy.linalg.solve_triangular(factor, jnp.eye(factor.shape[0], dtype=...  7.95 us
    unnamed x42, local copies, waits for them, and re-layouts  7.49 us
  transfers between devices with their start and end apart: 8, of which 8 were waited for; matrix products, arithmetic and copies ran while one was open for 12% of the time, Pallas kernels for 0%

profile of v1, /device:TPU:1, one launch (start us, length us, event | category | flops | bytes accessed | tf_op | source)
XLA Modules:
  0.0 310.1 jit_solution(6313687436195454852)
XLA Ops:
  0.7 0.9 convert_element_type.43
  1.6 16.5 %all_to_all.60 = bf16[16,2,32,128]{3,2,1,0:T(8,128)(2,1)S(1)} all-to-all(bf16[16,2,32,128]{3,2,1,0:T(8,128)(2,1)S(1)} %broadcast_in_dim.17), channel_id=1, replica_groups=mesh['row'=32,'col'=16] {'col'}, dimensions={0} | all-to-all | bytes 524288 | tf_op jit(solution)/shard_map/all_to_all | solution.py:24
  18.1 0.9 broadcast_in_dim.16
  19.0 14.7 %all-to-all-start = ((bf16[32,2,32,128]{3,2,1,0:T(8,128)(2,1)}), bf16[32,2,32,128]{3,2,1,0:T(8,128)(2,1)S(1)}, u32[]{:S(2)}, u32[]{:S(2)}) async-start(bf16[32,2,32,128]{3,2,1,0:T(8,128)(2,1)} %broadcast_in_dim.16), calls=%async_computation | async-start | bytes 1048576 | tf_op jit(solution)/shard_map/all_to_all | solution.py:24
  35.1 1.1 fusion.8
  36.2 0.9 copy.41
  37.1 28.2 %all-to-all-done = bf16[32,2,32,128]{3,2,1,0:T(8,128)(2,1)S(1)} async-done(((bf16[32,2,32,128]{3,2,1,0:T(8,128)(2,1)}), bf16[32,2,32,128]{3,2,1,0:T(8,128)(2,1)S(1)}, u32[]{:S(2)}, u32[]{:S(2)}) %all-to-all-start) | async-done | bytes 524320 | tf_op jit(solution)/shard_map/all_to_all | solution.py:24
  65.3 6.4 %all-to-all-start.3 = ((bf16[32,2,32,128]{3,2,1,0:T(8,128)(2,1)}), bf16[32,2,32,128]{3,2,1,0:T(8,128)(2,1)S(1)}, u32[]{:S(2)}, u32[]{:S(2)}) async-start(bf16[32,2,32,128]{3,2,1,0:T(8,128)(2,1)} %bitcast.66), calls=%async_computation.3 | async-start | bytes 1048576 | tf_op jit(solution)/shard_map/all_to_all | solution.py:24
  72.6 0.9 fusion.6
  73.5 0.9 fusion.10
  75.2 28.8 %all-to-all-done.3 = bf16[32,2,32,128]{3,2,1,0:T(8,128)(2,1)S(1)} async-done(((bf16[32,2,32,128]{3,2,1,0:T(8,128)(2,1)}), bf16[32,2,32,128]{3,2,1,0:T(8,128)(2,1)S(1)}, u32[]{:S(2)}, u32[]{:S(2)}) %all-to-all-start.3) | async-done | bytes 524320 | tf_op jit(solution)/shard_map/all_to_all | solution.py:24
  104.0 4.8 %all-to-all-start.1 = ((bf16[16,2,32,128]{3,2,1,0:T(8,128)(2,1)}), bf16[16,2,32,128]{3,2,1,0:T(8,128)(2,1)S(1)}, u32[]{:S(2)}, u32[]{:S(2)}) async-start(bf16[16,2,32,128]{3,2,1,0:T(8,128)(2,1)} %bitcast.61), calls=%async_computation.1 | async-start | bytes 524288 | tf_op jit(solution)/shard_map/all_to_all | solution.py:24
  109.0 7.0 %all-to-all-done.1 = bf16[16,2,32,128]{3,2,1,0:T(8,128)(2,1)S(1)} async-done(((bf16[16,2,32,128]{3,2,1,0:T(8,128)(2,1)}), bf16[16,2,32,128]{3,2,1,0:T(8,128)(2,1)S(1)}, u32[]{:S(2)}, u32[]{:S(2)}) %all-to-all-start.1) | async-done | bytes 262176 | tf_op jit(solution)/shard_map/all_to_all | solution.py:24
  117.0 10.1 %all_to_all.61 = f32[16,1,3072]{2,1,0:T(1,128)S(1)} all-to-all(f32[16,1,3072]{2,1,0:T(1,128)S(1)} %reshape.169), channel_id=1, replica_groups=mesh['row'=32,'col'=16] {'col'}, dimensions={0} | all-to-all | bytes 393216 | tf_op jit(solution)/shard_map/all_to_all | solution.py:24
  127.1 0.7 broadcast_in_dim.19
  127.9 4.1 %all-to-all-start.6 = ((bf16[16,2,32,128]{3,2,1,0:T(8,128)(2,1)}), bf16[16,2,32,128]{3,2,1,0:T(8,128)(2,1)S(1)}, u32[]{:S(2)}, u32[]{:S(2)}) async-start(bf16[16,2,32,128]{3,2,1,0:T(8,128)(2,1)} %broadcast_in_dim.19), calls=%async_computation.6 | async-start | bytes 524288 | tf_op jit(solution)/shard_map/all_to_all | solution.py:24
  132.6 1.1 reduce.4
  134.1 1.4 reshape.171
  135.6 3.7 %all-to-all-done.6 = bf16[16,2,32,128]{3,2,1,0:T(8,128)(2,1)S(1)} async-done(((bf16[16,2,32,128]{3,2,1,0:T(8,128)(2,1)}), bf16[16,2,32,128]{3,2,1,0:T(8,128)(2,1)S(1)}, u32[]{:S(2)}, u32[]{:S(2)}) %all-to-all-start.6) | async-done | bytes 262176 | tf_op jit(solution)/shard_map/all_to_all | solution.py:24
  139.3 4.9 %all-to-all-start.9 = ((f32[32,1,3072]{2,1,0:T(1,128)}), f32[32,1,3072]{2,1,0:T(1,128)S(1)}, u32[]{:S(2)}, u32[]{:S(2)}) async-start(f32[32,1,3072]{2,1,0:T(1,128)} %reshape.171), calls=%async_computation.9 | async-start | bytes 786432 | tf_op jit(solution)/shard_map/all_to_all | solution.py:24
  144.2 0.8 fusion.69
  144.9 0.7 gather_fusion.3
  145.7 24.6 %all-to-all-done.9 = f32[32,1,3072]{2,1,0:T(1,128)S(1)} async-done(((f32[32,1,3072]{2,1,0:T(1,128)}), f32[32,1,3072]{2,1,0:T(1,128)S(1)}, u32[]{:S(2)}, u32[]{:S(2)}) %all-to-all-start.9) | async-done | bytes 393248 | tf_op jit(solution)/shard_map/all_to_all | solution.py:24
  170.3 0.9 broadcast_in_dim.18
  171.3 6.5 %all-to-all-start.4 = ((bf16[32,2,32,128]{3,2,1,0:T(8,128)(2,1)}), bf16[32,2,32,128]{3,2,1,0:T(8,128)(2,1)}, u32[]{:S(2)}, u32[]{:S(2)}) async-start(bf16[32,2,32,128]{3,2,1,0:T(8,128)(2,1)} %broadcast_in_dim.18), calls=%async_computation.4 | async-start | bytes 1048576 | tf_op jit(solution)/shard_map/all_to_all | solution.py:24
  178.4 1.1 fusion.9
  179.5 0.9 copy.45
  180.4 1.5 reduce.5
  182.8 2.9 cholesky.59
  187.1 2.4 custom-call.7
  190.4 18.2 %all-to-all-done.4 = bf16[32,2,32,128]{3,2,1,0:T(8,128)(2,1)} async-done(((bf16[32,2,32,128]{3,2,1,0:T(8,128)(2,1)}), bf16[32,2,32,128]{3,2,1,0:T(8,128)(2,1)}, u32[]{:S(2)}, u32[]{:S(2)}) %all-to-all-start.4) | async-done | bytes 524320 | tf_op jit(solution)/shard_map/all_to_all | solution.py:24
  208.5 6.7 %all-to-all-start.7 = ((bf16[32,2,32,128]{3,2,1,0:T(8,128)(2,1)}), bf16[32,2,32,128]{3,2,1,0:T(8,128)(2,1)S(1)}, u32[]{:S(2)}, u32[]{:S(2)}) async-start(bf16[32,2,32,128]{3,2,1,0:T(8,128)(2,1)} %bitcast.209), calls=%async_computation.7 | async-start | bytes 1048576 | tf_op jit(solution)/shard_map/all_to_all | solution.py:24
  215.6 2.9 cholesky.70
  219.9 2.4 custom-call.8
  223.2 1.8 gather_fusion.2
  225.0 0.9 fusion.2
  226.0 0.9 fusion.11
  227.6 19.4 %all-to-all-done.7 = bf16[32,2,32,128]{3,2,1,0:T(8,128)(2,1)S(1)} async-done(((bf16[32,2,32,128]{3,2,1,0:T(8,128)(2,1)}), bf16[32,2,32,128]{3,2,1,0:T(8,128)(2,1)S(1)}, u32[]{:S(2)}, u32[]{:S(2)}) %all-to-all-start.7) | async-done | bytes 524320 | tf_op jit(solution)/shard_map/all_to_all | solution.py:24
  247.0 5.5 %all-to-all-start.5 = ((bf16[16,2,32,128]{3,2,1,0:T(8,128)(2,1)}), bf16[16,2,32,128]{3,2,1,0:T(8,128)(2,1)S(1)}, u32[]{:S(2)}, u32[]{:S(2)}) async-start(bf16[16,2,32,128]{3,2,1,0:T(8,128)(2,1)} %bitcast.71), calls=%async_computation.5 | async-start | bytes 524288 | tf_op jit(solution)/shard_map/all_to_all | solution.py:24
  252.8 7.0 %all-to-all-done.5 = bf16[16,2,32,128]{3,2,1,0:T(8,128)(2,1)S(1)} async-done(((bf16[16,2,32,128]{3,2,1,0:T(8,128)(2,1)}), bf16[16,2,32,128]{3,2,1,0:T(8,128)(2,1)S(1)}, u32[]{:S(2)}, u32[]{:S(2)}) %all-to-all-start.5) | async-done | bytes 262176 | tf_op jit(solution)/shard_map/all_to_all | solution.py:24
  260.6 0.9 fusion.15
  262.2 9.6 %all_to_all.62 = f32[16,1,2048]{2,1,0:T(1,128)S(1)} all-to-all(f32[16,1,2048]{2,1,0:T(1,128)S(1)} %reshape.173), channel_id=1, replica_groups=mesh['row'=32,'col'=16] {'col'}, dimensions={0} | all-to-all | bytes 262144 | tf_op jit(solution)/shard_map/all_to_all | solution.py:24
  271.8 0.9 reduce.6
  273.5 25.9 %all_to_all.63 = f32[32,1,2048]{2,1,0:T(1,128)S(1)} all-to-all(f32[32,1,2048]{2,1,0:T(1,128)S(1)} %reshape.175), channel_id=1, replica_groups=mesh['row'=32,'col'=16] {'row'}, dimensions={0} | all-to-all | bytes 524288 | tf_op jit(solution)/shard_map/all_to_all | solution.py:24
  299.5 1.2 reduce.7
  301.7 2.9 cholesky.81
  306.0 2.4 custom-call.9
  308.7 0.8 fusion.12
  (105 shorter events, 17.6 us)
Async XLA Ops:
  0.6 33.8 %copy-start = (bf16[1,1,48,128,128]{4,3,2,1,0:T(8,128)(2,1)S(1)}, bf16[1,1,48,128,128]{4,3,2,1,0:T(8,128)(2,1)}, u32[]{:S(2)}) copy-start(bf16[1,1,48,128,128]{4,3,2,1,0:T(8,128)(2,1)} %param.9) | copy-start | bytes 4718596
  0.6 33.1 %copy-start.12 = (s32[1,1,48]{2,1,0:T(1,128)S(1)}, s32[1,1,48]{2,1,0:T(1,128)}, u32[]{:S(2)}) copy-start(s32[1,1,48]{2,1,0:T(1,128)} %param.10) | copy-start | bytes 580
  19.0 46.3 %all-to-all-start = ((bf16[32,2,32,128]{3,2,1,0:T(8,128)(2,1)}), bf16[32,2,32,128]{3,2,1,0:T(8,128)(2,1)S(1)}, u32[]{:S(2)}, u32[]{:S(2)}) async-start(bf16[32,2,32,128]{3,2,1,0:T(8,128)(2,1)} %broadcast_in_dim.16), calls=%async_computation | async-start | bytes 1048576 | tf_op jit(solution)/shard_map/all_to_all | solution.py:24
  33.8 1.2 copy-start.9
  34.4 0.7 copy-start.10
  35.1 36.7 %copy-start.1 = (bf16[2,128,128]{2,1,0:T(8,128)(2,1)S(1)}, bf16[2,128,128]{2,1,0:T(8,128)(2,1)}, u32[]{:S(2)}) copy-start(bf16[2,128,128]{2,1,0:T(8,128)(2,1)} %param.12) | copy-start | bytes 196612
  65.3 38.6 %all-to-all-start.3 = ((bf16[32,2,32,128]{3,2,1,0:T(8,128)(2,1)}), bf16[32,2,32,128]{3,2,1,0:T(8,128)(2,1)S(1)}, u32[]{:S(2)}, u32[]{:S(2)}) async-start(bf16[32,2,32,128]{3,2,1,0:T(8,128)(2,1)} %bitcast.66), calls=%async_computation.3 | async-start | bytes 1048576 | tf_op jit(solution)/shard_map/all_to_all | solution.py:24
  71.8 1.7 copy-start.8
  73.5 35.2 %copy-start.3 = (f32[2,32,128]{2,1,0:T(8,128)S(1)}, f32[2,32,128]{2,1,0:T(8,128)}, u32[]{:S(2)}) copy-start(f32[2,32,128]{2,1,0:T(8,128)} %param.8) | copy-start | bytes 98308
  104.0 12.0 %all-to-all-start.1 = ((bf16[16,2,32,128]{3,2,1,0:T(8,128)(2,1)}), bf16[16,2,32,128]{3,2,1,0:T(8,128)(2,1)S(1)}, u32[]{:S(2)}, u32[]{:S(2)}) async-start(bf16[16,2,32,128]{3,2,1,0:T(8,128)(2,1)} %bitcast.61), calls=%async_computation.1 | async-start | bytes 524288 | tf_op jit(solution)/shard_map/all_to_all | solution.py:24
  116.2 11.7 %copy-start.5 = (f32[2,32,128]{2,1,0:T(8,128)}, f32[2,32,128]{2,1,0:T(8,128)S(1)}, u32[]{:S(2)}) copy-start(f32[2,32,128]{2,1,0:T(8,128)S(1)} %get-tuple-element.15) | copy-start | bytes 98308
  127.9 11.4 %all-to-all-start.6 = ((bf16[16,2,32,128]{3,2,1,0:T(8,128)(2,1)}), bf16[16,2,32,128]{3,2,1,0:T(8,128)(2,1)S(1)}, u32[]{:S(2)}, u32[]{:S(2)}) async-start(bf16[16,2,32,128]{3,2,1,0:T(8,128)(2,1)} %broadcast_in_dim.19), calls=%async_computation.6 | async-start | bytes 524288 | tf_op jit(solution)/shard_map/all_to_all | solution.py:24
  139.3 31.1 %all-to-all-start.9 = ((f32[32,1,3072]{2,1,0:T(1,128)}), f32[32,1,3072]{2,1,0:T(1,128)S(1)}, u32[]{:S(2)}, u32[]{:S(2)}) async-start(f32[32,1,3072]{2,1,0:T(1,128)} %reshape.171), calls=%async_computation.9 | async-start | bytes 786432 | tf_op jit(solution)/shard_map/all_to_all | solution.py:24
  171.3 37.3 %all-to-all-start.4 = ((bf16[32,2,32,128]{3,2,1,0:T(8,128)(2,1)}), bf16[32,2,32,128]{3,2,1,0:T(8,128)(2,1)}, u32[]{:S(2)}, u32[]{:S(2)}) async-start(bf16[32,2,32,128]{3,2,1,0:T(8,128)(2,1)} %broadcast_in_dim.18), calls=%async_computation.4 | async-start | bytes 1048576 | tf_op jit(solution)/shard_map/all_to_all | solution.py:24
  177.8 0.7 copy-start.11
  182.5 40.1 %copy-start.6 = (f32[2,32,128]{2,1,0:T(8,128)S(1)}, f32[2,32,128]{2,1,0:T(8,128)}, u32[]{:S(2)}) copy-start(f32[2,32,128]{2,1,0:T(8,128)} %copy-done.5) | copy-start | bytes 98308
  182.5 40.3 %copy-start.4 = (f32[2,32,128]{2,1,0:T(8,128)S(1)}, f32[2,32,128]{2,1,0:T(8,128)}, u32[]{:S(2)}) copy-start(f32[2,32,128]{2,1,0:T(8,128)} %param.8) | copy-start | bytes 98308
  208.5 38.5 %all-to-all-start.7 = ((bf16[32,2,32,128]{3,2,1,0:T(8,128)(2,1)}), bf16[32,2,32,128]{3,2,1,0:T(8,128)(2,1)S(1)}, u32[]{:S(2)}, u32[]{:S(2)}) async-start(bf16[32,2,32,128]{3,2,1,0:T(8,128)(2,1)} %bitcast.209), calls=%async_computation.7 | async-start | bytes 1048576 | tf_op jit(solution)/shard_map/all_to_all | solution.py:24
  225.0 0.9 copy-start.13
  225.9 33.9 %copy-start.2 = (bf16[2,128,128]{2,1,0:T(8,128)(2,1)S(1)}, bf16[2,128,128]{2,1,0:T(8,128)(2,1)}, u32[]{:S(2)}) copy-start(bf16[2,128,128]{2,1,0:T(8,128)(2,1)} %param.12) | copy-start | bytes 196612
  225.9 33.9 %copy-start.7 = (f32[2,32,128]{2,1,0:T(8,128)S(1)}, f32[2,32,128]{2,1,0:T(8,128)}, u32[]{:S(2)}) copy-start(f32[2,32,128]{2,1,0:T(8,128)} %fusion.69) | copy-start | bytes 98308
  247.0 12.8 %all-to-all-start.5 = ((bf16[16,2,32,128]{3,2,1,0:T(8,128)(2,1)}), bf16[16,2,32,128]{3,2,1,0:T(8,128)(2,1)S(1)}, u32[]{:S(2)}, u32[]{:S(2)}) async-start(bf16[16,2,32,128]{3,2,1,0:T(8,128)(2,1)} %bitcast.71), calls=%async_computation.5 | async-start | bytes 524288 | tf_op jit(solution)/shard_map/all_to_all | solution.py:24

commit v2 on v1

--- a/solution.py
+++ b/solution.py
@@ -24,15 +24,29 @@
     return lax.all_to_all(parts, axis, 0, 0, tiled=True)
 
 
-def gather(block, axis):
-    size = lax.axis_size(axis)
-    slab = jnp.broadcast_to(block[None], (size, *block.shape))
-    return swap(slab, axis)
+def copies(rows, count):
+    return jnp.broadcast_to(rows[None], (count, *rows.shape))
+
+
+def pack(values):
+    high = lax.reduce_precision(values, 8, 7)
+    rest = values - high
+    middle = lax.reduce_precision(rest, 8, 7)
+    terms = jnp.stack([high, middle, rest - middle], axis=-2).astype(jnp.bfloat16)
+    widths = [(0, 0)] * (terms.ndim - 2) + [(0, 5), (0, 128 - terms.shape[-1])]
+    return jnp.pad(terms, widths)
+
+
+def unpack(rows, width):
+    terms = rows[..., :3, :width].astype(jnp.float32)
+    return terms[..., 0, :] + (terms[..., 1, :] + terms[..., 2, :])
 
 
 def sum_all(stacked):
-    partial = jnp.sum(gather(stacked, "col"), axis=0)
-    return jnp.sum(gather(partial, "row"), axis=0)
+    flat = stacked.reshape(-1, 128)
+    partial = jnp.sum(swap(copies(flat, lax.axis_size("col")), "col"), axis=0)
+    total = jnp.sum(swap(copies(partial, lax.axis_size("row")), "row"), axis=0)
+    return total.reshape(stacked.shape)
 
 
 def block_sums(selected, products, row_count):
@@ -41,35 +55,48 @@
     return jnp.dot(picker, products, precision=highest)
 
 
-def scatter(sums, axis, shape):
-    parts = sums.astype(jnp.bfloat16).reshape(lax.axis_size(axis), *shape)
-    return jnp.sum(swap(parts, axis).astype(jnp.float32), axis=0)
-
-
-def apply_operator(vectors, tile_set, row_list, column_list, diagonal_blocks):
+def apply_operator(vectors, grams, tile_set, row_list, column_list, diagonal_blocks):
     narrow = vectors.astype(jnp.bfloat16)
     shape = narrow.shape
     own_blocks = shape[0]
+    height = shape[0] * shape[1]
+    own = narrow.reshape(height, shape[2])
+    rows, columns = lax.axis_size("row"), lax.axis_size("col")
     count_tiles = tile_set.shape[0]
-    column_slab = gather(narrow, "row").reshape(-1, *shape[1:])
-    row_slab = gather(narrow, "col").reshape(-1, *shape[1:])
+    width = grams.size // columns
+
+    sent = jnp.concatenate(
+        [copies(own, columns), pack(grams.reshape(columns, width))], axis=1
+    )
+    got = swap(sent, "col")
+    row_slab = got[:, :height].reshape(-1, *shape[1:])
+    piece = jnp.sum(unpack(got[:, height:], width), axis=0)
     lower_part = jnp.einsum(
         "tki,tij->tkj", row_slab[row_list], tile_set, preferred_element_type=jnp.float32
     ).reshape(count_tiles, -1)
-    from_columns = scatter(
-        block_sums(column_list, lower_part, own_blocks * lax.axis_size("row")), "row", shape
+    lower = block_sums(column_list, lower_part, own_blocks * rows).astype(jnp.bfloat16)
+    sent = jnp.concatenate(
+        [copies(own, rows), lower.reshape(rows, height, -1), copies(pack(piece), rows)], axis=1
     )
+    got = swap(sent, "row")
+    column_slab = got[:, :height].reshape(-1, *shape[1:])
+    from_columns = jnp.sum(got[:, height : 2 * height].astype(jnp.float32), axis=0)
+    piece = jnp.sum(unpack(got[:, 2 * height :], width), axis=0)
     upper_part = jnp.einsum(
         "tkj,tij->tki", column_slab[column_list], tile_set, preferred_element_type=jnp.float32
     ).reshape(count_tiles, -1)
-    from_rows = scatter(
-        block_sums(row_list, upper_part, own_blocks * lax.axis_size("col")), "col", shape
+    upper = block_sums(row_list, upper_part, own_blocks * columns).astype(jnp.bfloat16)
+    sent = jnp.concatenate(
+        [upper.reshape(columns, height, -1), copies(pack(piece), columns)], axis=1
     )
+    got = swap(sent, "col")
+    from_rows = jnp.sum(got[:, :height].astype(jnp.float32), axis=0)
     diagonal = 0.5 * (
         jnp.einsum("bkj,bij->bki", narrow, diagonal_blocks, preferred_element_type=jnp.float32)
         + jnp.einsum("bki,bij->bkj", narrow, diagonal_blocks, preferred_element_type=jnp.float32)
     )
-    return from_rows + from_columns + diagonal
+    image = (from_rows + from_columns).reshape(shape) + diagonal
+    return image, unpack(got[:, height:], width).reshape(grams.shape)
 
 
 def factor_of(gram):
@@ -82,16 +109,13 @@
 
 def local(start_block, tile_values, tile_rows, tile_columns, diagonal_blocks):
     matrix = (tile_values[0, 0], tile_rows[0, 0], tile_columns[0, 0], diagonal_blocks)
-    first = apply_operator(start_block, *matrix)
-    sums = sum_all(
-        jnp.stack(
-            [gram_of(start_block, start_block), gram_of(start_block, first), gram_of(first, first)]
-        )
-    )
-    second = apply_operator(first, *matrix)
-    _, inverse_start = factor_of(sums[0])
-    alpha_first = dot(dot(inverse_start, sums[1]), inverse_start.T)
-    image_gram = dot(dot(inverse_start, sums[2]), inverse_start.T)
+    start_gram = gram_of(start_block, start_block)[None]
+    first, start_sum = apply_operator(start_block, start_gram, *matrix)
+    first_grams = jnp.stack([gram_of(start_block, first), gram_of(first, first)])
+    second, sums = apply_operator(first, first_grams, *matrix)
+    _, inverse_start = factor_of(start_sum[0])
+    alpha_first = dot(dot(inverse_start, sums[0]), inverse_start.T)
+    image_gram = dot(dot(inverse_start, sums[1]), inverse_start.T)
     beta_first, inverse_first = factor_of(image_gram - dot(alpha_first.T, alpha_first))
     basis_start = mix(inverse_start, start_block)
     image_start = mix(inverse_start, first)

time: 312 us -> 267 us (0.86)
  waiting for transfers between devices: 137 us -> 122 us
  blocking collectives: 62.3 us -> 50.4 us
  starting transfers between devices: 53.8 us -> 42.7 us
  local copies, waits for them, and re-layouts: 15 us -> 6.4 us
    all_to_all x8 -> x5, waiting for transfers between devices: 137 us -> 122 us  [swap(): return lax.all_to_all(parts, axis, 0, 0, tiled=True)]
    all_to_all x4 -> x3, blocking collectives: 62.3 us -> 50.4 us  [swap(): return lax.all_to_all(parts, axis, 0, 0, tiled=True)]
    all_to_all x8 -> x5, starting transfers between devices: 53.8 us -> 42.7 us  [swap(): return lax.all_to_all(parts, axis, 0, 0, tiled=True)]
    unnamed x42 -> x12, local copies, waits for them, and re-layouts: 7.49 us -> 0.17 us
    all_to_all x4 -> x0, other arithmetic: 4.72 us -> none  [swap(): return lax.all_to_all(parts, axis, 0, 0, tiled=True)]
    concatenate x0 -> x6, other arithmetic: none -> 4.38 us  [the longest x2 2.16 us: apply_operator(): jnp.concatenate([copies(own, rows), lower.reshape(rows, height, -1), copi...]
  transfers between devices with their start and end apart: 8 -> 5, of which waited for: 8 -> 5; matrix products, arithmetic and copies ran while one was open for 12% -> 3% of each run, Pallas kernels for 0% -> 0%
where the time goes in v2:
time: 267 us; the launch traced here: 266 us
  waiting for transfers between devices  122 us (46%)
  blocking collectives  50.4 us (19%)
  starting transfers between devices  42.7 us (16%)
  other arithmetic  26.6 us (10%)
  matrix products  16 us (6%)
  local copies, waits for them, and re-layouts  6.4 us (2%)
    all_to_all x5, waiting for transfers between devices, swap(): return lax.all_to_all(parts, axis, 0, 0, tiled=True)  122 us
    all_to_all x3, blocking collectives, swap(): return lax.all_to_all(parts, axis, 0, 0, tiled=True)  50.4 us
    all_to_all x5, starting transfers between devices, swap(): return lax.all_to_all(parts, axis, 0, 0, tiled=True)  42.7 us
    another operation x9, other arithmetic, factor_of(): factor = jnp.linalg.cholesky(gram)  10.8 us
    another operation x4, other arithmetic, factor_of(): jax.scipy.linalg.solve_triangular(factor, jnp.eye(factor.shape[0], dtype=...  7.96 us
  transfers between devices with their start and end apart: 5, of which 5 were waited for; matrix products, arithmetic and copies ran while one was open for 3% of the time, Pallas kernels for 0%

profile of v2, /device:TPU:1, one launch (start us, length us, event | category | flops | bytes accessed | tf_op | source)
XLA Modules:
  0.0 265.8 jit_solution(2938548660046403260)
XLA Ops:
  0.7 1.1 convolution_bitcast_fusion.11
  1.7 0.8 convert_element_type.77
  2.6 0.7 fusion.27
  3.4 10.2 %all-to-all-start = ((bf16[16,72,128]{2,1,0:T(8,128)(2,1)}), bf16[16,72,128]{2,1,0:T(8,128)(2,1)S(1)}, u32[]{:S(2)}, u32[]{:S(2)}) async-start(bf16[16,72,128]{2,1,0:T(8,128)(2,1)} %fusion.27), calls=%async_computation | async-start | bytes 589824 | tf_op jit(solution)/shard_map/all_to_all | solution.py:24
  13.6 7.4 %all-to-all-done = bf16[16,72,128]{2,1,0:T(8,128)(2,1)S(1)} async-done(((bf16[16,72,128]{2,1,0:T(8,128)(2,1)}), bf16[16,72,128]{2,1,0:T(8,128)(2,1)S(1)}, u32[]{:S(2)}, u32[]{:S(2)}) %all-to-all-start) | async-done | bytes 294944 | tf_op jit(solution)/shard_map/all_to_all | solution.py:24
  21.1 0.6 gather_fusion
  21.8 0.5 fusion.6
  22.4 1.1 convolution_convert_fusion.1
  23.5 0.2 reshape.326
  23.9 1.1 pad_maximum_fusion
  25.0 14.0 %all-to-all-start.1 = ((bf16[32,136,128]{2,1,0:T(8,128)(2,1)}), bf16[32,136,128]{2,1,0:T(8,128)(2,1)S(1)}, u32[]{:S(2)}, u32[]{:S(2)}) async-start(bf16[32,136,128]{2,1,0:T(8,128)(2,1)} %pad_maximum_fusion), calls=%async_computation.1 | async-start | bytes 2228224 | tf_op jit(solution)/shard_map/all_to_all | solution.py:24
  39.1 54.0 %all-to-all-done.1 = bf16[32,136,128]{2,1,0:T(8,128)(2,1)S(1)} async-done(((bf16[32,136,128]{2,1,0:T(8,128)(2,1)}), bf16[32,136,128]{2,1,0:T(8,128)(2,1)S(1)}, u32[]{:S(2)}, u32[]{:S(2)}) %all-to-all-start.1) | async-done | bytes 1114144 | tf_op jit(solution)/shard_map/all_to_all | solution.py:24
  93.2 1.4 gather_fusion.1
  94.5 1.9 fusion.4
  96.4 0.9 convolution_convert_fusion.3
  97.5 0.7 pad_maximum_fusion.2
  98.3 5.3 %all-to-all-start.2 = ((bf16[16,72,128]{2,1,0:T(8,128)(2,1)}), bf16[16,72,128]{2,1,0:T(8,128)(2,1)S(1)}, u32[]{:S(2)}, u32[]{:S(2)}) async-start(bf16[16,72,128]{2,1,0:T(8,128)(2,1)} %pad_maximum_fusion.2), calls=%async_computation.2 | async-start | bytes 589824 | tf_op jit(solution)/shard_map/all_to_all | solution.py:24
  103.8 7.2 %all-to-all-done.2 = bf16[16,72,128]{2,1,0:T(8,128)(2,1)S(1)} async-done(((bf16[16,72,128]{2,1,0:T(8,128)(2,1)}), bf16[16,72,128]{2,1,0:T(8,128)(2,1)S(1)}, u32[]{:S(2)}, u32[]{:S(2)}) %all-to-all-start.2) | async-done | bytes 294944 | tf_op jit(solution)/shard_map/all_to_all | solution.py:24
  111.8 11.0 %all_to_all.40 = bf16[16,72,128]{2,1,0:T(8,128)(2,1)S(1)} all-to-all(bf16[16,72,128]{2,1,0:T(8,128)(2,1)S(1)} %fusion.28), channel_id=1, replica_groups=mesh['row'=32,'col'=16] {'col'}, dimensions={0} | all-to-all | bytes 589824 | tf_op jit(solution)/shard_map/all_to_all | solution.py:24
  122.9 0.6 gather_fusion.2
  123.5 0.5 fusion.2
  124.0 1.1 convolution_convert_fusion
  125.6 1.1 pad_maximum_fusion.1
  126.7 7.9 %all-to-all-start.4 = ((bf16[32,136,128]{2,1,0:T(8,128)(2,1)}), bf16[32,136,128]{2,1,0:T(8,128)(2,1)S(1)}, u32[]{:S(2)}, u32[]{:S(2)}) async-start(bf16[32,136,128]{2,1,0:T(8,128)(2,1)} %pad_maximum_fusion.1), calls=%async_computation.4 | async-start | bytes 2228224 | tf_op jit(solution)/shard_map/all_to_all | solution.py:24
  134.8 2.9 %cholesky.59 = f32[32,32]{1,0:T(8,128)S(1)} custom-call(f32[32,32]{1,0:T(8,128)S(1)} %fusion.49), custom_call_target="Cholesky" | custom-call | tf_op jit(solution)/shard_map/jit(cholesky)/cholesky | solution.py:103
  137.8 0.6 compare_reduce_fusion.2
  138.4 0.7 fusion.33
  139.1 2.4 custom-call.7
  142.1 46.6 %all-to-all-done.4 = bf16[32,136,128]{2,1,0:T(8,128)(2,1)S(1)} async-done(((bf16[32,136,128]{2,1,0:T(8,128)(2,1)}), bf16[32,136,128]{2,1,0:T(8,128)(2,1)S(1)}, u32[]{:S(2)}, u32[]{:S(2)}) %all-to-all-start.4) | async-done | bytes 1114144 | tf_op jit(solution)/shard_map/all_to_all | solution.py:24
  188.7 1.4 gather_fusion.3
  190.0 1.9 fusion
  191.9 0.9 convolution_convert_fusion.2
  193.1 0.7 pad_maximum_fusion.3
  193.8 5.3 %all-to-all-start.5 = ((bf16[16,72,128]{2,1,0:T(8,128)(2,1)}), bf16[16,72,128]{2,1,0:T(8,128)(2,1)S(1)}, u32[]{:S(2)}, u32[]{:S(2)}) async-start(bf16[16,72,128]{2,1,0:T(8,128)(2,1)} %pad_maximum_fusion.3), calls=%async_computation.5 | async-start | bytes 589824 | tf_op jit(solution)/shard_map/all_to_all | solution.py:24
  199.4 7.2 %all-to-all-done.5 = bf16[16,72,128]{2,1,0:T(8,128)(2,1)S(1)} async-done(((bf16[16,72,128]{2,1,0:T(8,128)(2,1)}), bf16[16,72,128]{2,1,0:T(8,128)(2,1)S(1)}, u32[]{:S(2)}, u32[]{:S(2)}) %all-to-all-start.5) | async-done | bytes 294944 | tf_op jit(solution)/shard_map/all_to_all | solution.py:24
  207.7 2.9 %cholesky.70 = f32[32,32]{1,0:T(8,128)S(1)} custom-call(f32[32,32]{1,0:T(8,128)S(1)} %fusion.41), custom_call_target="Cholesky" | custom-call | tf_op jit(solution)/shard_map/jit(cholesky)/cholesky | solution.py:103
  210.6 0.6 compare_reduce_fusion.1
  211.3 0.7 fusion.55
  212.0 2.4 custom-call.8
  215.8 0.9 fusion.11
  217.1 9.8 %all_to_all.41 = f32[16,16,128]{2,1,0:T(8,128)S(1)} all-to-all(f32[16,16,128]{2,1,0:T(8,128)S(1)} %broadcast_in_dim.38), channel_id=1, replica_groups=mesh['row'=32,'col'=16] {'col'}, dimensions={0} | all-to-all | bytes 262144 | tf_op jit(solution)/shard_map/all_to_all | solution.py:24
  226.9 29.7 %all_to_all.42 = f32[32,16,128]{2,1,0:T(8,128)S(1)} all-to-all(f32[32,16,128]{2,1,0:T(8,128)S(1)} %broadcast_in_dim.39), channel_id=1, replica_groups=mesh['row'=32,'col'=16] {'row'}, dimensions={0} | all-to-all | bytes 524288 | tf_op jit(solution)/shard_map/all_to_all | solution.py:24
  257.4 2.9 %cholesky.81 = f32[32,32]{1,0:T(8,128)S(1)} custom-call(f32[32,32]{1,0:T(8,128)S(1)} %fusion.37), custom_call_target="Cholesky" | custom-call | tf_op jit(solution)/shard_map/jit(cholesky)/cholesky | solution.py:103
  260.4 0.6 compare_reduce_fusion
  261.0 0.7 fusion.54
  261.7 2.4 custom-call.9
  264.4 0.8 fusion.8
  265.1 0.6 pad_maximum_fusion.6
  (117 shorter events, 7.5 us)
Async XLA Ops:
  0.6 21.1 %copy-start = (bf16[1,1,48,128,128]{4,3,2,1,0:T(8,128)(2,1)S(1)}, bf16[1,1,48,128,128]{4,3,2,1,0:T(8,128)(2,1)}, u32[]{:S(2)}) copy-start(bf16[1,1,48,128,128]{4,3,2,1,0:T(8,128)(2,1)} %param.9) | copy-start | bytes 4718596
  0.6 12.9 %copy-start.4 = (s32[1,1,48]{2,1,0:T(1,128)S(1)}, s32[1,1,48]{2,1,0:T(1,128)}, u32[]{:S(2)}) copy-start(s32[1,1,48]{2,1,0:T(1,128)} %param.10) | copy-start | bytes 580
  3.4 17.7 %all-to-all-start = ((bf16[16,72,128]{2,1,0:T(8,128)(2,1)}), bf16[16,72,128]{2,1,0:T(8,128)(2,1)S(1)}, u32[]{:S(2)}, u32[]{:S(2)}) async-start(bf16[16,72,128]{2,1,0:T(8,128)(2,1)} %fusion.27), calls=%async_computation | async-start | bytes 589824 | tf_op jit(solution)/shard_map/all_to_all | solution.py:24
  21.8 0.7 copy-start.3
  25.0 68.0 %all-to-all-start.1 = ((bf16[32,136,128]{2,1,0:T(8,128)(2,1)}), bf16[32,136,128]{2,1,0:T(8,128)(2,1)S(1)}, u32[]{:S(2)}, u32[]{:S(2)}) async-start(bf16[32,136,128]{2,1,0:T(8,128)(2,1)} %pad_maximum_fusion), calls=%async_computation.1 | async-start | bytes 2228224 | tf_op jit(solution)/shard_map/all_to_all | solution.py:24
  96.4 7.1 %copy-start.1 = (bf16[2,128,128]{2,1,0:T(8,128)(2,1)S(1)}, bf16[2,128,128]{2,1,0:T(8,128)(2,1)}, u32[]{:S(2)}) copy-start(bf16[2,128,128]{2,1,0:T(8,128)(2,1)} %param.12) | copy-start | bytes 196612
  97.4 13.8 %copy-start.2 = (f32[2,32,128]{2,1,0:T(8,128)S(1)}, f32[2,32,128]{2,1,0:T(8,128)}, u32[]{:S(2)}) copy-start(f32[2,32,128]{2,1,0:T(8,128)} %param.8) | copy-start | bytes 98308
  98.3 12.7 %all-to-all-start.2 = ((bf16[16,72,128]{2,1,0:T(8,128)(2,1)}), bf16[16,72,128]{2,1,0:T(8,128)(2,1)S(1)}, u32[]{:S(2)}, u32[]{:S(2)}) async-start(bf16[16,72,128]{2,1,0:T(8,128)(2,1)} %pad_maximum_fusion.2), calls=%async_computation.2 | async-start | bytes 589824 | tf_op jit(solution)/shard_map/all_to_all | solution.py:24
  126.7 61.9 %all-to-all-start.4 = ((bf16[32,136,128]{2,1,0:T(8,128)(2,1)}), bf16[32,136,128]{2,1,0:T(8,128)(2,1)S(1)}, u32[]{:S(2)}, u32[]{:S(2)}) async-start(bf16[32,136,128]{2,1,0:T(8,128)(2,1)} %pad_maximum_fusion.1), calls=%async_computation.4 | async-start | bytes 2228224 | tf_op jit(solution)/shard_map/all_to_all | solution.py:24
  193.8 12.7 %all-to-all-start.5 = ((bf16[16,72,128]{2,1,0:T(8,128)(2,1)}), bf16[16,72,128]{2,1,0:T(8,128)(2,1)S(1)}, u32[]{:S(2)}, u32[]{:S(2)}) async-start(bf16[16,72,128]{2,1,0:T(8,128)(2,1)} %pad_maximum_fusion.3), calls=%async_computation.5 | async-start | bytes 589824 | tf_op jit(solution)/shard_map/all_to_all | solution.py:24

commit v3 on v2

--- a/solution.py
+++ b/solution.py
@@ -3,9 +3,17 @@
 import jax
 import jax.numpy as jnp
 from jax import lax
+from jax.sharding import Mesh
 from jax.sharding import PartitionSpec as P
 
 highest = lax.Precision.HIGHEST
+
+AXES = ("x_high", "far", "near", "x_low", "y", "core")
+COLUMN = ("x_low", "y", "core")
+PLANE = ("x_high", *COLUMN)
+DEPTH = ("far", "near")
+NEAR = ("x_high", "near")
+FAR = ("far",)
 
 
 def gram_of(left_side, right_side):
@@ -44,8 +52,8 @@
 
 def sum_all(stacked):
     flat = stacked.reshape(-1, 128)
-    partial = jnp.sum(swap(copies(flat, lax.axis_size("col")), "col"), axis=0)
-    total = jnp.sum(swap(copies(partial, lax.axis_size("row")), "row"), axis=0)
+    partial = jnp.sum(swap(copies(flat, lax.axis_size(PLANE)), PLANE), axis=0)
+    total = jnp.sum(swap(copies(partial, lax.axis_size(DEPTH)), DEPTH), axis=0)
     return total.reshape(stacked.shape)
 
 
@@ -61,35 +69,48 @@
     own_blocks = shape[0]
     height = shape[0] * shape[1]
     own = narrow.reshape(height, shape[2])
-    rows, columns = lax.axis_size("row"), lax.axis_size("col")
+    fars, columns = lax.axis_size(FAR), lax.axis_size(COLUMN)
+    rows = 4 * fars
     count_tiles = tile_set.shape[0]
     width = grams.size // columns
 
     sent = jnp.concatenate(
         [copies(own, columns), pack(grams.reshape(columns, width))], axis=1
     )
-    got = swap(sent, "col")
+    got = swap(sent, COLUMN)
     row_slab = got[:, :height].reshape(-1, *shape[1:])
     piece = jnp.sum(unpack(got[:, height:], width), axis=0)
     lower_part = jnp.einsum(
         "tki,tij->tkj", row_slab[row_list], tile_set, preferred_element_type=jnp.float32
     ).reshape(count_tiles, -1)
     lower = block_sums(column_list, lower_part, own_blocks * rows).astype(jnp.bfloat16)
+    lower = lower.reshape(2, fars, 2, height, 128).transpose(0, 2, 1, 3, 4)
     sent = jnp.concatenate(
-        [copies(own, rows), lower.reshape(rows, height, -1), copies(pack(piece), rows)], axis=1
+        [lower.reshape(4, fars * height, 128), copies(pack(piece), 4)], axis=1
     )
-    got = swap(sent, "row")
-    column_slab = got[:, :height].reshape(-1, *shape[1:])
+    got = swap(sent, NEAR)
+    lower = jnp.sum(got[:, :-8].astype(jnp.float32), axis=0).astype(jnp.bfloat16)
+    piece = jnp.sum(unpack(got[:, -8:], width), axis=0)
+    sent = jnp.concatenate(
+        [copies(own, fars), lower.reshape(fars, height, 128), copies(pack(piece), fars)], axis=1
+    )
+    got = swap(sent, FAR)
     from_columns = jnp.sum(got[:, height : 2 * height].astype(jnp.float32), axis=0)
     piece = jnp.sum(unpack(got[:, 2 * height :], width), axis=0)
+    got = swap(copies(got[:, :height].reshape(fars * height, 128), 4), NEAR)
+    column_slab = got.reshape(-1, *shape[1:])
+    near_first = (column_list // (2 * own_blocks * fars)) * 2 + (column_list // own_blocks) % 2
+    column_place = (
+        near_first * fars + (column_list // (2 * own_blocks)) % fars
+    ) * own_blocks + column_list % own_blocks
     upper_part = jnp.einsum(
-        "tkj,tij->tki", column_slab[column_list], tile_set, preferred_element_type=jnp.float32
+        "tkj,tij->tki", column_slab[column_place], tile_set, preferred_element_type=jnp.float32
     ).reshape(count_tiles, -1)
     upper = block_sums(row_list, upper_part, own_blocks * columns).astype(jnp.bfloat16)
     sent = jnp.concatenate(
         [upper.reshape(columns, height, -1), copies(pack(piece), columns)], axis=1
     )
-    got = swap(sent, "col")
+    got = swap(sent, COLUMN)
     from_rows = jnp.sum(got[:, :height].astype(jnp.float32), axis=0)
     diagonal = 0.5 * (
         jnp.einsum("bkj,bij->bki", narrow, diagonal_blocks, preferred_element_type=jnp.float32)
@@ -127,7 +148,7 @@
     beta_last, inverse_last = factor_of(last[1] - dot(alpha_last.T, alpha_last))
     basis_last = mix(inverse_last, image_first - mix(alpha_last.T, basis_first))
     scaling = math.sqrt(
-        start_block.shape[0] * start_block.shape[2] * lax.axis_size("row") * lax.axis_size("col")
+        start_block.shape[0] * start_block.shape[2] * lax.axis_size(PLANE) * lax.axis_size(DEPTH)
     )
     return (
         basis_last * scaling,
@@ -137,17 +158,20 @@
 
 
 def solution(mesh):
+    split = Mesh(mesh.devices.reshape(2, 8, 2, 2, 4, 2), AXES)
+    rows = ("x_high", "far", "near")
+    owner = P((*COLUMN, *rows), None, None)
     placed = (
-        P(("col", "row"), None, None),
-        P("row", "col", None, None, None),
-        P("row", "col", None),
-        P("row", "col", None),
-        P(("col", "row"), None, None),
+        owner,
+        P(rows, COLUMN, None, None, None),
+        P(rows, COLUMN, None),
+        P(rows, COLUMN, None),
+        owner,
     )
     return jax.shard_map(
         local,
-        mesh=mesh,
+        mesh=split,
         in_specs=placed,
-        out_specs=(P(("col", "row"), None, None), P(), P()),
+        out_specs=(owner, P(), P()),
         check_vma=False,
     )

time: 267 us -> 232 us (0.87)
  waiting for transfers between devices: 122 us -> 45.8 us
  blocking collectives: 50.4 us -> 95.1 us
    all_to_all x5 -> x6, waiting for transfers between devices: 122 us -> 45.8 us  [swap(): return lax.all_to_all(parts, axis, 0, 0, tiled=True)]
    all_to_all x3 -> x6, blocking collectives: 50.4 us -> 95.1 us  [swap(): return lax.all_to_all(parts, axis, 0, 0, tiled=True)]
    all_to_all x5 -> x6, starting transfers between devices: 42.7 us -> 41.8 us  [swap(): return lax.all_to_all(parts, axis, 0, 0, tiled=True)]
  transfers between devices with their start and end apart: 5 -> 6, of which waited for: 5 -> 6; matrix products, arithmetic and copies ran while one was open for 3% -> 3% of each run, Pallas kernels for 0% -> 0%
where the time goes in v3:
time: 232 us; the launch traced here: 230 us
  blocking collectives  95.1 us (41%)
  waiting for transfers between devices  45.8 us (20%)
  starting transfers between devices  41.8 us (18%)
  other arithmetic  25.5 us (11%)
  matrix products  13.9 us (6%)
  local copies, waits for them, and re-layouts  6.46 us (3%)
    all_to_all x6, blocking collectives, swap(): return lax.all_to_all(parts, axis, 0, 0, tiled=True)  95.1 us
    all_to_all x6, waiting for transfers between devices, swap(): return lax.all_to_all(parts, axis, 0, 0, tiled=True)  45.8 us
    all_to_all x6, starting transfers between devices, swap(): return lax.all_to_all(parts, axis, 0, 0, tiled=True)  41.8 us
    another operation x9, other arithmetic, factor_of(): factor = jnp.linalg.cholesky(gram)  10.8 us
    another operation x4, other arithmetic, factor_of(): jax.scipy.linalg.solve_triangular(factor, jnp.eye(factor.shape[0], dtype=...  7.96 us
  transfers between devices with their start and end apart: 6, of which 6 were waited for; matrix products, arithmetic and copies ran while one was open for 3% of the time, Pallas kernels for 0%

profile of v3, /device:TPU:1, one launch (start us, length us, event | category | flops | bytes accessed | tf_op | source)
XLA Modules:
  0.0 230.0 jit_solution(18144910850710119172)
XLA Ops:
  0.7 0.9 convert_element_type.91
  1.5 1.0 convolution_bitcast_fusion.11
  2.7 0.7 fusion.27
  3.4 10.2 %all-to-all-start = ((bf16[16,72,128]{2,1,0:T(8,128)(2,1)}), bf16[16,72,128]{2,1,0:T(8,128)(2,1)S(1)}, u32[]{:S(2)}, u32[]{:S(2)}) async-start(bf16[16,72,128]{2,1,0:T(8,128)(2,1)} %fusion.27), calls=%async_computation | async-start | bytes 589824 | tf_op jit(solution)/shard_map/all_to_all | solution.py:32
  13.7 7.4 %all-to-all-done = bf16[16,72,128]{2,1,0:T(8,128)(2,1)S(1)} async-done(((bf16[16,72,128]{2,1,0:T(8,128)(2,1)}), bf16[16,72,128]{2,1,0:T(8,128)(2,1)S(1)}, u32[]{:S(2)}, u32[]{:S(2)}) %all-to-all-start) | async-done | bytes 294944 | tf_op jit(solution)/shard_map/all_to_all | solution.py:32
  21.2 0.6 gather_fusion
  22.5 1.1 convolution_convert_fusion.1
  24.0 11.5 %all_to_all.60 = bf16[4,520,128]{2,1,0:T(8,128)(2,1)S(1)} all-to-all(bf16[4,520,128]{2,1,0:T(8,128)(2,1)S(1)} %pad_maximum_fusion), channel_id=1, replica_groups=mesh['x_high'=2,'far'=8,'near'=2,'x_low'=2,'y'=4,'core'=2] {'x_high','ne..., dimensions={0} | all-to-all | bytes 1064960 | tf_op jit(solution)/shard_map/all_to_all | solution.py:32
  35.6 30.6 %all_to_all.61 = bf16[8,136,128]{2,1,0:T(8,128)(2,1)S(1)} all-to-all(bf16[8,136,128]{2,1,0:T(8,128)(2,1)S(1)} %pad_maximum_fusion.4), channel_id=1, replica_groups=mesh['x_high'=2,'far'=8,'near'=2,'x_low'=2,'y'=4,'core'=2] {'far'}, dimensions={0} | all-to-all | bytes 557056 | tf_op jit(solution)/shard_map/all_to_all | solution.py:32
  66.2 0.9 broadcast_in_dim.44
  67.1 3.5 %all-to-all-start.3 = ((bf16[4,512,128]{2,1,0:T(8,128)(2,1)}), bf16[4,512,128]{2,1,0:T(8,128)(2,1)S(1)}, u32[]{:S(2)}, u32[]{:S(2)}) async-start(bf16[4,512,128]{2,1,0:T(8,128)(2,1)} %broadcast_in_dim.44), calls=%async_computation.3 | async-start | bytes 1048576 | tf_op jit(solution)/shard_map/all_to_all | solution.py:32
  70.7 6.8 %all-to-all-done.3 = bf16[4,512,128]{2,1,0:T(8,128)(2,1)S(1)} async-done(((bf16[4,512,128]{2,1,0:T(8,128)(2,1)}), bf16[4,512,128]{2,1,0:T(8,128)(2,1)S(1)}, u32[]{:S(2)}, u32[]{:S(2)}) %all-to-all-start.3) | async-done | bytes 524320 | tf_op jit(solution)/shard_map/all_to_all | solution.py:32
  78.1 0.9 fusion.4
  79.0 0.9 convolution_convert_fusion.3
  80.1 0.7 pad_maximum_fusion.2
  80.9 10.4 %all-to-all-start.4 = ((bf16[16,72,128]{2,1,0:T(8,128)(2,1)}), bf16[16,72,128]{2,1,0:T(8,128)(2,1)S(1)}, u32[]{:S(2)}, u32[]{:S(2)}) async-start(bf16[16,72,128]{2,1,0:T(8,128)(2,1)} %pad_maximum_fusion.2), calls=%async_computation.4 | async-start | bytes 589824 | tf_op jit(solution)/shard_map/all_to_all | solution.py:32
  91.5 7.2 %all-to-all-done.4 = bf16[16,72,128]{2,1,0:T(8,128)(2,1)S(1)} async-done(((bf16[16,72,128]{2,1,0:T(8,128)(2,1)}), bf16[16,72,128]{2,1,0:T(8,128)(2,1)S(1)}, u32[]{:S(2)}, u32[]{:S(2)}) %all-to-all-start.4) | async-done | bytes 294944 | tf_op jit(solution)/shard_map/all_to_all | solution.py:32
  99.5 11.0 %all_to_all.62 = bf16[16,72,128]{2,1,0:T(8,128)(2,1)S(1)} all-to-all(bf16[16,72,128]{2,1,0:T(8,128)(2,1)S(1)} %fusion.28), channel_id=1, replica_groups=mesh['x_high'=2,'far'=8,'near'=2,'x_low'=2,'y'=4,'core'=2] {'x_low','y',..., dimensions={0} | all-to-all | bytes 589824 | tf_op jit(solution)/shard_map/all_to_all | solution.py:32
  111.7 1.1 convolution_convert_fusion
  113.2 11.5 %all_to_all.63 = bf16[4,520,128]{2,1,0:T(8,128)(2,1)S(1)} all-to-all(bf16[4,520,128]{2,1,0:T(8,128)(2,1)S(1)} %pad_maximum_fusion.1), channel_id=1, replica_groups=mesh['x_high'=2,'far'=8,'near'=2,'x_low'=2,'y'=4,'core'=2] {'x_high','ne..., dimensions={0} | all-to-all | bytes 1064960 | tf_op jit(solution)/shard_map/all_to_all | solution.py:32
  124.9 0.7 pad_maximum_fusion.5
  125.7 4.0 %all-to-all-start.7 = ((bf16[8,136,128]{2,1,0:T(8,128)(2,1)}), bf16[8,136,128]{2,1,0:T(8,128)(2,1)S(1)}, u32[]{:S(2)}, u32[]{:S(2)}) async-start(bf16[8,136,128]{2,1,0:T(8,128)(2,1)} %pad_maximum_fusion.5), calls=%async_computation.7 | async-start | bytes 557056 | tf_op jit(solution)/shard_map/all_to_all | solution.py:32
  129.9 2.9 %cholesky.59 = f32[32,32]{1,0:T(8,128)S(1)} custom-call(f32[32,32]{1,0:T(8,128)S(1)} %fusion.47), custom_call_target="Cholesky" | custom-call | tf_op jit(solution)/shard_map/jit(cholesky)/cholesky | solution.py:124
  132.9 0.6 compare_reduce_fusion.2
  133.5 14.0 %all-to-all-done.7 = bf16[8,136,128]{2,1,0:T(8,128)(2,1)S(1)} async-done(((bf16[8,136,128]{2,1,0:T(8,128)(2,1)}), bf16[8,136,128]{2,1,0:T(8,128)(2,1)S(1)}, u32[]{:S(2)}, u32[]{:S(2)}) %all-to-all-start.7) | async-done | bytes 278560 | tf_op jit(solution)/shard_map/all_to_all | solution.py:32
  147.5 0.9 broadcast_in_dim.53
  148.4 3.5 %all-to-all-start.8 = ((bf16[4,512,128]{2,1,0:T(8,128)(2,1)}), bf16[4,512,128]{2,1,0:T(8,128)(2,1)S(1)}, u32[]{:S(2)}, u32[]{:S(2)}) async-start(bf16[4,512,128]{2,1,0:T(8,128)(2,1)} %broadcast_in_dim.53), calls=%async_computation.8 | async-start | bytes 1048576 | tf_op jit(solution)/shard_map/all_to_all | solution.py:32
  151.9 0.7 fusion.33
  152.5 2.4 %custom-call.7 = f32[1,32,32]{1,2,0:T(8,128)S(1)} custom-call(f32[1,32,32]{2,1,0:T(8,128)S(1)} %fusion.33), custom_call_target="InvertDiagBlocksLowerTriangular" | custom-call | tf_op jit(solution)/shard_map/jit(_solve_triangular)/triangular_solve | solution.py:125
  155.6 3.2 %all-to-all-done.8 = bf16[4,512,128]{2,1,0:T(8,128)(2,1)S(1)} async-done(((bf16[4,512,128]{2,1,0:T(8,128)(2,1)}), bf16[4,512,128]{2,1,0:T(8,128)(2,1)S(1)}, u32[]{:S(2)}, u32[]{:S(2)}) %all-to-all-start.8) | async-done | bytes 524320 | tf_op jit(solution)/shard_map/all_to_all | solution.py:32
  159.4 0.9 fusion
  160.3 0.9 convolution_convert_fusion.2
  161.4 0.7 pad_maximum_fusion.3
  162.1 10.2 %all-to-all-start.9 = ((bf16[16,72,128]{2,1,0:T(8,128)(2,1)}), bf16[16,72,128]{2,1,0:T(8,128)(2,1)S(1)}, u32[]{:S(2)}, u32[]{:S(2)}) async-start(bf16[16,72,128]{2,1,0:T(8,128)(2,1)} %pad_maximum_fusion.3), calls=%async_computation.9 | async-start | bytes 589824 | tf_op jit(solution)/shard_map/all_to_all | solution.py:32
  172.5 7.2 %all-to-all-done.9 = bf16[16,72,128]{2,1,0:T(8,128)(2,1)S(1)} async-done(((bf16[16,72,128]{2,1,0:T(8,128)(2,1)}), bf16[16,72,128]{2,1,0:T(8,128)(2,1)S(1)}, u32[]{:S(2)}, u32[]{:S(2)}) %all-to-all-start.9) | async-done | bytes 294944 | tf_op jit(solution)/shard_map/all_to_all | solution.py:32
  181.7 2.9 %cholesky.70 = f32[32,32]{1,0:T(8,128)S(1)} custom-call(f32[32,32]{1,0:T(8,128)S(1)} %fusion.39), custom_call_target="Cholesky" | custom-call | tf_op jit(solution)/shard_map/jit(cholesky)/cholesky | solution.py:124
  184.6 0.6 compare_reduce_fusion.1
  185.3 0.7 fusion.51
  185.9 2.4 %custom-call.8 = f32[1,32,32]{1,2,0:T(8,128)S(1)} custom-call(f32[1,32,32]{2,1,0:T(8,128)S(1)} %get-tuple-element.8), custom_call_target="InvertDiagBlocksLowerTriangular" | custom-call | tf_op jit(solution)/shard_map/jit(_solve_triangular)/triangular_solve | solution.py:125
  188.9 0.9 fusion.11
  190.3 13.7 %all_to_all.64 = f32[32,16,128]{2,1,0:T(8,128)S(1)} all-to-all(f32[32,16,128]{2,1,0:T(8,128)S(1)} %broadcast_in_dim.56), channel_id=1, replica_groups=mesh['x_high'=2,'far'=8,'near'=2,'x_low'=2,'y'=4,'core'=2] {'x_high','x_..., dimensions={0} | all-to-all | bytes 524288 | tf_op jit(solution)/shard_map/all_to_all | solution.py:32
  204.0 16.8 %all_to_all.65 = f32[16,16,128]{2,1,0:T(8,128)S(1)} all-to-all(f32[16,16,128]{2,1,0:T(8,128)S(1)} %broadcast_in_dim.57), channel_id=1, replica_groups=mesh['x_high'=2,'far'=8,'near'=2,'x_low'=2,'y'=4,'core'=2] {'far','near'}, dimensions={0} | all-to-all | bytes 262144 | tf_op jit(solution)/shard_map/all_to_all | solution.py:32
  221.7 2.9 %cholesky.81 = f32[32,32]{1,0:T(8,128)S(1)} custom-call(f32[32,32]{1,0:T(8,128)S(1)} %fusion.35), custom_call_target="Cholesky" | custom-call | tf_op jit(solution)/shard_map/jit(cholesky)/cholesky | solution.py:124
  224.6 0.6 compare_reduce_fusion
  225.3 0.7 fusion.50
  225.9 2.4 %custom-call.9 = f32[1,32,32]{1,2,0:T(8,128)S(1)} custom-call(f32[1,32,32]{2,1,0:T(8,128)S(1)} %get-tuple-element.10), custom_call_target="InvertDiagBlocksLowerTriangular" | custom-call | tf_op jit(solution)/shard_map/jit(_solve_triangular)/triangular_solve | solution.py:125
  228.6 0.8 fusion.8
  229.4 0.6 pad_maximum_fusion.8
  (142 shorter events, 10.7 us)
Async XLA Ops:
  0.6 21.2 %copy-start = (bf16[1,1,48,128,128]{4,3,2,1,0:T(8,128)(2,1)S(1)}, bf16[1,1,48,128,128]{4,3,2,1,0:T(8,128)(2,1)}, u32[]{:S(2)}) copy-start(bf16[1,1,48,128,128]{4,3,2,1,0:T(8,128)(2,1)} %param.9) | copy-start | bytes 4718596
  0.6 13.0 %copy-start.4 = (s32[1,1,48]{2,1,0:T(1,128)S(1)}, s32[1,1,48]{2,1,0:T(1,128)}, u32[]{:S(2)}) copy-start(s32[1,1,48]{2,1,0:T(1,128)} %param.10) | copy-start | bytes 580
  3.4 17.7 %all-to-all-start = ((bf16[16,72,128]{2,1,0:T(8,128)(2,1)}), bf16[16,72,128]{2,1,0:T(8,128)(2,1)S(1)}, u32[]{:S(2)}, u32[]{:S(2)}) async-start(bf16[16,72,128]{2,1,0:T(8,128)(2,1)} %fusion.27), calls=%async_computation | async-start | bytes 589824 | tf_op jit(solution)/shard_map/all_to_all | solution.py:32
  21.8 0.7 copy-start.3
  67.1 10.4 %all-to-all-start.3 = ((bf16[4,512,128]{2,1,0:T(8,128)(2,1)}), bf16[4,512,128]{2,1,0:T(8,128)(2,1)S(1)}, u32[]{:S(2)}, u32[]{:S(2)}) async-start(bf16[4,512,128]{2,1,0:T(8,128)(2,1)} %broadcast_in_dim.44), calls=%async_computation.3 | async-start | bytes 1048576 | tf_op jit(solution)/shard_map/all_to_all | solution.py:32
  79.0 12.3 %copy-start.1 = (bf16[2,128,128]{2,1,0:T(8,128)(2,1)S(1)}, bf16[2,128,128]{2,1,0:T(8,128)(2,1)}, u32[]{:S(2)}) copy-start(bf16[2,128,128]{2,1,0:T(8,128)(2,1)} %param.12) | copy-start | bytes 196612
  80.0 19.1 %copy-start.2 = (f32[2,32,128]{2,1,0:T(8,128)S(1)}, f32[2,32,128]{2,1,0:T(8,128)}, u32[]{:S(2)}) copy-start(f32[2,32,128]{2,1,0:T(8,128)} %param.8) | copy-start | bytes 98308
  80.9 17.8 %all-to-all-start.4 = ((bf16[16,72,128]{2,1,0:T(8,128)(2,1)}), bf16[16,72,128]{2,1,0:T(8,128)(2,1)S(1)}, u32[]{:S(2)}, u32[]{:S(2)}) async-start(bf16[16,72,128]{2,1,0:T(8,128)(2,1)} %pad_maximum_fusion.2), calls=%async_computation.4 | async-start | bytes 589824 | tf_op jit(solution)/shard_map/all_to_all | solution.py:32
  125.7 21.9 %all-to-all-start.7 = ((bf16[8,136,128]{2,1,0:T(8,128)(2,1)}), bf16[8,136,128]{2,1,0:T(8,128)(2,1)S(1)}, u32[]{:S(2)}, u32[]{:S(2)}) async-start(bf16[8,136,128]{2,1,0:T(8,128)(2,1)} %pad_maximum_fusion.5), calls=%async_computation.7 | async-start | bytes 557056 | tf_op jit(solution)/shard_map/all_to_all | solution.py:32
  148.4 10.4 %all-to-all-start.8 = ((bf16[4,512,128]{2,1,0:T(8,128)(2,1)}), bf16[4,512,128]{2,1,0:T(8,128)(2,1)S(1)}, u32[]{:S(2)}, u32[]{:S(2)}) async-start(bf16[4,512,128]{2,1,0:T(8,128)(2,1)} %broadcast_in_dim.53), calls=%async_computation.8 | async-start | bytes 1048576 | tf_op jit(solution)/shard_map/all_to_all | solution.py:32
  162.1 17.6 %all-to-all-start.9 = ((bf16[16,72,128]{2,1,0:T(8,128)(2,1)}), bf16[16,72,128]{2,1,0:T(8,128)(2,1)S(1)}, u32[]{:S(2)}, u32[]{:S(2)}) async-start(bf16[16,72,128]{2,1,0:T(8,128)(2,1)} %pad_maximum_fusion.3), calls=%async_computation.9 | async-start | bytes 589824 | tf_op jit(solution)/shard_map/all_to_all | solution.py:32

commit v4 on v1

v4 whole, which is shorter than its diff:
```python
import functools
import math

import jax
import jax.numpy as jnp
from jax import lax
from jax.experimental import pallas as pl
from jax.experimental.pallas import tpu as pltpu
from jax.sharding import Mesh
from jax.sharding import PartitionSpec as P

AXES = ("x_high", "far", "near", "x_low", "y", "core")
COLUMN = ("x_low", "y", "core")
PLANE = ("x_high", *COLUMN)
DEPTH = ("far", "near")
NEAR = ("x_high", "near")
FAR = ("far",)

NEARS = 4
FARS = 8
COLUMNS = 16
K = 32
OWN = 64
SLAB = FARS * OWN
EXTRA = 16
TERMS = 3
GROUP = 8

highest = lax.Precision.HIGHEST
f32 = jnp.float32
bf16 = jnp.bfloat16


def swap(parts, axis):
    return lax.all_to_all(parts, axis, 0, 0, tiled=True)


def call(kernel, outs, scalars, arrays, scratch=()):
    specs = [pl.BlockSpec(memory_space=pltpu.SMEM)] * len(scalars)
    specs += [pl.BlockSpec(memory_space=pltpu.VMEM)] * len(arrays)
    return pl.pallas_call(
        kernel,
        out_shape=outs,
        in_specs=specs,
        out_specs=jax.tree.map(lambda _: pl.BlockSpec(memory_space=pltpu.VMEM), outs),
        scratch_shapes=list(scratch),
        compiler_params=pltpu.CompilerParams(vmem_limit_bytes=16 * 2**20),
    )(*scalars, *arrays)


def out(shape, dtype):
    return jax.ShapeDtypeStruct(shape, dtype)


def iota(shape, dimension):
    return lax.broadcasted_iota(jnp.int32, shape, dimension)


def dot(left, right):
    return jnp.dot(left, right, precision=highest, preferred_element_type=f32)


def dot_t(left, right, precision=highest):
    return lax.dot_general(
        left, right, (((1,), (1,)), ((), ())), precision=precision, preferred_element_type=f32
    )


def terms_of(values):
    high = values.astype(bf16)
    rest = values - high.astype(f32)
    middle = rest.astype(bf16)
    low = (rest - middle.astype(f32)).astype(bf16)
    return high, middle, low


def one_hot(condition):
    return jnp.where(condition, 1.0, 0.0).astype(bf16)


def spread_slices(grams):
    source = jnp.concatenate(terms_of(grams), axis=0)
    shape = (COLUMNS * EXTRA, TERMS * K)
    row, column = iota(shape, 0), iota(shape, 1)
    place = row & (EXTRA - 1)
    wanted = (place >> 1) * K + (row >> 4) * 2 + (place & 1)
    picker = one_hot((place < 2 * TERMS) & (column == wanted))
    return jnp.dot(picker, source, preferred_element_type=f32).astype(bf16)


def sum_slices(pieces):
    shape = (EXTRA, pieces.shape[0])
    row, column = iota(shape, 0), iota(shape, 1)
    picker = one_hot(((column & 15) < 2 * TERMS) & ((column & 1) == (row & 1)))
    total = jnp.dot(picker, pieces, preferred_element_type=f32)
    high, middle, low = (term.astype(f32) for term in terms_of(total))
    place = iota(total.shape, 0)
    chosen = jnp.where(place < 2, high, jnp.where(place < 4, middle, low))
    return jnp.where(place < 2 * TERMS, chosen, 0.0).astype(bf16)


def join_slices(pieces):
    shape = (K, pieces.shape[0])
    row, column = iota(shape, 0), iota(shape, 1)
    picker = one_hot(
        ((column >> 4) == (row >> 1)) & ((column & 15) < 2 * TERMS) & ((column & 1) == (row & 1))
    )
    return jnp.dot(picker, pieces, preferred_element_type=f32)


def factor_of(gram):
    shape = (K, 128)
    row, column = iota(shape, 0), iota(shape, 1)
    work = jnp.where(column < K, gram, jnp.where(column == row + K, 1.0, 0.0))
    for step in range(K):
        across = jnp.broadcast_to(work[:, step : step + 1], shape)
        pivot = across[step : step + 1, :]
        guess = lax.rsqrt(pivot)
        scale = guess * (1.5 - 0.5 * pivot * guess * guess)
        lead = work[step : step + 1, :] * scale
        lower = work - (across * scale) * lead
        work = jnp.where(row > step, lower, jnp.where(row == step, lead, work))
    upper = jnp.where((column < K) & (column >= row), work, 0.0)
    inverse = pltpu.roll(work, 128 - K, 1)
    return upper[:, :K], inverse[:, :K]


def flip(matrix):
    eye = jnp.where(iota((K, K), 0) == iota((K, K), 1), 1.0, 0.0)
    return dot_t(eye, matrix)


def shifted(block, place, places):
    empty = jnp.zeros_like(block)
    return jnp.concatenate([block if i == place else empty for i in range(places)], axis=0)


def fill_first(message, narrow, grams):
    message[:, OWN:, :] = spread_slices(grams).reshape(COLUMNS, EXTRA, 128)
    for device in range(COLUMNS):
        message[device, :OWN, :] = narrow


def prepare_kernel(start, message):
    grams = jnp.zeros((K, 128), f32)
    for block in range(OWN // K):
        vectors = start[block * K : (block + 1) * K, :]
        grams += dot_t(vectors, shifted(vectors, 0, 4))
    fill_first(message, start[...].astype(bf16), grams)


def lower_kernel(rows, columns, got, tiles, message, total):
    total[...] = jnp.zeros_like(total)
    count = tiles.shape[0]
    for base in range(0, count, GROUP):
        parts = []
        for tile in range(base, base + GROUP):
            place = rows[tile]
            vectors = got[place >> 1, pl.ds(pl.multiple_of((place & 1) * K, K), K), :]
            parts.append(jnp.dot(vectors, tiles[tile], preferred_element_type=f32))
        for tile in range(base, base + GROUP):
            place = columns[tile]
            owner = place >> 1
            near = (owner >> 4) * 2 + (owner & 1)
            spot = (near * FARS + ((owner >> 1) & 7)) * 2 + (place & 1)
            where = pl.ds(pl.multiple_of(spot * K, K), K)
            total[where, :] += parts[tile - base]
    message[:, :SLAB, :] = total[...].astype(bf16).reshape(NEARS, SLAB, 128)
    piece = sum_slices(got[:, OWN:, :].reshape(COLUMNS * EXTRA, 128))
    for device in range(NEARS):
        message[device, SLAB:, :] = piece


def near_kernel(got, vectors, message):
    total = got[0, :SLAB, :].astype(f32)
    for device in range(1, NEARS):
        total += got[device, :SLAB, :].astype(f32)
    message[:, OWN : 2 * OWN, :] = total.astype(bf16).reshape(FARS, OWN, 128)
    piece = sum_slices(got[:, SLAB:, :].reshape(NEARS * EXTRA, 128))
    narrow = vectors[...].astype(bf16)
    for device in range(FARS):
        message[device, :OWN, :] = narrow
        message[device, 2 * OWN :, :] = piece


def far_kernel(got, message, column_sums, piece):
    total = got[0, OWN : 2 * OWN, :].astype(f32)
    for device in range(1, FARS):
        total += got[device, OWN : 2 * OWN, :].astype(f32)
    column_sums[...] = total
    piece[...] = sum_slices(got[:, 2 * OWN :, :].reshape(FARS * EXTRA, 128))
    slab = got[:, :OWN, :].reshape(SLAB, 128)
    for device in range(NEARS):
        message[device, :, :] = slab


def upper_kernel(rows, columns, got, tiles, piece, message, total):
    total[...] = jnp.zeros_like(total)
    count = tiles.shape[0]
    for base in range(0, count, GROUP):
        parts = []
        for tile in range(base, base + GROUP):
            place = columns[tile]
            owner = place >> 1
            near = (owner >> 4) * 2 + (owner & 1)
            spot = ((owner >> 1) & 7) * 2 + (place & 1)
            vectors = got[near, pl.ds(pl.multiple_of(spot * K, K), K), :]
            parts.append(dot_t(vectors, tiles[tile], None))
        for tile in range(base, base + GROUP):
            where = pl.ds(pl.multiple_of(rows[tile] * K, K), K)
            total[where, :] += parts[tile - base]
    message[:, :OWN, :] = total[...].astype(bf16).reshape(COLUMNS, OWN, 128)
    for device in range(COLUMNS):
        message[device, OWN:, :] = piece[...]


def image_of(got, column_sums, vectors, diagonal):
    images = []
    for block in range(OWN // K):
        where = slice(block * K, (block + 1) * K)
        narrow = vectors[where, :].astype(bf16)
        image = dot_t(narrow, diagonal[block], None)
        image += jnp.dot(narrow, diagonal[block], preferred_element_type=f32)
        image = 0.5 * image + column_sums[where, :]
        total = got[0, where, :].astype(f32)
        for device in range(1, COLUMNS):
            total += got[device, where, :].astype(f32)
        images.append(image + total)
    return images


def middle_kernel(got, column_sums, start, diagonal, image, start_sum, message):
    images = image_of(got, column_sums, start, diagonal)
    start_sum[...] = join_slices(got[:, OWN:, :].reshape(COLUMNS * EXTRA, 128))
    grams = jnp.zeros((K, 128), f32)
    for block in range(OWN // K):
        where = slice(block * K, (block + 1) * K)
        image[where, :] = images[block]
        joint = jnp.concatenate([start[where, :], images[block]] + [jnp.zeros((K, 128), f32)] * 2)
        grams += dot_t(images[block], joint)
    fill_first(message, jnp.concatenate(images).astype(bf16), grams)


def factor_kernel(gram, inverse):
    inverse[...] = factor_of(gram[...])[1]


def finish_kernel(
    got, column_sums, start, first, diagonal, inverse_start, basis, image, alpha, beta, message
):
    images = image_of(got, column_sums, first, diagonal)
    sums = join_slices(got[:, OWN:, :].reshape(COLUMNS * EXTRA, 128))
    inverse = inverse_start[...]
    alpha_t = dot_t(dot(inverse, sums[:, :K]), inverse)
    image_gram = dot_t(dot(inverse, pltpu.roll(sums, 128 - K, 1)[:, :K]), inverse)
    wide = jnp.zeros((128 - K, K), f32)
    square = dot_t(alpha_t, jnp.concatenate([alpha_t, wide]))
    upper, inverse_first = factor_of(
        jnp.concatenate([image_gram, jnp.zeros((K, 128 - K), f32)], axis=1) - square
    )
    packed = jnp.zeros((K // 2, 128), f32)
    for block in range(OWN // K):
        where = slice(block * K, (block + 1) * K)
        basis_start = dot(inverse, start[where, :])
        image_start = dot(inverse, first[where, :])
        current = dot(inverse_first, image_start - dot(alpha_t, basis_start))
        moved = dot(inverse, images[block]) - dot(alpha_t, image_start)
        result = dot(inverse_first, moved) - dot(upper, basis_start)
        basis[where, :] = current
        image[where, :] = result
        for half in range(2):
            top = result[half * (K // 2) : (half + 1) * (K // 2), :]
            empty = jnp.zeros_like(result)
            pair = [current, empty, result, empty] if half == 0 else [empty, current, empty, result]
            packed += dot_t(top, jnp.concatenate(pair))
    for device in range(message.shape[0]):
        message[device, :, :] = packed
    alpha[...] = flip(alpha_t)
    beta[...] = flip(upper)


def plane_kernel(got, message):
    total = got[0]
    for device in range(1, got.shape[0]):
        total += got[device]
    for device in range(message.shape[0]):
        message[device, :, :] = total


def last_kernel(scaling, got, basis, image, result, alpha, beta):
    total = got[0]
    for device in range(1, got.shape[0]):
        total += got[device]
    turned = [total] + [pltpu.roll(total, 128 - K * place, 1) for place in range(1, 4)]
    alpha_t = jnp.concatenate(turned[:2])[:, :K]
    image_gram = jnp.concatenate(turned[2:])
    wide = jnp.zeros((128 - K, K), f32)
    square = dot_t(alpha_t, jnp.concatenate([alpha_t, wide]))
    upper, inverse = factor_of(image_gram - square)
    for block in range(OWN // K):
        where = slice(block * K, (block + 1) * K)
        residual = image[where, :] - dot(alpha_t, basis[where, :])
        result[where, :] = dot(inverse, residual) * scaling
    alpha[...] = flip(alpha_t)
    beta[...] = flip(upper)


def exchange(message, vectors, tiles, rows, columns):
    got = swap(message, COLUMN)
    sent = call(
        lower_kernel,
        out((NEARS, SLAB + EXTRA, 128), bf16),
        (rows, columns),
        (got, tiles),
        (pltpu.VMEM((NEARS * SLAB, 128), f32),),
    )
    got = swap(sent, NEAR)
    sent = call(near_kernel, out((FARS, 2 * OWN + EXTRA, 128), bf16), (), (got, vectors))
    got = swap(sent, FAR)
    sent, column_sums, piece = call(
        far_kernel,
        (out((NEARS, SLAB, 128), bf16), out((OWN, 128), f32), out((EXTRA, 128), bf16)),
        (),
        (got,),
    )
    got = swap(sent, NEAR)
    sent = call(
        upper_kernel,
        out((COLUMNS, OWN + EXTRA, 128), bf16),
        (rows, columns),
        (got, tiles, piece),
        (pltpu.VMEM((COLUMNS * OWN, 128), f32),),
    )
    return swap(sent, COLUMN), column_sums


def local(start_block, tile_values, tile_rows, tile_columns, diagonal_blocks):
    start = start_block.reshape(OWN, 128)
    matrix = (tile_values[0, 0], tile_rows[0, 0], tile_columns[0, 0])
    first_message = out((COLUMNS, OWN + EXTRA, 128), bf16)
    vectors = out((OWN, 128), f32)
    square = out((K, K), f32)
    message = call(prepare_kernel, first_message, (), (start,))
    got, column_sums = exchange(message, start, *matrix)
    first, start_sum, message = call(
        middle_kernel,
        (vectors, out((K, 128), f32), first_message),
        (),
        (got, column_sums, start, diagonal_blocks),
    )
    inverse_start = call(factor_kernel, square, (), (start_sum,))
    got, column_sums = exchange(message, first, *matrix)
    planes, depths = lax.axis_size(PLANE), lax.axis_size(DEPTH)
    basis, image, alpha_first, beta_first, message = call(
        finish_kernel,
        (vectors, vectors, square, square, out((planes, K // 2, 128), f32)),
        (),
        (got, column_sums, start, first, diagonal_blocks, inverse_start),
    )
    got = swap(message, PLANE)
    message = call(plane_kernel, out((depths, K // 2, 128), f32), (), (got,))
    got = swap(message, DEPTH)
    scaling = math.sqrt(start_block.shape[0] * start_block.shape[2] * planes * depths)
    result, alpha_last, beta_last = call(
        functools.partial(last_kernel, scaling),
        (vectors, square, square),
        (),
        (got, basis, image),
    )
    return (
        result.reshape(start_block.shape),
        jnp.stack([alpha_first, alpha_last]),
        jnp.stack([beta_first, beta_last]),
    )


def solution(mesh):
    split = Mesh(mesh.devices.reshape(2, FARS, 2, 2, 4, 2), AXES)
    rows = ("x_high", "far", "near")
    owner = P((*COLUMN, *rows), None, None)
    placed = (
        owner,
        P(rows, COLUMN, None, None, None),
        P(rows, COLUMN, None),
        P(rows, COLUMN, None),
        owner,
    )
    return jax.shard_map(
        local,
        mesh=split,
        in_specs=placed,
        out_specs=(owner, P(), P()),
        check_vma=False,
    )
```

time: 312 us -> 215 us (0.69)
  waiting for transfers between devices: 137 us -> 4.93 us
  blocking collectives: 62.3 us -> 174 us
  starting transfers between devices: 53.8 us -> 9.98 us
  other arithmetic: 27.1 us -> 0.63 us
  Pallas kernels: 0 us -> 19.7 us
  matrix products: 13.7 us -> 0 us
  local copies, waits for them, and re-layouts: 15 us -> 3.49 us
    all_to_all x8 -> x1, waiting for transfers between devices: 137 us -> 4.93 us  [swap(): return lax.all_to_all(parts, axis, 0, 0, tiled=True)]
    all_to_all x4 -> x11, blocking collectives: 62.3 us -> 174 us  [swap(): return lax.all_to_all(parts, axis, 0, 0, tiled=True)]
    all_to_all x8 -> x1, starting transfers between devices: 53.8 us -> 9.98 us  [swap(): return lax.all_to_all(parts, axis, 0, 0, tiled=True)]
    another operation x17 -> x0, other arithmetic: 20.2 us -> none  [the longest x9 10.9 us: factor_of(): factor = jnp.linalg.cholesky(gram)]
    pallas_call x0 -> x14, Pallas kernels: none -> 19.7 us  [call(): pl.pallas_call(kernel, out_shape=outs, in_specs=specs, out_specs=jax.tree...]
    dot_general x33 -> x0, matrix products: 13 us -> none  [the longest x4 4.02 us: block_sums(): return jnp.dot(picker, products, precision=highest)]
    all_to_all x4 -> x0, other arithmetic: 4.72 us -> none  [swap(): return lax.all_to_all(parts, axis, 0, 0, tiled=True)]
    unnamed x42 -> x18, local copies, waits for them, and re-layouts: 7.49 us -> 3.49 us
  transfers between devices with their start and end apart: 8 -> 1, of which waited for: 8 -> 1; matrix products, arithmetic and copies ran while one was open for 12% -> 0% of each run, Pallas kernels for 0% -> 1%
where the time goes in v4:
time: 215 us; the launch traced here: 214 us
  blocking collectives  174 us (81%)
  Pallas kernels  19.7 us (9%)
  starting transfers between devices  9.98 us (5%)
  waiting for transfers between devices  4.93 us (2%)
  local copies, waits for them, and re-layouts  3.49 us (2%)
    all_to_all x11, blocking collectives, swap(): return lax.all_to_all(parts, axis, 0, 0, tiled=True)  174 us
    pallas_call x14, Pallas kernels, call(): pl.pallas_call(kernel, out_shape=outs, in_specs=specs, out_specs=jax.tree...  19.7 us
    all_to_all x1, starting transfers between devices, swap(): return lax.all_to_all(parts, axis, 0, 0, tiled=True)  9.98 us
    all_to_all x1, waiting for transfers between devices, swap(): return lax.all_to_all(parts, axis, 0, 0, tiled=True)  4.93 us
  transfers between devices with their start and end apart: 1, of which 1 were waited for; matrix products, arithmetic and copies ran while one was open for 0% of the time, Pallas kernels for 1%

profile of v4, /device:TPU:1, one launch (start us, length us, event | category | flops | bytes accessed | tf_op | source)
XLA Modules:
  0.0 213.5 jit_solution(17791820921488777142)
XLA Ops:
  0.6 0.0 copy-start.2
  0.6 0.7 copy-done.2
  1.4 0.4 shard_map.76
  1.8 17.1 %all_to_all.60.got = bf16[16,80,128]{2,1,0:T(8,128)(2,1)S(1)} all-to-all(bf16[16,80,128]{2,1,0:T(8,128)(2,1)S(1)} %shard_map.76), channel_id=1, replica_groups=mesh['x_high'=2,'far'=8,'near'=2,'x_low'=2,'y'=4,'core'=2] {'x_low','y',..., dimensions={0} | all-to-all | bytes 655360 | tf_op jit(solution)/shard_map/all_to_all | solution.py:35
  18.8 0.0 copy-start
  18.8 1.4 copy-done
  20.2 0.0 copy-start.5
  20.2 0.7 copy-done.5
  20.9 0.0 copy-start.7
  20.9 0.7 copy-done.7
  21.5 0.0 copy-start.3
  21.5 1.1 shard_map.77
  22.7 11.6 %all_to_all.61.got = bf16[4,528,128]{2,1,0:T(8,128)(2,1)S(1)} all-to-all(bf16[4,528,128]{2,1,0:T(8,128)(2,1)S(1)} %shard_map.77), channel_id=1, replica_groups=mesh['x_high'=2,'far'=8,'near'=2,'x_low'=2,'y'=4,'core'=2] {'x_high','ne..., dimensions={0} | all-to-all | bytes 1081344 | tf_op jit(solution)/shard_map/all_to_all | solution.py:35
  34.3 0.0 copy-done.3
  34.3 0.0 copy-start.1
  34.3 0.0 copy-start.6
  34.3 0.0 copy-start.8
  34.3 0.1 shard_map.78
  34.4 32.8 %all_to_all.62.got = bf16[8,144,128]{2,1,0:T(8,128)(2,1)S(1)} all-to-all(bf16[8,144,128]{2,1,0:T(8,128)(2,1)S(1)} %shard_map.78), channel_id=1, replica_groups=mesh['x_high'=2,'far'=8,'near'=2,'x_low'=2,'y'=4,'core'=2] {'far'}, dimensions={0} | all-to-all | bytes 589824 | tf_op jit(solution)/shard_map/all_to_all | solution.py:35
  67.2 0.2 shard_map.79
  67.4 9.9 %all_to_all.63.got = bf16[4,512,128]{2,1,0:T(8,128)(2,1)S(1)} all-to-all(bf16[4,512,128]{2,1,0:T(8,128)(2,1)S(1)} %get-tuple-element.20), channel_id=1, replica_groups=mesh['x_high'=2,'far'=8,'near'=2,'x_low'=2,'y'=4,'core'=2] {'x_high','ne..., dimensions={0} | all-to-all | bytes 1048576 | tf_op jit(solution)/shard_map/all_to_all | solution.py:35
  77.3 0.0 copy-start.4
  77.3 0.0 copy-done.1
  77.3 0.0 copy-done.6
  77.3 0.0 copy-done.8
  77.3 1.5 shard_map.80
  78.8 17.4 %all_to_all.64.got = bf16[16,80,128]{2,1,0:T(8,128)(2,1)S(1)} all-to-all(bf16[16,80,128]{2,1,0:T(8,128)(2,1)S(1)} %shard_map.80), channel_id=1, replica_groups=mesh['x_high'=2,'far'=8,'near'=2,'x_low'=2,'y'=4,'core'=2] {'x_low','y',..., dimensions={0} | all-to-all | bytes 655360 | tf_op jit(solution)/shard_map/all_to_all | solution.py:35
  96.2 0.0 copy-done.4
  96.2 0.7 shard_map.81
  96.9 11.4 %all_to_all.65.got = bf16[16,80,128]{2,1,0:T(8,128)(2,1)S(1)} all-to-all(bf16[16,80,128]{2,1,0:T(8,128)(2,1)S(1)} %get-tuple-element.23), channel_id=1, replica_groups=mesh['x_high'=2,'far'=8,'near'=2,'x_low'=2,'y'=4,'core'=2] {'x_low','y',..., dimensions={0} | all-to-all | bytes 655360 | tf_op jit(solution)/shard_map/all_to_all | solution.py:35
  108.3 1.1 shard_map.82
  109.4 11.5 %all_to_all.66.got = bf16[4,528,128]{2,1,0:T(8,128)(2,1)S(1)} all-to-all(bf16[4,528,128]{2,1,0:T(8,128)(2,1)S(1)} %shard_map.82), channel_id=1, replica_groups=mesh['x_high'=2,'far'=8,'near'=2,'x_low'=2,'y'=4,'core'=2] {'x_high','ne..., dimensions={0} | all-to-all | bytes 1081344 | tf_op jit(solution)/shard_map/all_to_all | solution.py:35
  120.9 0.1 shard_map.83
  121.0 23.1 %all_to_all.67.got = bf16[8,144,128]{2,1,0:T(8,128)(2,1)S(1)} all-to-all(bf16[8,144,128]{2,1,0:T(8,128)(2,1)S(1)} %shard_map.83), channel_id=1, replica_groups=mesh['x_high'=2,'far'=8,'near'=2,'x_low'=2,'y'=4,'core'=2] {'far'}, dimensions={0} | all-to-all | bytes 589824 | tf_op jit(solution)/shard_map/all_to_all | solution.py:35
  144.1 0.2 shard_map.84
  144.3 9.9 %all_to_all.68.got = bf16[4,512,128]{2,1,0:T(8,128)(2,1)S(1)} all-to-all(bf16[4,512,128]{2,1,0:T(8,128)(2,1)S(1)} %get-tuple-element.25), channel_id=1, replica_groups=mesh['x_high'=2,'far'=8,'near'=2,'x_low'=2,'y'=4,'core'=2] {'x_high','ne..., dimensions={0} | all-to-all | bytes 1048576 | tf_op jit(solution)/shard_map/all_to_all | solution.py:35
  154.2 2.2 %shard_map.85 = bf16[16,80,128]{2,1,0:T(8,128)(2,1)} custom-call(s32[48]{0:T(128)S(1)} %bitcast.24, s32[48]{0:T(128)S(1)} %bitcast.28, bf16[4,512,128]{2,1,0:T(8,128)(2,1)S(1)} %all_to_all.68.got, bf16[48,128,128]{2,1,0:T(8,128)(2,1)S(1)} %bitcast.12, bf16[16,128]{1,0:T(8,128)(2,1)S(1)} %get-tuple-element.26.piece), custom_call_target="tpu_custom_call" | custom-call | tf_op jit(solution)/shard_map/pallas_call | solution.py:41
  156.5 10.0 %all-to-all-start.9 = ((bf16[16,80,128]{2,1,0:T(8,128)(2,1)}), bf16[16,80,128]{2,1,0:T(8,128)(2,1)S(1)}, u32[]{:S(2)}, u32[]{:S(2)}) async-start(bf16[16,80,128]{2,1,0:T(8,128)(2,1)} %shard_map.85), calls=%async_computation.9 | async-start | bytes 655360 | tf_op jit(solution)/shard_map/all_to_all | solution.py:35
  166.4 2.8 %shard_map.86.inverse_start = f32[32,32]{1,0:T(8,128)S(1)} custom-call(f32[32,128]{1,0:T(8,128)S(1)} %get-tuple-element.28.gram), custom_call_target="tpu_custom_call" | custom-call | tf_op jit(solution)/shard_map/pallas_call | solution.py:41
  169.2 4.9 %all-to-all-done.9.got = bf16[16,80,128]{2,1,0:T(8,128)(2,1)S(1)} async-done(((bf16[16,80,128]{2,1,0:T(8,128)(2,1)}), bf16[16,80,128]{2,1,0:T(8,128)(2,1)S(1)}, u32[]{:S(2)}, u32[]{:S(2)}) %all-to-all-start.9) | async-done | bytes 327712 | tf_op jit(solution)/shard_map/all_to_all | solution.py:35
  174.1 5.3 %shard_map.87 = (f32[64,128]{1,0:T(8,128)S(1)}, f32[64,128]{1,0:T(8,128)S(1)}, f32[32,32]{1,0:T(8,128)S(1)}, f32[32,32]{1,0:T(8,128)S(1)}, f32[32,16,128]{2,1,0:T(8,128)S(1)}) custom-call(bf16[16,80,128]{2,1,0:T(8,128)(2,1)S(1)} %all-to-all-done.9.got, f32[64,128]{1,0:T(8,128)S(1)} %get-tuple-element.27.column_sums, f32[64,128]{1,0:T(8,128)S(1)} %bitcast.16, ...), custom_call_target="tpu_custom_call" | custom-call | tf_op jit(solution)/shard_map/pallas_call | solution.py:41
  179.4 13.3 %all_to_all.69.got = f32[32,16,128]{2,1,0:T(8,128)S(1)} all-to-all(f32[32,16,128]{2,1,0:T(8,128)S(1)} %get-tuple-element.29), channel_id=1, replica_groups=mesh['x_high'=2,'far'=8,'near'=2,'x_low'=2,'y'=4,'core'=2] {'x_high','x_..., dimensions={0} | all-to-all | bytes 524288 | tf_op jit(solution)/shard_map/all_to_all | solution.py:35
  192.8 16.2 %all_to_all.70.got = f32[16,16,128]{2,1,0:T(8,128)S(1)} all-to-all(f32[16,16,128]{2,1,0:T(8,128)S(1)} %shard_map.88), channel_id=1, replica_groups=mesh['x_high'=2,'far'=8,'near'=2,'x_low'=2,'y'=4,'core'=2] {'far','near'}, dimensions={0} | all-to-all | bytes 262144 | tf_op jit(solution)/shard_map/all_to_all | solution.py:35
  208.9 3.9 %shard_map.89 = (f32[64,128]{1,0:T(8,128)}, f32[32,32]{1,0:T(8,128)S(1)}, f32[32,32]{1,0:T(8,128)S(1)}) custom-call(f32[16,16,128]{2,1,0:T(8,128)S(1)} %all_to_all.70.got, f32[64,128]{1,0:T(8,128)S(1)} %get-tuple-element.30.basis, f32[64,128]{1,0:T(8,128)S(1)} %get-tuple-element.31.image), custom_call_target="tpu_custom_call" | custom-call | tf_op jit(solution)/shard_map/pallas_call | solution.py:41
  212.9 0.6 pad_maximum_fusion
  (1 shorter events, 0.0 us)
Async XLA Ops:
  0.6 0.8 copy-start.2
  18.8 1.4 copy-start
  20.2 0.7 copy-start.5
  20.9 0.7 copy-start.7
  21.5 12.7 %copy-start.3 = (f32[2,32,128]{2,1,0:T(8,128)S(1)}, f32[2,32,128]{2,1,0:T(8,128)}, u32[]{:S(2)}) copy-start(f32[2,32,128]{2,1,0:T(8,128)} %param.5) | copy-start | bytes 98308
  34.3 43.0 %copy-start.1 = (bf16[1,1,48,128,128]{4,3,2,1,0:T(8,128)(2,1)S(1)}, bf16[1,1,48,128,128]{4,3,2,1,0:T(8,128)(2,1)}, u32[]{:S(2)}) copy-start(bf16[1,1,48,128,128]{4,3,2,1,0:T(8,128)(2,1)} %param.6) | copy-start | bytes 4718596
  34.3 43.0 %copy-start.6 = (s32[1,1,48]{2,1,0:T(1,128)S(1)}, s32[1,1,48]{2,1,0:T(1,128)}, u32[]{:S(2)}) copy-start(s32[1,1,48]{2,1,0:T(1,128)} %param.7) | copy-start | bytes 580
  34.3 43.0 %copy-start.8 = (s32[1,1,48]{2,1,0:T(1,128)S(1)}, s32[1,1,48]{2,1,0:T(1,128)}, u32[]{:S(2)}) copy-start(s32[1,1,48]{2,1,0:T(1,128)} %param.8) | copy-start | bytes 580
  77.3 18.9 %copy-start.4 = (bf16[2,128,128]{2,1,0:T(8,128)(2,1)S(1)}, bf16[2,128,128]{2,1,0:T(8,128)(2,1)}, u32[]{:S(2)}) copy-start(bf16[2,128,128]{2,1,0:T(8,128)(2,1)} %diagonal.3) | copy-start | bytes 196612
  156.5 17.7 %all-to-all-start.9 = ((bf16[16,80,128]{2,1,0:T(8,128)(2,1)}), bf16[16,80,128]{2,1,0:T(8,128)(2,1)S(1)}, u32[]{:S(2)}, u32[]{:S(2)}) async-start(bf16[16,80,128]{2,1,0:T(8,128)(2,1)} %shard_map.85), calls=%async_computation.9 | async-start | bytes 655360 | tf_op jit(solution)/shard_map/all_to_all | solution.py:35

commit v5 on v4

--- a/solution.py
+++ b/solution.py
@@ -25,6 +25,7 @@
 EXTRA = 16
 TERMS = 3
 GROUP = 8
+PANEL = 8
 
 highest = lax.Precision.HIGHEST
 f32 = jnp.float32
@@ -112,14 +113,25 @@
     shape = (K, 128)
     row, column = iota(shape, 0), iota(shape, 1)
     work = jnp.where(column < K, gram, jnp.where(column == row + K, 1.0, 0.0))
-    for step in range(K):
-        across = jnp.broadcast_to(work[:, step : step + 1], shape)
-        pivot = across[step : step + 1, :]
-        guess = lax.rsqrt(pivot)
-        scale = guess * (1.5 - 0.5 * pivot * guess * guess)
-        lead = work[step : step + 1, :] * scale
-        lower = work - (across * scale) * lead
-        work = jnp.where(row > step, lower, jnp.where(row == step, lead, work))
+    for base in range(0, K, PANEL):
+        columns = [
+            jnp.broadcast_to(work[:, base + step : base + step + 1], shape) for step in range(PANEL)
+        ]
+        leads = [work[base + step : base + step + 1, :] for step in range(PANEL)]
+        for step in range(PANEL):
+            scale = lax.rsqrt(columns[step][base + step : base + step + 1, :])
+            columns[step] *= scale
+            leads[step] *= scale
+            for later in range(step + 1, PANEL):
+                share = columns[step][base + later : base + later + 1, :]
+                columns[later] -= columns[step] * share
+                leads[later] -= leads[step] * share
+        lower = work
+        for step in range(PANEL):
+            lower -= columns[step] * leads[step]
+        work = jnp.where(row >= base + PANEL, lower, work)
+        for step in range(PANEL):
+            work = jnp.where(row == base + step, leads[step], work)
     upper = jnp.where((column < K) & (column >= row), work, 0.0)
     inverse = pltpu.roll(work, 128 - K, 1)
     return upper[:, :K], inverse[:, :K]
@@ -139,6 +151,10 @@
     message[:, OWN:, :] = spread_slices(grams).reshape(COLUMNS, EXTRA, 128)
     for device in range(COLUMNS):
         message[device, :OWN, :] = narrow
+
+
+def stage_kernel(tiles, staged):
+    staged[...] = tiles[...]
 
 
 def prepare_kernel(start, message):
@@ -149,17 +165,17 @@
     fill_first(message, start[...].astype(bf16), grams)
 
 
-def lower_kernel(rows, columns, got, tiles, message, total):
+def lower_kernel(lists, got, tiles, message, total):
     total[...] = jnp.zeros_like(total)
     count = tiles.shape[0]
     for base in range(0, count, GROUP):
         parts = []
         for tile in range(base, base + GROUP):
-            place = rows[tile]
+            place = lists[tile]
             vectors = got[place >> 1, pl.ds(pl.multiple_of((place & 1) * K, K), K), :]
             parts.append(jnp.dot(vectors, tiles[tile], preferred_element_type=f32))
         for tile in range(base, base + GROUP):
-            place = columns[tile]
+            place = lists[count + tile]
             owner = place >> 1
             near = (owner >> 4) * 2 + (owner & 1)
             spot = (near * FARS + ((owner >> 1) & 7)) * 2 + (place & 1)
@@ -194,20 +210,20 @@
         message[device, :, :] = slab
 
 
-def upper_kernel(rows, columns, got, tiles, piece, message, total):
+def upper_kernel(lists, got, tiles, piece, message, total):
     total[...] = jnp.zeros_like(total)
     count = tiles.shape[0]
     for base in range(0, count, GROUP):
         parts = []
         for tile in range(base, base + GROUP):
-            place = columns[tile]
+            place = lists[count + tile]
             owner = place >> 1
             near = (owner >> 4) * 2 + (owner & 1)
             spot = ((owner >> 1) & 7) * 2 + (place & 1)
             vectors = got[near, pl.ds(pl.multiple_of(spot * K, K), K), :]
             parts.append(dot_t(vectors, tiles[tile], None))
         for tile in range(base, base + GROUP):
-            where = pl.ds(pl.multiple_of(rows[tile] * K, K), K)
+            where = pl.ds(pl.multiple_of(lists[tile] * K, K), K)
             total[where, :] += parts[tile - base]
     message[:, :OWN, :] = total[...].astype(bf16).reshape(COLUMNS, OWN, 128)
     for device in range(COLUMNS):
@@ -287,7 +303,7 @@
         message[device, :, :] = total
 
 
-def last_kernel(scaling, got, basis, image, result, alpha, beta):
+def last_kernel(scaling, got, basis, image, alpha_first, beta_first, result, alphas, betas):
     total = got[0]
     for device in range(1, got.shape[0]):
         total += got[device]
@@ -301,16 +317,18 @@
         where = slice(block * K, (block + 1) * K)
         residual = image[where, :] - dot(alpha_t, basis[where, :])
         result[where, :] = dot(inverse, residual) * scaling
-    alpha[...] = flip(alpha_t)
-    beta[...] = flip(upper)
-
-
-def exchange(message, vectors, tiles, rows, columns):
+    alphas[0] = alpha_first[...]
+    alphas[1] = flip(alpha_t)
+    betas[0] = beta_first[...]
+    betas[1] = flip(upper)
+
+
+def exchange(message, vectors, tiles, lists):
     got = swap(message, COLUMN)
     sent = call(
         lower_kernel,
         out((NEARS, SLAB + EXTRA, 128), bf16),
-        (rows, columns),
+        (lists,),
         (got, tiles),
         (pltpu.VMEM((NEARS * SLAB, 128), f32),),
     )
@@ -327,7 +345,7 @@
     sent = call(
         upper_kernel,
         out((COLUMNS, OWN + EXTRA, 128), bf16),
-        (rows, columns),
+        (lists,),
         (got, tiles, piece),
         (pltpu.VMEM((COLUMNS * OWN, 128), f32),),
     )
@@ -336,7 +354,11 @@
 
 def local(start_block, tile_values, tile_rows, tile_columns, diagonal_blocks):
     start = start_block.reshape(OWN, 128)
-    matrix = (tile_values[0, 0], tile_rows[0, 0], tile_columns[0, 0])
+    tiles = tile_values[0, 0]
+    matrix = (
+        call(stage_kernel, out(tiles.shape, bf16), (), (tiles,)),
+        jnp.concatenate([tile_rows[0, 0], tile_columns[0, 0]]),
+    )
     first_message = out((COLUMNS, OWN + EXTRA, 128), bf16)
     vectors = out((OWN, 128), f32)
     square = out((K, K), f32)
@@ -361,17 +383,14 @@
     message = call(plane_kernel, out((depths, K // 2, 128), f32), (), (got,))
     got = swap(message, DEPTH)
     scaling = math.sqrt(start_block.shape[0] * start_block.shape[2] * planes * depths)
-    result, alpha_last, beta_last = call(
+    pair = out((2, K, K), f32)
+    result, alphas, betas = call(
         functools.partial(last_kernel, scaling),
-        (vectors, square, square),
+        (vectors, pair, pair),
         (),
-        (got, basis, image),
-    )
-    return (
-        result.reshape(start_block.shape),
-        jnp.stack([alpha_first, alpha_last]),
-        jnp.stack([beta_first, beta_last]),
-    )
+        (got, basis, image, alpha_first, beta_first),
+    )
+    return result.reshape(start_block.shape), alphas, betas
 
 
 def solution(mesh):

time: 215 us -> 208 us (0.967)
  blocking collectives: 174 us -> 156 us
  starting transfers between devices: 9.98 us -> 20.2 us
  waiting for transfers between devices: 4.93 us -> 12.5 us
  Pallas kernels: 19.7 us -> 14.4 us
    all_to_all x11 -> x10, blocking collectives: 174 us -> 156 us  [swap(): return lax.all_to_all(parts, axis, 0, 0, tiled=True)]
    all_to_all x1 -> x2, starting transfers between devices: 9.98 us -> 20.2 us  [swap(): return lax.all_to_all(parts, axis, 0, 0, tiled=True)]
    all_to_all x1 -> x2, waiting for transfers between devices: 4.93 us -> 12.5 us  [swap(): return lax.all_to_all(parts, axis, 0, 0, tiled=True)]
    pallas_call x14 -> x15, Pallas kernels: 19.7 us -> 14.4 us  [call(): pl.pallas_call(kernel, out_shape=outs, in_specs=specs, out_specs=jax.tree...]
  transfers between devices with their start and end apart: 1 -> 2, of which waited for: 1 -> 2; matrix products, arithmetic and copies ran while one was open for 0% -> 0% of each run, Pallas kernels for 1% -> 0%
where the time goes in v5:
time: 208 us; the launch traced here: 207 us
  blocking collectives  156 us (75%)
  starting transfers between devices  20.2 us (10%)
  Pallas kernels  14.4 us (7%)
  waiting for transfers between devices  12.5 us (6%)
  local copies, waits for them, and re-layouts  2.73 us (1%)
    all_to_all x10, blocking collectives, swap(): return lax.all_to_all(parts, axis, 0, 0, tiled=True)  156 us
    all_to_all x2, starting transfers between devices, swap(): return lax.all_to_all(parts, axis, 0, 0, tiled=True)  20.2 us
    pallas_call x15, Pallas kernels, call(): pl.pallas_call(kernel, out_shape=outs, in_specs=specs, out_specs=jax.tree...  14.4 us
    all_to_all x2, waiting for transfers between devices, swap(): return lax.all_to_all(parts, axis, 0, 0, tiled=True)  12.5 us
  transfers between devices with their start and end apart: 2, of which 2 were waited for; matrix products, arithmetic and copies ran while one was open for 0% of the time, Pallas kernels for 0%

profile of v5, /device:TPU:1, one launch (start us, length us, event | category | flops | bytes accessed | tf_op | source)
XLA Modules:
  0.0 206.8 jit_solution(9463492993862323934)
XLA Ops:
  0.6 0.0 copy-start.1
  0.6 0.7 copy-done.1
  1.4 1.1 shard_map.76
  2.5 10.2 %all-to-all-start = ((bf16[16,80,128]{2,1,0:T(8,128)(2,1)}), bf16[16,80,128]{2,1,0:T(8,128)(2,1)S(1)}, u32[]{:S(2)}, u32[]{:S(2)}) async-start(bf16[16,80,128]{2,1,0:T(8,128)(2,1)} %shard_map.76), calls=%async_computation | async-start | bytes 655360 | tf_op jit(solution)/shard_map/all_to_all | solution.py:36
  12.7 0.0 copy-start
  12.7 1.4 copy-done
  14.1 0.0 copy-start.4
  14.1 0.0 copy-start.5
  14.1 0.1 shard_map.77.tiles
  14.2 0.5 copy-done.4
  14.7 0.0 copy-done.5
  14.8 0.1 pad_add_fusion.lists
  14.8 0.0 copy-start.2
  14.8 5.6 %all-to-all-done.got = bf16[16,80,128]{2,1,0:T(8,128)(2,1)S(1)} async-done(((bf16[16,80,128]{2,1,0:T(8,128)(2,1)}), bf16[16,80,128]{2,1,0:T(8,128)(2,1)S(1)}, u32[]{:S(2)}, u32[]{:S(2)}) %all-to-all-start) | async-done | bytes 327712 | tf_op jit(solution)/shard_map/all_to_all | solution.py:36
  20.5 1.1 shard_map.78
  21.6 11.5 %all_to_all.60.got = bf16[4,528,128]{2,1,0:T(8,128)(2,1)S(1)} all-to-all(bf16[4,528,128]{2,1,0:T(8,128)(2,1)S(1)} %shard_map.78), channel_id=1, replica_groups=mesh['x_high'=2,'far'=8,'near'=2,'x_low'=2,'y'=4,'core'=2] {'x_high','ne..., dimensions={0} | all-to-all | bytes 1081344 | tf_op jit(solution)/shard_map/all_to_all | solution.py:36
  33.1 0.0 copy-done.2
  33.1 0.1 shard_map.79
  33.2 32.1 %all_to_all.61.got = bf16[8,144,128]{2,1,0:T(8,128)(2,1)S(1)} all-to-all(bf16[8,144,128]{2,1,0:T(8,128)(2,1)S(1)} %shard_map.79), channel_id=1, replica_groups=mesh['x_high'=2,'far'=8,'near'=2,'x_low'=2,'y'=4,'core'=2] {'far'}, dimensions={0} | all-to-all | bytes 589824 | tf_op jit(solution)/shard_map/all_to_all | solution.py:36
  65.3 0.2 shard_map.80
  65.5 9.9 %all_to_all.62.got = bf16[4,512,128]{2,1,0:T(8,128)(2,1)S(1)} all-to-all(bf16[4,512,128]{2,1,0:T(8,128)(2,1)S(1)} %get-tuple-element.20), channel_id=1, replica_groups=mesh['x_high'=2,'far'=8,'near'=2,'x_low'=2,'y'=4,'core'=2] {'x_high','ne..., dimensions={0} | all-to-all | bytes 1048576 | tf_op jit(solution)/shard_map/all_to_all | solution.py:36
  75.3 0.0 copy-start.3
  75.3 1.5 shard_map.81
  76.8 17.4 %all_to_all.63.got = bf16[16,80,128]{2,1,0:T(8,128)(2,1)S(1)} all-to-all(bf16[16,80,128]{2,1,0:T(8,128)(2,1)S(1)} %shard_map.81), channel_id=1, replica_groups=mesh['x_high'=2,'far'=8,'near'=2,'x_low'=2,'y'=4,'core'=2] {'x_low','y',..., dimensions={0} | all-to-all | bytes 655360 | tf_op jit(solution)/shard_map/all_to_all | solution.py:36
  94.2 0.0 copy-done.3
  94.3 0.7 shard_map.82
  94.9 11.4 %all_to_all.64.got = bf16[16,80,128]{2,1,0:T(8,128)(2,1)S(1)} all-to-all(bf16[16,80,128]{2,1,0:T(8,128)(2,1)S(1)} %get-tuple-element.23), channel_id=1, replica_groups=mesh['x_high'=2,'far'=8,'near'=2,'x_low'=2,'y'=4,'core'=2] {'x_low','y',..., dimensions={0} | all-to-all | bytes 655360 | tf_op jit(solution)/shard_map/all_to_all | solution.py:36
  106.3 1.1 shard_map.83
  107.4 11.5 %all_to_all.65.got = bf16[4,528,128]{2,1,0:T(8,128)(2,1)S(1)} all-to-all(bf16[4,528,128]{2,1,0:T(8,128)(2,1)S(1)} %shard_map.83), channel_id=1, replica_groups=mesh['x_high'=2,'far'=8,'near'=2,'x_low'=2,'y'=4,'core'=2] {'x_high','ne..., dimensions={0} | all-to-all | bytes 1081344 | tf_op jit(solution)/shard_map/all_to_all | solution.py:36
  118.9 0.1 shard_map.84
  119.0 23.1 %all_to_all.66.got = bf16[8,144,128]{2,1,0:T(8,128)(2,1)S(1)} all-to-all(bf16[8,144,128]{2,1,0:T(8,128)(2,1)S(1)} %shard_map.84), channel_id=1, replica_groups=mesh['x_high'=2,'far'=8,'near'=2,'x_low'=2,'y'=4,'core'=2] {'far'}, dimensions={0} | all-to-all | bytes 589824 | tf_op jit(solution)/shard_map/all_to_all | solution.py:36
  142.2 0.2 shard_map.85
  142.4 9.9 %all_to_all.67.got = bf16[4,512,128]{2,1,0:T(8,128)(2,1)S(1)} all-to-all(bf16[4,512,128]{2,1,0:T(8,128)(2,1)S(1)} %get-tuple-element.25), channel_id=1, replica_groups=mesh['x_high'=2,'far'=8,'near'=2,'x_low'=2,'y'=4,'core'=2] {'x_high','ne..., dimensions={0} | all-to-all | bytes 1048576 | tf_op jit(solution)/shard_map/all_to_all | solution.py:36
  152.2 2.2 %shard_map.86 = bf16[16,80,128]{2,1,0:T(8,128)(2,1)} custom-call(s32[96]{0:T(128)S(1)} %pad_add_fusion.lists, bf16[4,512,128]{2,1,0:T(8,128)(2,1)S(1)} %all_to_all.67.got, bf16[48,128,128]{2,1,0:T(8,128)(2,1)S(1)} %shard_map.77.tiles, bf16[16,128]{1,0:T(8,128)(2,1)S(1)} %get-tuple-element.26.piece), custom_call_target="tpu_custom_call" | custom-call | tf_op jit(solution)/shard_map/pallas_call | solution.py:42
  154.5 10.0 %all-to-all-start.9 = ((bf16[16,80,128]{2,1,0:T(8,128)(2,1)}), bf16[16,80,128]{2,1,0:T(8,128)(2,1)S(1)}, u32[]{:S(2)}, u32[]{:S(2)}) async-start(bf16[16,80,128]{2,1,0:T(8,128)(2,1)} %shard_map.86), calls=%async_computation.9 | async-start | bytes 655360 | tf_op jit(solution)/shard_map/all_to_all | solution.py:36
  164.5 0.7 shard_map.87.inverse_start
  165.2 6.9 %all-to-all-done.9.got = bf16[16,80,128]{2,1,0:T(8,128)(2,1)S(1)} async-done(((bf16[16,80,128]{2,1,0:T(8,128)(2,1)}), bf16[16,80,128]{2,1,0:T(8,128)(2,1)S(1)}, u32[]{:S(2)}, u32[]{:S(2)}) %all-to-all-start.9) | async-done | bytes 327712 | tf_op jit(solution)/shard_map/all_to_all | solution.py:36
  172.1 3.2 %shard_map.88 = (f32[64,128]{1,0:T(8,128)S(1)}, f32[64,128]{1,0:T(8,128)S(1)}, f32[32,32]{1,0:T(8,128)S(1)}, f32[32,32]{1,0:T(8,128)S(1)}, f32[32,16,128]{2,1,0:T(8,128)S(1)}) custom-call(bf16[16,80,128]{2,1,0:T(8,128)(2,1)S(1)} %all-to-all-done.9.got, f32[64,128]{1,0:T(8,128)S(1)} %get-tuple-element.27.column_sums, f32[64,128]{1,0:T(8,128)S(1)} %bitcast.9, ...), custom_call_target="tpu_custom_call" | custom-call | tf_op jit(solution)/shard_map/pallas_call | solution.py:42
  175.4 13.3 %all_to_all.68.got = f32[32,16,128]{2,1,0:T(8,128)S(1)} all-to-all(f32[32,16,128]{2,1,0:T(8,128)S(1)} %get-tuple-element.29), channel_id=1, replica_groups=mesh['x_high'=2,'far'=8,'near'=2,'x_low'=2,'y'=4,'core'=2] {'x_high','x_..., dimensions={0} | all-to-all | bytes 524288 | tf_op jit(solution)/shard_map/all_to_all | solution.py:36
  188.7 16.2 %all_to_all.69.got = f32[16,16,128]{2,1,0:T(8,128)S(1)} all-to-all(f32[16,16,128]{2,1,0:T(8,128)S(1)} %shard_map.89), channel_id=1, replica_groups=mesh['x_high'=2,'far'=8,'near'=2,'x_low'=2,'y'=4,'core'=2] {'far','near'}, dimensions={0} | all-to-all | bytes 262144 | tf_op jit(solution)/shard_map/all_to_all | solution.py:36
  204.9 1.9 shard_map.90
  (1 shorter events, 0.0 us)
Async XLA Ops:
  0.6 0.8 copy-start.1
  2.5 18.0 %all-to-all-start = ((bf16[16,80,128]{2,1,0:T(8,128)(2,1)}), bf16[16,80,128]{2,1,0:T(8,128)(2,1)S(1)}, u32[]{:S(2)}, u32[]{:S(2)}) async-start(bf16[16,80,128]{2,1,0:T(8,128)(2,1)} %shard_map.76), calls=%async_computation | async-start | bytes 655360 | tf_op jit(solution)/shard_map/all_to_all | solution.py:36
  12.7 1.4 copy-start
  14.1 0.7 copy-start.4
  14.1 0.7 copy-start.5
  14.8 18.2 %copy-start.2 = (f32[2,32,128]{2,1,0:T(8,128)S(1)}, f32[2,32,128]{2,1,0:T(8,128)}, u32[]{:S(2)}) copy-start(f32[2,32,128]{2,1,0:T(8,128)} %param.5) | copy-start | bytes 98308
  75.3 18.9 %copy-start.3 = (bf16[2,128,128]{2,1,0:T(8,128)(2,1)S(1)}, bf16[2,128,128]{2,1,0:T(8,128)(2,1)}, u32[]{:S(2)}) copy-start(bf16[2,128,128]{2,1,0:T(8,128)(2,1)} %diagonal.3) | copy-start | bytes 196612
  154.5 17.7 %all-to-all-start.9 = ((bf16[16,80,128]{2,1,0:T(8,128)(2,1)}), bf16[16,80,128]{2,1,0:T(8,128)(2,1)S(1)}, u32[]{:S(2)}, u32[]{:S(2)}) async-start(bf16[16,80,128]{2,1,0:T(8,128)(2,1)} %shard_map.86), calls=%async_computation.9 | async-start | bytes 655360 | tf_op jit(solution)/shard_map/all_to_all | solution.py:36

commit v6 on v5

--- a/solution.py
+++ b/solution.py
@@ -142,15 +142,9 @@
     return dot_t(eye, matrix)
 
 
-def shifted(block, place, places):
-    empty = jnp.zeros_like(block)
-    return jnp.concatenate([block if i == place else empty for i in range(places)], axis=0)
-
-
-def fill_first(message, narrow, grams):
-    message[:, OWN:, :] = spread_slices(grams).reshape(COLUMNS, EXTRA, 128)
-    for device in range(COLUMNS):
-        message[device, :OWN, :] = narrow
+def fill(message, rows):
+    for device in range(message.shape[0]):
+        message[device, : rows.shape[0], :] = rows
 
 
 def stage_kernel(tiles, staged):
@@ -158,11 +152,7 @@
 
 
 def prepare_kernel(start, message):
-    grams = jnp.zeros((K, 128), f32)
-    for block in range(OWN // K):
-        vectors = start[block * K : (block + 1) * K, :]
-        grams += dot_t(vectors, shifted(vectors, 0, 4))
-    fill_first(message, start[...].astype(bf16), grams)
+    fill(message, start[...].astype(bf16))
 
 
 def lower_kernel(lists, got, tiles, message, total):
@@ -182,9 +172,10 @@
             where = pl.ds(pl.multiple_of(spot * K, K), K)
             total[where, :] += parts[tile - base]
     message[:, :SLAB, :] = total[...].astype(bf16).reshape(NEARS, SLAB, 128)
-    piece = sum_slices(got[:, OWN:, :].reshape(COLUMNS * EXTRA, 128))
-    for device in range(NEARS):
-        message[device, SLAB:, :] = piece
+    if got.shape[1] > OWN:
+        piece = sum_slices(got[:, OWN:, :].reshape(COLUMNS * EXTRA, 128))
+        for device in range(NEARS):
+            message[device, SLAB:, :] = piece
 
 
 def near_kernel(got, vectors, message):
@@ -192,25 +183,25 @@
     for device in range(1, NEARS):
         total += got[device, :SLAB, :].astype(f32)
     message[:, OWN : 2 * OWN, :] = total.astype(bf16).reshape(FARS, OWN, 128)
-    piece = sum_slices(got[:, SLAB:, :].reshape(NEARS * EXTRA, 128))
-    narrow = vectors[...].astype(bf16)
-    for device in range(FARS):
-        message[device, :OWN, :] = narrow
-        message[device, 2 * OWN :, :] = piece
-
-
-def far_kernel(got, message, column_sums, piece):
+    fill(message, vectors[...].astype(bf16))
+    if got.shape[1] > SLAB:
+        piece = sum_slices(got[:, SLAB:, :].reshape(NEARS * EXTRA, 128))
+        for device in range(FARS):
+            message[device, 2 * OWN :, :] = piece
+
+
+def far_kernel(got, message, column_sums, *piece):
     total = got[0, OWN : 2 * OWN, :].astype(f32)
     for device in range(1, FARS):
         total += got[device, OWN : 2 * OWN, :].astype(f32)
     column_sums[...] = total
-    piece[...] = sum_slices(got[:, 2 * OWN :, :].reshape(FARS * EXTRA, 128))
-    slab = got[:, :OWN, :].reshape(SLAB, 128)
-    for device in range(NEARS):
-        message[device, :, :] = slab
-
-
-def upper_kernel(lists, got, tiles, piece, message, total):
+    if piece:
+        piece[0][...] = sum_slices(got[:, 2 * OWN :, :].reshape(FARS * EXTRA, 128))
+    fill(message, got[:, :OWN, :].reshape(SLAB, 128))
+
+
+def upper_kernel(lists, got, tiles, *refs):
+    *piece, message, total = refs
     total[...] = jnp.zeros_like(total)
     count = tiles.shape[0]
     for base in range(0, count, GROUP):
@@ -226,8 +217,9 @@
             where = pl.ds(pl.multiple_of(lists[tile] * K, K), K)
             total[where, :] += parts[tile - base]
     message[:, :OWN, :] = total[...].astype(bf16).reshape(COLUMNS, OWN, 128)
-    for device in range(COLUMNS):
-        message[device, OWN:, :] = piece[...]
+    if piece:
+        for device in range(COLUMNS):
+            message[device, OWN:, :] = piece[0][...]
 
 
 def image_of(got, column_sums, vectors, diagonal):
@@ -245,30 +237,28 @@
     return images
 
 
-def middle_kernel(got, column_sums, start, diagonal, image, start_sum, message):
+def middle_kernel(got, column_sums, start, diagonal, image, message):
     images = image_of(got, column_sums, start, diagonal)
-    start_sum[...] = join_slices(got[:, OWN:, :].reshape(COLUMNS * EXTRA, 128))
     grams = jnp.zeros((K, 128), f32)
+    empty = jnp.zeros((K, 128), f32)
     for block in range(OWN // K):
         where = slice(block * K, (block + 1) * K)
+        vectors = start[where, :]
         image[where, :] = images[block]
-        joint = jnp.concatenate([start[where, :], images[block]] + [jnp.zeros((K, 128), f32)] * 2)
-        grams += dot_t(images[block], joint)
-    fill_first(message, jnp.concatenate(images).astype(bf16), grams)
-
-
-def factor_kernel(gram, inverse):
-    inverse[...] = factor_of(gram[...])[1]
+        grams += dot_t(vectors, jnp.concatenate([vectors, empty, empty, empty]))
+        grams += dot_t(images[block], jnp.concatenate([empty, vectors, images[block], empty]))
+    fill(message, jnp.concatenate(images).astype(bf16))
+    message[:, OWN:, :] = spread_slices(grams).reshape(COLUMNS, EXTRA, 128)
 
 
 def finish_kernel(
-    got, column_sums, start, first, diagonal, inverse_start, basis, image, alpha, beta, message
+    got, column_sums, start, first, diagonal, basis, image, alpha, beta, message
 ):
     images = image_of(got, column_sums, first, diagonal)
     sums = join_slices(got[:, OWN:, :].reshape(COLUMNS * EXTRA, 128))
-    inverse = inverse_start[...]
-    alpha_t = dot_t(dot(inverse, sums[:, :K]), inverse)
-    image_gram = dot_t(dot(inverse, pltpu.roll(sums, 128 - K, 1)[:, :K]), inverse)
+    inverse = factor_of(sums)[1]
+    alpha_t = dot_t(dot(inverse, pltpu.roll(sums, 128 - K, 1)[:, :K]), inverse)
+    image_gram = dot_t(dot(inverse, pltpu.roll(sums, 128 - 2 * K, 1)[:, :K]), inverse)
     wide = jnp.zeros((128 - K, K), f32)
     square = dot_t(alpha_t, jnp.concatenate([alpha_t, wide]))
     upper, inverse_first = factor_of(
@@ -324,29 +314,28 @@
 
 
 def exchange(message, vectors, tiles, lists):
+    extra = message.shape[1] - OWN
     got = swap(message, COLUMN)
     sent = call(
         lower_kernel,
-        out((NEARS, SLAB + EXTRA, 128), bf16),
+        out((NEARS, SLAB + extra, 128), bf16),
         (lists,),
         (got, tiles),
         (pltpu.VMEM((NEARS * SLAB, 128), f32),),
     )
     got = swap(sent, NEAR)
-    sent = call(near_kernel, out((FARS, 2 * OWN + EXTRA, 128), bf16), (), (got, vectors))
+    sent = call(near_kernel, out((FARS, 2 * OWN + extra, 128), bf16), (), (got, vectors))
     got = swap(sent, FAR)
-    sent, column_sums, piece = call(
-        far_kernel,
-        (out((NEARS, SLAB, 128), bf16), out((OWN, 128), f32), out((EXTRA, 128), bf16)),
-        (),
-        (got,),
-    )
+    outs = [out((NEARS, SLAB, 128), bf16), out((OWN, 128), f32)]
+    if extra:
+        outs.append(out((extra, 128), bf16))
+    sent, column_sums, *piece = call(far_kernel, outs, (), (got,))
     got = swap(sent, NEAR)
     sent = call(
         upper_kernel,
-        out((COLUMNS, OWN + EXTRA, 128), bf16),
+        out((COLUMNS, OWN + extra, 128), bf16),
         (lists,),
-        (got, tiles, piece),
+        (got, tiles, *piece),
         (pltpu.VMEM((COLUMNS * OWN, 128), f32),),
     )
     return swap(sent, COLUMN), column_sums
@@ -359,25 +348,23 @@
         call(stage_kernel, out(tiles.shape, bf16), (), (tiles,)),
         jnp.concatenate([tile_rows[0, 0], tile_columns[0, 0]]),
     )
-    first_message = out((COLUMNS, OWN + EXTRA, 128), bf16)
     vectors = out((OWN, 128), f32)
     square = out((K, K), f32)
-    message = call(prepare_kernel, first_message, (), (start,))
+    message = call(prepare_kernel, out((COLUMNS, OWN, 128), bf16), (), (start,))
     got, column_sums = exchange(message, start, *matrix)
-    first, start_sum, message = call(
+    first, message = call(
         middle_kernel,
-        (vectors, out((K, 128), f32), first_message),
+        (vectors, out((COLUMNS, OWN + EXTRA, 128), bf16)),
         (),
         (got, column_sums, start, diagonal_blocks),
     )
-    inverse_start = call(factor_kernel, square, (), (start_sum,))
     got, column_sums = exchange(message, first, *matrix)
     planes, depths = lax.axis_size(PLANE), lax.axis_size(DEPTH)
     basis, image, alpha_first, beta_first, message = call(
         finish_kernel,
         (vectors, vectors, square, square, out((planes, K // 2, 128), f32)),
         (),
-        (got, column_sums, start, first, diagonal_blocks, inverse_start),
+        (got, column_sums, start, first, diagonal_blocks),
     )
     got = swap(message, PLANE)
     message = call(plane_kernel, out((depths, K // 2, 128), f32), (), (got,))

time: 208 us -> 204 us (0.981)
  blocking collectives: 156 us -> 170 us
  starting transfers between devices: 20.2 us -> 10.2 us
  waiting for transfers between devices: 12.5 us -> 5.08 us
    all_to_all x10 -> x11, blocking collectives: 156 us -> 170 us  [swap(): return lax.all_to_all(parts, axis, 0, 0, tiled=True)]
    all_to_all x2 -> x1, starting transfers between devices: 20.2 us -> 10.2 us  [swap(): return lax.all_to_all(parts, axis, 0, 0, tiled=True)]
    all_to_all x2 -> x1, waiting for transfers between devices: 12.5 us -> 5.08 us  [swap(): return lax.all_to_all(parts, axis, 0, 0, tiled=True)]
    pallas_call x15 -> x14, Pallas kernels: 14.4 us -> 13.2 us  [call(): pl.pallas_call(kernel, out_shape=outs, in_specs=specs, out_specs=jax.tree...]
  transfers between devices with their start and end apart: 2 -> 1, of which waited for: 2 -> 1; matrix products, arithmetic and copies ran while one was open for 0% -> 0% of each run, Pallas kernels for 0% -> 0%
where the time goes in v6:
time: 204 us; the launch traced here: 202 us
  blocking collectives  170 us (83%)
  Pallas kernels  13.2 us (6%)
  starting transfers between devices  10.2 us (5%)
  waiting for transfers between devices  5.08 us (2%)
  local copies, waits for them, and re-layouts  2.73 us (1%)
    all_to_all x11, blocking collectives, swap(): return lax.all_to_all(parts, axis, 0, 0, tiled=True)  170 us
    pallas_call x14, Pallas kernels, call(): pl.pallas_call(kernel, out_shape=outs, in_specs=specs, out_specs=jax.tree...  13.2 us
    all_to_all x1, starting transfers between devices, swap(): return lax.all_to_all(parts, axis, 0, 0, tiled=True)  10.2 us
    all_to_all x1, waiting for transfers between devices, swap(): return lax.all_to_all(parts, axis, 0, 0, tiled=True)  5.08 us
  transfers between devices with their start and end apart: 1, of which 1 were waited for; matrix products, arithmetic and copies ran while one was open for 0% of the time, Pallas kernels for 0%

profile of v6, /device:TPU:1, one launch (start us, length us, event | category | flops | bytes accessed | tf_op | source)
XLA Modules:
  0.0 202.4 jit_solution(18314921486731183537)
XLA Ops:
  0.6 0.0 copy-start.1
  0.6 0.7 copy-done.1
  1.4 0.7 shard_map.76
  2.1 10.2 %all-to-all-start = ((bf16[16,64,128]{2,1,0:T(8,128)(2,1)}), bf16[16,64,128]{2,1,0:T(8,128)(2,1)S(1)}, u32[]{:S(2)}, u32[]{:S(2)}) async-start(bf16[16,64,128]{2,1,0:T(8,128)(2,1)} %shard_map.76), calls=%async_computation | async-start | bytes 524288 | tf_op jit(solution)/shard_map/all_to_all | solution.py:36
  12.3 0.0 copy-start
  12.3 1.4 copy-done
  13.7 0.0 copy-start.4
  13.7 0.0 copy-start.5
  13.7 0.1 shard_map.77.tiles
  13.8 0.5 copy-done.4
  14.4 0.0 copy-done.5
  14.4 0.1 pad_add_fusion.lists
  14.5 0.0 copy-start.2
  14.5 5.1 %all-to-all-done.got = bf16[16,64,128]{2,1,0:T(8,128)(2,1)S(1)} async-done(((bf16[16,64,128]{2,1,0:T(8,128)(2,1)}), bf16[16,64,128]{2,1,0:T(8,128)(2,1)S(1)}, u32[]{:S(2)}, u32[]{:S(2)}) %all-to-all-start) | async-done | bytes 262176 | tf_op jit(solution)/shard_map/all_to_all | solution.py:36
  19.6 1.1 shard_map.78
  20.7 11.1 %all_to_all.60.got = bf16[4,512,128]{2,1,0:T(8,128)(2,1)S(1)} all-to-all(bf16[4,512,128]{2,1,0:T(8,128)(2,1)S(1)} %shard_map.78), channel_id=1, replica_groups=mesh['x_high'=2,'far'=8,'near'=2,'x_low'=2,'y'=4,'core'=2] {'x_high','ne..., dimensions={0} | all-to-all | bytes 1048576 | tf_op jit(solution)/shard_map/all_to_all | solution.py:36
  31.8 0.0 copy-done.2
  31.8 0.1 shard_map.79
  31.9 28.9 %all_to_all.61.got = bf16[8,128,128]{2,1,0:T(8,128)(2,1)S(1)} all-to-all(bf16[8,128,128]{2,1,0:T(8,128)(2,1)S(1)} %shard_map.79), channel_id=1, replica_groups=mesh['x_high'=2,'far'=8,'near'=2,'x_low'=2,'y'=4,'core'=2] {'far'}, dimensions={0} | all-to-all | bytes 524288 | tf_op jit(solution)/shard_map/all_to_all | solution.py:36
  60.8 0.1 shard_map.80
  60.9 10.7 %all_to_all.62.got = bf16[4,512,128]{2,1,0:T(8,128)(2,1)S(1)} all-to-all(bf16[4,512,128]{2,1,0:T(8,128)(2,1)S(1)} %get-tuple-element.18), channel_id=1, replica_groups=mesh['x_high'=2,'far'=8,'near'=2,'x_low'=2,'y'=4,'core'=2] {'x_high','ne..., dimensions={0} | all-to-all | bytes 1048576 | tf_op jit(solution)/shard_map/all_to_all | solution.py:36
  71.6 0.0 copy-start.3
  71.6 1.5 shard_map.81
  73.1 17.4 %all_to_all.63.got = bf16[16,64,128]{2,1,0:T(8,128)(2,1)S(1)} all-to-all(bf16[16,64,128]{2,1,0:T(8,128)(2,1)S(1)} %shard_map.81), channel_id=1, replica_groups=mesh['x_high'=2,'far'=8,'near'=2,'x_low'=2,'y'=4,'core'=2] {'x_low','y',..., dimensions={0} | all-to-all | bytes 524288 | tf_op jit(solution)/shard_map/all_to_all | solution.py:36
  90.5 0.0 copy-done.3
  90.5 0.7 shard_map.82
  91.2 11.2 %all_to_all.64.got = bf16[16,80,128]{2,1,0:T(8,128)(2,1)S(1)} all-to-all(bf16[16,80,128]{2,1,0:T(8,128)(2,1)S(1)} %get-tuple-element.20), channel_id=1, replica_groups=mesh['x_high'=2,'far'=8,'near'=2,'x_low'=2,'y'=4,'core'=2] {'x_low','y',..., dimensions={0} | all-to-all | bytes 655360 | tf_op jit(solution)/shard_map/all_to_all | solution.py:36
  102.4 1.1 shard_map.83
  103.5 11.5 %all_to_all.65.got = bf16[4,528,128]{2,1,0:T(8,128)(2,1)S(1)} all-to-all(bf16[4,528,128]{2,1,0:T(8,128)(2,1)S(1)} %shard_map.83), channel_id=1, replica_groups=mesh['x_high'=2,'far'=8,'near'=2,'x_low'=2,'y'=4,'core'=2] {'x_high','ne..., dimensions={0} | all-to-all | bytes 1081344 | tf_op jit(solution)/shard_map/all_to_all | solution.py:36
  115.0 0.1 shard_map.84
  115.1 22.8 %all_to_all.66.got = bf16[8,144,128]{2,1,0:T(8,128)(2,1)S(1)} all-to-all(bf16[8,144,128]{2,1,0:T(8,128)(2,1)S(1)} %shard_map.84), channel_id=1, replica_groups=mesh['x_high'=2,'far'=8,'near'=2,'x_low'=2,'y'=4,'core'=2] {'far'}, dimensions={0} | all-to-all | bytes 589824 | tf_op jit(solution)/shard_map/all_to_all | solution.py:36
  138.0 0.2 shard_map.85
  138.2 9.9 %all_to_all.67.got = bf16[4,512,128]{2,1,0:T(8,128)(2,1)S(1)} all-to-all(bf16[4,512,128]{2,1,0:T(8,128)(2,1)S(1)} %get-tuple-element.22), channel_id=1, replica_groups=mesh['x_high'=2,'far'=8,'near'=2,'x_low'=2,'y'=4,'core'=2] {'x_high','ne..., dimensions={0} | all-to-all | bytes 1048576 | tf_op jit(solution)/shard_map/all_to_all | solution.py:36
  148.1 1.5 shard_map.86
  149.6 17.4 %all_to_all.68.got = bf16[16,80,128]{2,1,0:T(8,128)(2,1)S(1)} all-to-all(bf16[16,80,128]{2,1,0:T(8,128)(2,1)S(1)} %shard_map.86), channel_id=1, replica_groups=mesh['x_high'=2,'far'=8,'near'=2,'x_low'=2,'y'=4,'core'=2] {'x_low','y',..., dimensions={0} | all-to-all | bytes 655360 | tf_op jit(solution)/shard_map/all_to_all | solution.py:36
  167.0 4.0 %shard_map.87 = (f32[64,128]{1,0:T(8,128)S(1)}, f32[64,128]{1,0:T(8,128)S(1)}, f32[32,32]{1,0:T(8,128)S(1)}, f32[32,32]{1,0:T(8,128)S(1)}, f32[32,16,128]{2,1,0:T(8,128)S(1)}) custom-call(bf16[16,80,128]{2,1,0:T(8,128)(2,1)S(1)} %all_to_all.68.got, f32[64,128]{1,0:T(8,128)S(1)} %get-tuple-element.24.column_sums, f32[64,128]{1,0:T(8,128)S(1)} %bitcast.9, ...), custom_call_target="tpu_custom_call" | custom-call | tf_op jit(solution)/shard_map/pallas_call | solution.py:42
  171.0 13.3 %all_to_all.69.got = f32[32,16,128]{2,1,0:T(8,128)S(1)} all-to-all(f32[32,16,128]{2,1,0:T(8,128)S(1)} %get-tuple-element.25), channel_id=1, replica_groups=mesh['x_high'=2,'far'=8,'near'=2,'x_low'=2,'y'=4,'core'=2] {'x_high','x_..., dimensions={0} | all-to-all | bytes 524288 | tf_op jit(solution)/shard_map/all_to_all | solution.py:36
  184.4 16.1 %all_to_all.70.got = f32[16,16,128]{2,1,0:T(8,128)S(1)} all-to-all(f32[16,16,128]{2,1,0:T(8,128)S(1)} %shard_map.88), channel_id=1, replica_groups=mesh['x_high'=2,'far'=8,'near'=2,'x_low'=2,'y'=4,'core'=2] {'far','near'}, dimensions={0} | all-to-all | bytes 262144 | tf_op jit(solution)/shard_map/all_to_all | solution.py:36
  200.5 1.9 shard_map.89
  (1 shorter events, 0.0 us)
Async XLA Ops:
  0.6 0.8 copy-start.1
  2.1 17.4 %all-to-all-start = ((bf16[16,64,128]{2,1,0:T(8,128)(2,1)}), bf16[16,64,128]{2,1,0:T(8,128)(2,1)S(1)}, u32[]{:S(2)}, u32[]{:S(2)}) async-start(bf16[16,64,128]{2,1,0:T(8,128)(2,1)} %shard_map.76), calls=%async_computation | async-start | bytes 524288 | tf_op jit(solution)/shard_map/all_to_all | solution.py:36
  12.3 1.4 copy-start
  13.7 0.7 copy-start.4
  13.7 0.7 copy-start.5
  14.5 17.3 %copy-start.2 = (f32[2,32,128]{2,1,0:T(8,128)S(1)}, f32[2,32,128]{2,1,0:T(8,128)}, u32[]{:S(2)}) copy-start(f32[2,32,128]{2,1,0:T(8,128)} %param.5) | copy-start | bytes 98308
  71.6 18.9 %copy-start.3 = (bf16[2,128,128]{2,1,0:T(8,128)(2,1)S(1)}, bf16[2,128,128]{2,1,0:T(8,128)(2,1)}, u32[]{:S(2)}) copy-start(bf16[2,128,128]{2,1,0:T(8,128)(2,1)} %diagonal.3) | copy-start | bytes 196612

commit v7 on v6

--- a/solution.py
+++ b/solution.py
@@ -109,11 +109,12 @@
     return jnp.dot(picker, pieces, preferred_element_type=f32)
 
 
-def factor_of(gram):
-    shape = (K, 128)
+def eliminate(gram):
+    count = gram.shape[0]
+    shape = (count, 128)
     row, column = iota(shape, 0), iota(shape, 1)
-    work = jnp.where(column < K, gram, jnp.where(column == row + K, 1.0, 0.0))
-    for base in range(0, K, PANEL):
+    work = jnp.where(column < count, gram, jnp.where(column == row + count, 1.0, 0.0))
+    for base in range(0, count, PANEL):
         columns = [
             jnp.broadcast_to(work[:, base + step : base + step + 1], shape) for step in range(PANEL)
         ]
@@ -132,9 +133,15 @@
         work = jnp.where(row >= base + PANEL, lower, work)
         for step in range(PANEL):
             work = jnp.where(row == base + step, leads[step], work)
-    upper = jnp.where((column < K) & (column >= row), work, 0.0)
-    inverse = pltpu.roll(work, 128 - K, 1)
-    return upper[:, :K], inverse[:, :K]
+    return work
+
+
+def lanes(matrix, place):
+    return (pltpu.roll(matrix, 128 - K * place, 1) if place else matrix)[:, :K]
+
+
+def upper_part(matrix):
+    return jnp.where(iota((K, K), 1) >= iota((K, K), 0), matrix, 0.0)
 
 
 def flip(matrix):
@@ -147,8 +154,10 @@
         message[device, : rows.shape[0], :] = rows
 
 
-def stage_kernel(tiles, staged):
-    staged[...] = tiles[...]
+def stage_kernel(tiles, staged, turned):
+    for tile in range(tiles.shape[0]):
+        staged[tile] = tiles[tile]
+        turned[tile] = tiles[tile].T
 
 
 def prepare_kernel(start, message):
@@ -212,7 +221,7 @@
             near = (owner >> 4) * 2 + (owner & 1)
             spot = ((owner >> 1) & 7) * 2 + (place & 1)
             vectors = got[near, pl.ds(pl.multiple_of(spot * K, K), K), :]
-            parts.append(dot_t(vectors, tiles[tile], None))
+            parts.append(jnp.dot(vectors, tiles[tile], preferred_element_type=f32))
         for tile in range(base, base + GROUP):
             where = pl.ds(pl.multiple_of(lists[tile] * K, K), K)
             total[where, :] += parts[tile - base]
@@ -245,8 +254,9 @@
         where = slice(block * K, (block + 1) * K)
         vectors = start[where, :]
         image[where, :] = images[block]
-        grams += dot_t(vectors, jnp.concatenate([vectors, empty, empty, empty]))
-        grams += dot_t(images[block], jnp.concatenate([empty, vectors, images[block], empty]))
+        pair = [vectors, images[block]]
+        grams += dot_t(vectors, jnp.concatenate(pair + [empty, empty]))
+        grams += dot_t(images[block], jnp.concatenate([empty, empty] + pair))
     fill(message, jnp.concatenate(images).astype(bf16))
     message[:, OWN:, :] = spread_slices(grams).reshape(COLUMNS, EXTRA, 128)
 
@@ -256,22 +266,17 @@
 ):
     images = image_of(got, column_sums, first, diagonal)
     sums = join_slices(got[:, OWN:, :].reshape(COLUMNS * EXTRA, 128))
-    inverse = factor_of(sums)[1]
-    alpha_t = dot_t(dot(inverse, pltpu.roll(sums, 128 - K, 1)[:, :K]), inverse)
-    image_gram = dot_t(dot(inverse, pltpu.roll(sums, 128 - 2 * K, 1)[:, :K]), inverse)
-    wide = jnp.zeros((128 - K, K), f32)
-    square = dot_t(alpha_t, jnp.concatenate([alpha_t, wide]))
-    upper, inverse_first = factor_of(
-        jnp.concatenate([image_gram, jnp.zeros((K, 128 - K), f32)], axis=1) - square
-    )
+    work = eliminate(jnp.concatenate([sums, pltpu.roll(sums, 128 - 2 * K, 1)]))
+    upper = upper_part(lanes(work[K:], 1))
+    inverse = lanes(work[:K], 2)
+    weights = pltpu.roll(work[K:], 128 - 2 * K, 1)[:, : 2 * K]
+    back = dot(dot_t(upper, inverse), inverse)
     packed = jnp.zeros((K // 2, 128), f32)
     for block in range(OWN // K):
         where = slice(block * K, (block + 1) * K)
-        basis_start = dot(inverse, start[where, :])
-        image_start = dot(inverse, first[where, :])
-        current = dot(inverse_first, image_start - dot(alpha_t, basis_start))
-        moved = dot(inverse, images[block]) - dot(alpha_t, image_start)
-        result = dot(inverse_first, moved) - dot(upper, basis_start)
+        current = dot(weights, jnp.concatenate([start[where, :], first[where, :]]))
+        result = dot(weights, jnp.concatenate([first[where, :], images[block]]))
+        result -= dot(back, start[where, :])
         basis[where, :] = current
         image[where, :] = result
         for half in range(2):
@@ -281,8 +286,8 @@
             packed += dot_t(top, jnp.concatenate(pair))
     for device in range(message.shape[0]):
         message[device, :, :] = packed
-    alpha[...] = flip(alpha_t)
-    beta[...] = flip(upper)
+    alpha[...] = dot_t(lanes(work[:K], 1), inverse)
+    beta[...] = dot_t(inverse, upper)
 
 
 def plane_kernel(got, message):
@@ -302,7 +307,8 @@
     image_gram = jnp.concatenate(turned[2:])
     wide = jnp.zeros((128 - K, K), f32)
     square = dot_t(alpha_t, jnp.concatenate([alpha_t, wide]))
-    upper, inverse = factor_of(image_gram - square)
+    work = eliminate(image_gram - square)
+    upper, inverse = upper_part(work[:, :K]), lanes(work, 1)
     for block in range(OWN // K):
         where = slice(block * K, (block + 1) * K)
         residual = image[where, :] - dot(alpha_t, basis[where, :])
@@ -313,7 +319,7 @@
     betas[1] = flip(upper)
 
 
-def exchange(message, vectors, tiles, lists):
+def exchange(message, vectors, tiles, turned, lists):
     extra = message.shape[1] - OWN
     got = swap(message, COLUMN)
     sent = call(
@@ -335,7 +341,7 @@
         upper_kernel,
         out((COLUMNS, OWN + extra, 128), bf16),
         (lists,),
-        (got, tiles, *piece),
+        (got, turned, *piece),
         (pltpu.VMEM((COLUMNS * OWN, 128), f32),),
     )
     return swap(sent, COLUMN), column_sums
@@ -345,7 +351,7 @@
     start = start_block.reshape(OWN, 128)
     tiles = tile_values[0, 0]
     matrix = (
-        call(stage_kernel, out(tiles.shape, bf16), (), (tiles,)),
+        *call(stage_kernel, (out(tiles.shape, bf16), out(tiles.shape, bf16)), (), (tiles,)),
         jnp.concatenate([tile_rows[0, 0], tile_columns[0, 0]]),
     )
     vectors = out((OWN, 128), f32)

time: 204 us -> 202 us (level)
  no operation moved by 1% of the time
where the time goes in v7:
time: 202 us; the launch traced here: 201 us
  blocking collectives  170 us (84%)
  Pallas kernels  12.2 us (6%)
  starting transfers between devices  10.2 us (5%)
  waiting for transfers between devices  5.21 us (3%)
  local copies, waits for them, and re-layouts  2.18 us (1%)
    all_to_all x11, blocking collectives, swap(): return lax.all_to_all(parts, axis, 0, 0, tiled=True)  170 us
    pallas_call x14, Pallas kernels, call(): pl.pallas_call(kernel, out_shape=outs, in_specs=specs, out_specs=jax.tree...  12.2 us
    all_to_all x1, starting transfers between devices, swap(): return lax.all_to_all(parts, axis, 0, 0, tiled=True)  10.2 us
    all_to_all x1, waiting for transfers between devices, swap(): return lax.all_to_all(parts, axis, 0, 0, tiled=True)  5.21 us
  transfers between devices with their start and end apart: 1, of which 1 were waited for; matrix products, arithmetic and copies ran while one was open for 0% of the time, Pallas kernels for 0%

profile of v7, /device:TPU:1, one launch (start us, length us, event | category | flops | bytes accessed | tf_op | source)
XLA Modules:
  0.0 201.0 jit_solution(5824701227507265379)
XLA Ops:
  0.6 0.0 copy-start.4
  0.6 0.0 copy-start.5
  0.7 0.0 copy-start.1
  0.7 0.8 copy-done.1
  1.4 0.7 shard_map.76
  2.1 10.2 %all-to-all-start = ((bf16[16,64,128]{2,1,0:T(8,128)(2,1)}), bf16[16,64,128]{2,1,0:T(8,128)(2,1)S(1)}, u32[]{:S(2)}, u32[]{:S(2)}) async-start(bf16[16,64,128]{2,1,0:T(8,128)(2,1)} %shard_map.76), calls=%async_computation | async-start | bytes 524288 | tf_op jit(solution)/shard_map/all_to_all | solution.py:36
  12.3 0.0 copy-start
  12.4 1.4 copy-done
  13.8 0.5 shard_map.77
  14.3 0.0 copy-done.4
  14.3 0.0 copy-done.5
  14.3 0.1 pad_add_fusion.lists
  14.4 5.2 %all-to-all-done.got = bf16[16,64,128]{2,1,0:T(8,128)(2,1)S(1)} async-done(((bf16[16,64,128]{2,1,0:T(8,128)(2,1)}), bf16[16,64,128]{2,1,0:T(8,128)(2,1)S(1)}, u32[]{:S(2)}, u32[]{:S(2)}) %all-to-all-start) | async-done | bytes 262176 | tf_op jit(solution)/shard_map/all_to_all | solution.py:36
  19.6 0.0 copy-start.2
  19.6 1.1 shard_map.78
  20.7 11.1 %all_to_all.60.got = bf16[4,512,128]{2,1,0:T(8,128)(2,1)S(1)} all-to-all(bf16[4,512,128]{2,1,0:T(8,128)(2,1)S(1)} %shard_map.78), channel_id=1, replica_groups=mesh['x_high'=2,'far'=8,'near'=2,'x_low'=2,'y'=4,'core'=2] {'x_high','ne..., dimensions={0} | all-to-all | bytes 1048576 | tf_op jit(solution)/shard_map/all_to_all | solution.py:36
  31.8 0.0 copy-done.2
  31.8 0.1 shard_map.79
  31.9 28.9 %all_to_all.61.got = bf16[8,128,128]{2,1,0:T(8,128)(2,1)S(1)} all-to-all(bf16[8,128,128]{2,1,0:T(8,128)(2,1)S(1)} %shard_map.79), channel_id=1, replica_groups=mesh['x_high'=2,'far'=8,'near'=2,'x_low'=2,'y'=4,'core'=2] {'far'}, dimensions={0} | all-to-all | bytes 524288 | tf_op jit(solution)/shard_map/all_to_all | solution.py:36
  60.9 0.1 shard_map.80
  60.9 10.7 %all_to_all.62.got = bf16[4,512,128]{2,1,0:T(8,128)(2,1)S(1)} all-to-all(bf16[4,512,128]{2,1,0:T(8,128)(2,1)S(1)} %get-tuple-element.21), channel_id=1, replica_groups=mesh['x_high'=2,'far'=8,'near'=2,'x_low'=2,'y'=4,'core'=2] {'x_high','ne..., dimensions={0} | all-to-all | bytes 1048576 | tf_op jit(solution)/shard_map/all_to_all | solution.py:36
  71.6 0.0 copy-start.3
  71.6 1.1 shard_map.81
  72.8 17.4 %all_to_all.63.got = bf16[16,64,128]{2,1,0:T(8,128)(2,1)S(1)} all-to-all(bf16[16,64,128]{2,1,0:T(8,128)(2,1)S(1)} %shard_map.81), channel_id=1, replica_groups=mesh['x_high'=2,'far'=8,'near'=2,'x_low'=2,'y'=4,'core'=2] {'x_low','y',..., dimensions={0} | all-to-all | bytes 524288 | tf_op jit(solution)/shard_map/all_to_all | solution.py:36
  90.1 0.0 copy-done.3
  90.1 0.8 shard_map.82
  90.9 11.2 %all_to_all.64.got = bf16[16,80,128]{2,1,0:T(8,128)(2,1)S(1)} all-to-all(bf16[16,80,128]{2,1,0:T(8,128)(2,1)S(1)} %get-tuple-element.24), channel_id=1, replica_groups=mesh['x_high'=2,'far'=8,'near'=2,'x_low'=2,'y'=4,'core'=2] {'x_low','y',..., dimensions={0} | all-to-all | bytes 655360 | tf_op jit(solution)/shard_map/all_to_all | solution.py:36
  102.1 1.1 shard_map.83
  103.3 11.5 %all_to_all.65.got = bf16[4,528,128]{2,1,0:T(8,128)(2,1)S(1)} all-to-all(bf16[4,528,128]{2,1,0:T(8,128)(2,1)S(1)} %shard_map.83), channel_id=1, replica_groups=mesh['x_high'=2,'far'=8,'near'=2,'x_low'=2,'y'=4,'core'=2] {'x_high','ne..., dimensions={0} | all-to-all | bytes 1081344 | tf_op jit(solution)/shard_map/all_to_all | solution.py:36
  114.7 0.1 shard_map.84
  114.9 22.8 %all_to_all.66.got = bf16[8,144,128]{2,1,0:T(8,128)(2,1)S(1)} all-to-all(bf16[8,144,128]{2,1,0:T(8,128)(2,1)S(1)} %shard_map.84), channel_id=1, replica_groups=mesh['x_high'=2,'far'=8,'near'=2,'x_low'=2,'y'=4,'core'=2] {'far'}, dimensions={0} | all-to-all | bytes 589824 | tf_op jit(solution)/shard_map/all_to_all | solution.py:36
  137.7 0.2 shard_map.85
  137.9 9.9 %all_to_all.67.got = bf16[4,512,128]{2,1,0:T(8,128)(2,1)S(1)} all-to-all(bf16[4,512,128]{2,1,0:T(8,128)(2,1)S(1)} %get-tuple-element.26), channel_id=1, replica_groups=mesh['x_high'=2,'far'=8,'near'=2,'x_low'=2,'y'=4,'core'=2] {'x_high','ne..., dimensions={0} | all-to-all | bytes 1048576 | tf_op jit(solution)/shard_map/all_to_all | solution.py:36
  147.8 1.1 shard_map.86
  148.9 17.5 %all_to_all.68.got = bf16[16,80,128]{2,1,0:T(8,128)(2,1)S(1)} all-to-all(bf16[16,80,128]{2,1,0:T(8,128)(2,1)S(1)} %shard_map.86), channel_id=1, replica_groups=mesh['x_high'=2,'far'=8,'near'=2,'x_low'=2,'y'=4,'core'=2] {'x_low','y',..., dimensions={0} | all-to-all | bytes 655360 | tf_op jit(solution)/shard_map/all_to_all | solution.py:36
  166.3 3.3 %shard_map.87 = (f32[64,128]{1,0:T(8,128)S(1)}, f32[64,128]{1,0:T(8,128)S(1)}, f32[32,32]{1,0:T(8,128)S(1)}, f32[32,32]{1,0:T(8,128)S(1)}, f32[32,16,128]{2,1,0:T(8,128)S(1)}) custom-call(bf16[16,80,128]{2,1,0:T(8,128)(2,1)S(1)} %all_to_all.68.got, f32[64,128]{1,0:T(8,128)S(1)} %get-tuple-element.28.column_sums, f32[64,128]{1,0:T(8,128)S(1)} %bitcast.9, ...), custom_call_target="tpu_custom_call" | custom-call | tf_op jit(solution)/shard_map/pallas_call | solution.py:42
  169.6 13.3 %all_to_all.69.got = f32[32,16,128]{2,1,0:T(8,128)S(1)} all-to-all(f32[32,16,128]{2,1,0:T(8,128)S(1)} %get-tuple-element.29), channel_id=1, replica_groups=mesh['x_high'=2,'far'=8,'near'=2,'x_low'=2,'y'=4,'core'=2] {'x_high','x_..., dimensions={0} | all-to-all | bytes 524288 | tf_op jit(solution)/shard_map/all_to_all | solution.py:36
  183.0 16.2 %all_to_all.70.got = f32[16,16,128]{2,1,0:T(8,128)S(1)} all-to-all(f32[16,16,128]{2,1,0:T(8,128)S(1)} %shard_map.88), channel_id=1, replica_groups=mesh['x_high'=2,'far'=8,'near'=2,'x_low'=2,'y'=4,'core'=2] {'far','near'}, dimensions={0} | all-to-all | bytes 262144 | tf_op jit(solution)/shard_map/all_to_all | solution.py:36
  199.1 1.9 shard_map.89
  (1 shorter events, 0.0 us)
Async XLA Ops:
  0.6 13.6 %copy-start.4 = (s32[1,1,48]{2,1,0:T(1,128)S(1)}, s32[1,1,48]{2,1,0:T(1,128)}, u32[]{:S(2)}) copy-start(s32[1,1,48]{2,1,0:T(1,128)} %param.8) | copy-start | bytes 580
  0.6 13.6 %copy-start.5 = (s32[1,1,48]{2,1,0:T(1,128)S(1)}, s32[1,1,48]{2,1,0:T(1,128)}, u32[]{:S(2)}) copy-start(s32[1,1,48]{2,1,0:T(1,128)} %param.7) | copy-start | bytes 580
  0.7 0.8 copy-start.1
  2.1 17.4 %all-to-all-start = ((bf16[16,64,128]{2,1,0:T(8,128)(2,1)}), bf16[16,64,128]{2,1,0:T(8,128)(2,1)S(1)}, u32[]{:S(2)}, u32[]{:S(2)}) async-start(bf16[16,64,128]{2,1,0:T(8,128)(2,1)} %shard_map.76), calls=%async_computation | async-start | bytes 524288 | tf_op jit(solution)/shard_map/all_to_all | solution.py:36
  12.3 1.4 copy-start
  19.6 12.3 %copy-start.2 = (f32[2,32,128]{2,1,0:T(8,128)S(1)}, f32[2,32,128]{2,1,0:T(8,128)}, u32[]{:S(2)}) copy-start(f32[2,32,128]{2,1,0:T(8,128)} %param.5) | copy-start | bytes 98308
  71.6 18.5 %copy-start.3 = (bf16[2,128,128]{2,1,0:T(8,128)(2,1)S(1)}, bf16[2,128,128]{2,1,0:T(8,128)(2,1)}, u32[]{:S(2)}) copy-start(bf16[2,128,128]{2,1,0:T(8,128)(2,1)} %diagonal.3) | copy-start | bytes 196612

commit v8 on v7

--- a/solution.py
+++ b/solution.py
@@ -26,6 +26,7 @@
 TERMS = 3
 GROUP = 8
 PANEL = 8
+PACKED = K * K + 128
 
 highest = lax.Precision.HIGHEST
 f32 = jnp.float32
@@ -160,8 +161,27 @@
         turned[tile] = tiles[tile].T
 
 
-def prepare_kernel(start, message):
-    fill(message, start[...].astype(bf16))
+def pack(square, cross):
+    row, column = iota((K, 128), 0), iota((K, 128), 1)
+    both = jnp.where(column < K, jnp.where(row >= column, square, cross), 0.0)
+    quarter = K // 4
+    folded = both[:quarter]
+    for place in range(1, 4):
+        folded += pltpu.roll(both[place * quarter : (place + 1) * quarter], K * place, 1)
+    middle = jnp.sum(jnp.where(row == column, cross, 0.0), axis=0, keepdims=True)
+    return jnp.concatenate([folded[line : line + 1] for line in range(quarter)] + [middle], axis=1)
+
+
+def unpack(packed):
+    quarter = K // 4
+    folded = jnp.concatenate([packed[:, 128 * line : 128 * (line + 1)] for line in range(quarter)])
+    both = jnp.concatenate([lanes(folded, place) for place in range(4)])
+    other = flip(both)
+    row, column = iota((K, K), 0), iota((K, K), 1)
+    square = jnp.where(row >= column, both, other)
+    middle = packed[:, 128 * quarter : 128 * quarter + K]
+    cross = jnp.where(row < column, both, jnp.where(row == column, middle, other))
+    return square, cross
 
 
 def lower_kernel(lists, got, tiles, message, total):
@@ -271,7 +291,9 @@
     inverse = lanes(work[:K], 2)
     weights = pltpu.roll(work[K:], 128 - 2 * K, 1)[:, : 2 * K]
     back = dot(dot_t(upper, inverse), inverse)
-    packed = jnp.zeros((K // 2, 128), f32)
+    square = jnp.zeros((K, 128), f32)
+    cross = jnp.zeros((K, 128), f32)
+    empty = [jnp.zeros((K, 128), f32)] * 3
     for block in range(OWN // K):
         where = slice(block * K, (block + 1) * K)
         current = dot(weights, jnp.concatenate([start[where, :], first[where, :]]))
@@ -279,13 +301,12 @@
         result -= dot(back, start[where, :])
         basis[where, :] = current
         image[where, :] = result
-        for half in range(2):
-            top = result[half * (K // 2) : (half + 1) * (K // 2), :]
-            empty = jnp.zeros_like(result)
-            pair = [current, empty, result, empty] if half == 0 else [empty, current, empty, result]
-            packed += dot_t(top, jnp.concatenate(pair))
+        wide = jnp.concatenate([result] + empty)
+        square += dot_t(result, wide)
+        cross += dot_t(current, wide)
+    packed = pack(square, cross)
     for device in range(message.shape[0]):
-        message[device, :, :] = packed
+        message[device] = packed
     alpha[...] = dot_t(lanes(work[:K], 1), inverse)
     beta[...] = dot_t(inverse, upper)
 
@@ -302,19 +323,16 @@
     total = got[0]
     for device in range(1, got.shape[0]):
         total += got[device]
-    turned = [total] + [pltpu.roll(total, 128 - K * place, 1) for place in range(1, 4)]
-    alpha_t = jnp.concatenate(turned[:2])[:, :K]
-    image_gram = jnp.concatenate(turned[2:])
-    wide = jnp.zeros((128 - K, K), f32)
-    square = dot_t(alpha_t, jnp.concatenate([alpha_t, wide]))
-    work = eliminate(image_gram - square)
+    image_gram, alpha_last = unpack(total)
+    wide = jnp.zeros((K, 128 - K), f32)
+    work = eliminate(jnp.concatenate([image_gram - dot(alpha_last, alpha_last), wide], axis=1))
     upper, inverse = upper_part(work[:, :K]), lanes(work, 1)
     for block in range(OWN // K):
         where = slice(block * K, (block + 1) * K)
-        residual = image[where, :] - dot(alpha_t, basis[where, :])
+        residual = image[where, :] - dot(alpha_last, basis[where, :])
         result[where, :] = dot(inverse, residual) * scaling
     alphas[0] = alpha_first[...]
-    alphas[1] = flip(alpha_t)
+    alphas[1] = alpha_last
     betas[0] = beta_first[...]
     betas[1] = flip(upper)
 
@@ -356,7 +374,7 @@
     )
     vectors = out((OWN, 128), f32)
     square = out((K, K), f32)
-    message = call(prepare_kernel, out((COLUMNS, OWN, 128), bf16), (), (start,))
+    message = jnp.broadcast_to(start.astype(bf16), (COLUMNS, OWN, 128))
     got, column_sums = exchange(message, start, *matrix)
     first, message = call(
         middle_kernel,
@@ -368,12 +386,12 @@
     planes, depths = lax.axis_size(PLANE), lax.axis_size(DEPTH)
     basis, image, alpha_first, beta_first, message = call(
         finish_kernel,
-        (vectors, vectors, square, square, out((planes, K // 2, 128), f32)),
+        (vectors, vectors, square, square, out((planes, 1, PACKED), f32)),
         (),
         (got, column_sums, start, first, diagonal_blocks),
     )
     got = swap(message, PLANE)
-    message = call(plane_kernel, out((depths, K // 2, 128), f32), (), (got,))
+    message = call(plane_kernel, out((depths, 1, PACKED), f32), (), (got,))
     got = swap(message, DEPTH)
     scaling = math.sqrt(start_block.shape[0] * start_block.shape[2] * planes * depths)
     pair = out((2, K, K), f32)

time: 202 us -> 200 us (0.990)
    pallas_call x14 -> x13, Pallas kernels: 12.2 us -> 11.1 us  [call(): pl.pallas_call(kernel, out_shape=outs, in_specs=specs, out_specs=jax.tree...]
where the time goes in v8:
time: 200 us; the launch traced here: 199 us
  blocking collectives  169 us (84%)
  Pallas kernels  11.1 us (6%)
  starting transfers between devices  10.2 us (5%)
  waiting for transfers between devices  5.21 us (3%)
  local copies, waits for them, and re-layouts  2.18 us (1%)
    all_to_all x11, blocking collectives, swap(): return lax.all_to_all(parts, axis, 0, 0, tiled=True)  169 us
    pallas_call x13, Pallas kernels, call(): pl.pallas_call(kernel, out_shape=outs, in_specs=specs, out_specs=jax.tree...  11.1 us
    all_to_all x1, starting transfers between devices, swap(): return lax.all_to_all(parts, axis, 0, 0, tiled=True)  10.2 us
    all_to_all x1, waiting for transfers between devices, swap(): return lax.all_to_all(parts, axis, 0, 0, tiled=True)  5.21 us
  transfers between devices with their start and end apart: 1, of which 1 were waited for; matrix products, arithmetic and copies ran while one was open for 0% of the time, Pallas kernels for 0%

profile of v8, /device:TPU:1, one launch (start us, length us, event | category | flops | bytes accessed | tf_op | source)
XLA Modules:
  0.0 199.0 jit_solution(9057194312344618684)
XLA Ops:
  0.6 0.0 copy-start.3
  0.6 0.0 copy-start.4
  0.7 0.8 bitcast_convert_fusion
  1.4 0.8 broadcast_in_dim.3
  2.2 10.2 %all-to-all-start = ((bf16[16,64,128]{2,1,0:T(8,128)(2,1)}), bf16[16,64,128]{2,1,0:T(8,128)(2,1)S(1)}, u32[]{:S(2)}, u32[]{:S(2)}) async-start(bf16[16,64,128]{2,1,0:T(8,128)(2,1)} %broadcast_in_dim.3), calls=%async_computation | async-start | bytes 524288 | tf_op jit(solution)/shard_map/all_to_all | solution.py:37
  12.4 0.0 copy-start
  12.4 1.4 copy-done
  13.8 0.5 shard_map.76
  14.3 0.0 copy-done.3
  14.3 0.0 copy-done.4
  14.3 0.1 pad_add_fusion.lists
  14.4 5.2 %all-to-all-done.got = bf16[16,64,128]{2,1,0:T(8,128)(2,1)S(1)} async-done(((bf16[16,64,128]{2,1,0:T(8,128)(2,1)}), bf16[16,64,128]{2,1,0:T(8,128)(2,1)S(1)}, u32[]{:S(2)}, u32[]{:S(2)}) %all-to-all-start) | async-done | bytes 262176 | tf_op jit(solution)/shard_map/all_to_all | solution.py:37
  19.6 0.0 copy-start.1
  19.6 1.1 shard_map.77
  20.7 11.1 %all_to_all.60.got = bf16[4,512,128]{2,1,0:T(8,128)(2,1)S(1)} all-to-all(bf16[4,512,128]{2,1,0:T(8,128)(2,1)S(1)} %shard_map.77), channel_id=1, replica_groups=mesh['x_high'=2,'far'=8,'near'=2,'x_low'=2,'y'=4,'core'=2] {'x_high','ne..., dimensions={0} | all-to-all | bytes 1048576 | tf_op jit(solution)/shard_map/all_to_all | solution.py:37
  31.9 0.0 copy-done.1
  31.9 0.1 shard_map.78
  31.9 28.9 %all_to_all.61.got = bf16[8,128,128]{2,1,0:T(8,128)(2,1)S(1)} all-to-all(bf16[8,128,128]{2,1,0:T(8,128)(2,1)S(1)} %shard_map.78), channel_id=1, replica_groups=mesh['x_high'=2,'far'=8,'near'=2,'x_low'=2,'y'=4,'core'=2] {'far'}, dimensions={0} | all-to-all | bytes 524288 | tf_op jit(solution)/shard_map/all_to_all | solution.py:37
  60.9 0.1 shard_map.79
  61.0 10.7 %all_to_all.62.got = bf16[4,512,128]{2,1,0:T(8,128)(2,1)S(1)} all-to-all(bf16[4,512,128]{2,1,0:T(8,128)(2,1)S(1)} %get-tuple-element.21), channel_id=1, replica_groups=mesh['x_high'=2,'far'=8,'near'=2,'x_low'=2,'y'=4,'core'=2] {'x_high','ne..., dimensions={0} | all-to-all | bytes 1048576 | tf_op jit(solution)/shard_map/all_to_all | solution.py:37
  71.7 0.0 copy-start.2
  71.7 1.1 shard_map.80
  72.8 17.4 %all_to_all.63.got = bf16[16,64,128]{2,1,0:T(8,128)(2,1)S(1)} all-to-all(bf16[16,64,128]{2,1,0:T(8,128)(2,1)S(1)} %shard_map.80), channel_id=1, replica_groups=mesh['x_high'=2,'far'=8,'near'=2,'x_low'=2,'y'=4,'core'=2] {'x_low','y',..., dimensions={0} | all-to-all | bytes 524288 | tf_op jit(solution)/shard_map/all_to_all | solution.py:37
  90.2 0.0 copy-done.2
  90.2 0.8 shard_map.81
  91.0 11.2 %all_to_all.64.got = bf16[16,80,128]{2,1,0:T(8,128)(2,1)S(1)} all-to-all(bf16[16,80,128]{2,1,0:T(8,128)(2,1)S(1)} %get-tuple-element.24), channel_id=1, replica_groups=mesh['x_high'=2,'far'=8,'near'=2,'x_low'=2,'y'=4,'core'=2] {'x_low','y',..., dimensions={0} | all-to-all | bytes 655360 | tf_op jit(solution)/shard_map/all_to_all | solution.py:37
  102.2 1.1 shard_map.82
  103.3 11.5 %all_to_all.65.got = bf16[4,528,128]{2,1,0:T(8,128)(2,1)S(1)} all-to-all(bf16[4,528,128]{2,1,0:T(8,128)(2,1)S(1)} %shard_map.82), channel_id=1, replica_groups=mesh['x_high'=2,'far'=8,'near'=2,'x_low'=2,'y'=4,'core'=2] {'x_high','ne..., dimensions={0} | all-to-all | bytes 1081344 | tf_op jit(solution)/shard_map/all_to_all | solution.py:37
  114.8 0.1 shard_map.83
  114.9 22.8 %all_to_all.66.got = bf16[8,144,128]{2,1,0:T(8,128)(2,1)S(1)} all-to-all(bf16[8,144,128]{2,1,0:T(8,128)(2,1)S(1)} %shard_map.83), channel_id=1, replica_groups=mesh['x_high'=2,'far'=8,'near'=2,'x_low'=2,'y'=4,'core'=2] {'far'}, dimensions={0} | all-to-all | bytes 589824 | tf_op jit(solution)/shard_map/all_to_all | solution.py:37
  137.7 0.2 shard_map.84
  137.9 9.9 %all_to_all.67.got = bf16[4,512,128]{2,1,0:T(8,128)(2,1)S(1)} all-to-all(bf16[4,512,128]{2,1,0:T(8,128)(2,1)S(1)} %get-tuple-element.26), channel_id=1, replica_groups=mesh['x_high'=2,'far'=8,'near'=2,'x_low'=2,'y'=4,'core'=2] {'x_high','ne..., dimensions={0} | all-to-all | bytes 1048576 | tf_op jit(solution)/shard_map/all_to_all | solution.py:37
  147.8 1.1 shard_map.85
  148.9 17.5 %all_to_all.68.got = bf16[16,80,128]{2,1,0:T(8,128)(2,1)S(1)} all-to-all(bf16[16,80,128]{2,1,0:T(8,128)(2,1)S(1)} %shard_map.85), channel_id=1, replica_groups=mesh['x_high'=2,'far'=8,'near'=2,'x_low'=2,'y'=4,'core'=2] {'x_low','y',..., dimensions={0} | all-to-all | bytes 655360 | tf_op jit(solution)/shard_map/all_to_all | solution.py:37
  166.4 2.7 %shard_map.86 = (f32[64,128]{1,0:T(8,128)S(1)}, f32[64,128]{1,0:T(8,128)S(1)}, f32[32,32]{1,0:T(8,128)S(1)}, f32[32,32]{1,0:T(8,128)S(1)}, f32[32,1,1152]{2,1,0:T(1,128)S(1)}) custom-call(bf16[16,80,128]{2,1,0:T(8,128)(2,1)S(1)} %all_to_all.68.got, f32[64,128]{1,0:T(8,128)S(1)} %get-tuple-element.28.column_sums, f32[64,128]{1,0:T(8,128)S(1)} %bitcast.9, ...), custom_call_target="tpu_custom_call" | custom-call | tf_op jit(solution)/shard_map/pallas_call | solution.py:43
  169.1 12.2 %all_to_all.69.got = f32[32,1,1152]{2,1,0:T(1,128)S(1)} all-to-all(f32[32,1,1152]{2,1,0:T(1,128)S(1)} %get-tuple-element.29), channel_id=1, replica_groups=mesh['x_high'=2,'far'=8,'near'=2,'x_low'=2,'y'=4,'core'=2] {'x_high','x_..., dimensions={0} | all-to-all | bytes 294912 | tf_op jit(solution)/shard_map/all_to_all | solution.py:37
  181.3 15.7 %all_to_all.70.got = f32[16,1,1152]{2,1,0:T(1,128)S(1)} all-to-all(f32[16,1,1152]{2,1,0:T(1,128)S(1)} %shard_map.87), channel_id=1, replica_groups=mesh['x_high'=2,'far'=8,'near'=2,'x_low'=2,'y'=4,'core'=2] {'far','near'}, dimensions={0} | all-to-all | bytes 147456 | tf_op jit(solution)/shard_map/all_to_all | solution.py:37
  197.0 2.0 %shard_map.88 = (f32[64,128]{1,0:T(8,128)}, f32[2,32,32]{2,1,0:T(8,128)}, f32[2,32,32]{2,1,0:T(8,128)}) custom-call(f32[16,1,1152]{2,1,0:T(1,128)S(1)} %all_to_all.70.got, f32[64,128]{1,0:T(8,128)S(1)} %get-tuple-element.30.basis, f32[64,128]{1,0:T(8,128)S(1)} %get-tuple-element.31.image, f32[32,32]{1,0:T(8,128)S(1)} %get-tuple-element.32.alpha_first, ...), custom_call_target="tpu_custom_call" | custom-call | tf_op jit(solution)/shard_map/pallas_call | solution.py:43
  (1 shorter events, 0.0 us)
Async XLA Ops:
  0.6 13.7 %copy-start.3 = (s32[1,1,48]{2,1,0:T(1,128)S(1)}, s32[1,1,48]{2,1,0:T(1,128)}, u32[]{:S(2)}) copy-start(s32[1,1,48]{2,1,0:T(1,128)} %param.8) | copy-start | bytes 580
  0.6 13.7 %copy-start.4 = (s32[1,1,48]{2,1,0:T(1,128)S(1)}, s32[1,1,48]{2,1,0:T(1,128)}, u32[]{:S(2)}) copy-start(s32[1,1,48]{2,1,0:T(1,128)} %param.7) | copy-start | bytes 580
  2.2 17.4 %all-to-all-start = ((bf16[16,64,128]{2,1,0:T(8,128)(2,1)}), bf16[16,64,128]{2,1,0:T(8,128)(2,1)S(1)}, u32[]{:S(2)}, u32[]{:S(2)}) async-start(bf16[16,64,128]{2,1,0:T(8,128)(2,1)} %broadcast_in_dim.3), calls=%async_computation | async-start | bytes 524288 | tf_op jit(solution)/shard_map/all_to_all | solution.py:37
  12.4 1.4 copy-start
  19.6 12.3 %copy-start.1 = (f32[2,32,128]{2,1,0:T(8,128)S(1)}, f32[2,32,128]{2,1,0:T(8,128)}, u32[]{:S(2)}) copy-start(f32[2,32,128]{2,1,0:T(8,128)} %param.5) | copy-start | bytes 98308
  71.7 18.5 %copy-start.2 = (bf16[2,128,128]{2,1,0:T(8,128)(2,1)S(1)}, bf16[2,128,128]{2,1,0:T(8,128)(2,1)}, u32[]{:S(2)}) copy-start(bf16[2,128,128]{2,1,0:T(8,128)(2,1)} %diagonal.3) | copy-start | bytes 196612

commit v9 on v8

--- a/solution.py
+++ b/solution.py
@@ -25,7 +25,7 @@
 EXTRA = 16
 TERMS = 3
 GROUP = 8
-PANEL = 8
+PANEL = 16
 PACKED = K * K + 128
 
 highest = lax.Precision.HIGHEST
@@ -159,6 +159,10 @@
     for tile in range(tiles.shape[0]):
         staged[tile] = tiles[tile]
         turned[tile] = tiles[tile].T
+
+
+def prepare_kernel(start, message):
+    fill(message, start[...].astype(bf16))
 
 
 def pack(square, cross):
@@ -374,7 +378,7 @@
     )
     vectors = out((OWN, 128), f32)
     square = out((K, K), f32)
-    message = jnp.broadcast_to(start.astype(bf16), (COLUMNS, OWN, 128))
+    message = call(prepare_kernel, out((COLUMNS, OWN, 128), bf16), (), (start,))
     got, column_sums = exchange(message, start, *matrix)
     first, message = call(
         middle_kernel,

time: 200 us -> 199 us (level)
    pallas_call x13 -> x14, Pallas kernels: 11.1 us -> 11.4 us  [call(): pl.pallas_call(kernel, out_shape=outs, in_specs=specs, out_specs=jax.tree...]
where the time goes in v9:
time: 199 us
  blocking collectives  169 us (85%)
  Pallas kernels  11.4 us (6%)
  starting transfers between devices  10.2 us (5%)
  waiting for transfers between devices  5.21 us (3%)
  local copies, waits for them, and re-layouts  2.18 us (1%)
    all_to_all x11, blocking collectives, swap(): return lax.all_to_all(parts, axis, 0, 0, tiled=True)  169 us
    pallas_call x14, Pallas kernels, call(): pl.pallas_call(kernel, out_shape=outs, in_specs=specs, out_specs=jax.tree...  11.4 us
    all_to_all x1, starting transfers between devices, swap(): return lax.all_to_all(parts, axis, 0, 0, tiled=True)  10.2 us
    all_to_all x1, waiting for transfers between devices, swap(): return lax.all_to_all(parts, axis, 0, 0, tiled=True)  5.21 us
  transfers between devices with their start and end apart: 1, of which 1 were waited for; matrix products, arithmetic and copies ran while one was open for 0% of the time, Pallas kernels for 0%

profile of v9, /device:TPU:1, one launch (start us, length us, event | category | flops | bytes accessed | tf_op | source)
XLA Modules:
  0.0 198.6 jit_solution(6208970263396639861)
XLA Ops:
  0.6 0.0 copy-start.4
  0.6 0.0 copy-start.5
  0.7 0.0 copy-start.1
  0.7 0.8 copy-done.1
  1.4 0.7 shard_map.76
  2.1 10.2 %all-to-all-start = ((bf16[16,64,128]{2,1,0:T(8,128)(2,1)}), bf16[16,64,128]{2,1,0:T(8,128)(2,1)S(1)}, u32[]{:S(2)}, u32[]{:S(2)}) async-start(bf16[16,64,128]{2,1,0:T(8,128)(2,1)} %shard_map.76), calls=%async_computation | async-start | bytes 524288 | tf_op jit(solution)/shard_map/all_to_all | solution.py:37
  12.3 0.0 copy-start
  12.4 1.4 copy-done
  13.8 0.5 shard_map.77
  14.3 0.0 copy-done.4
  14.3 0.0 copy-done.5
  14.3 0.1 pad_add_fusion.lists
  14.4 5.2 %all-to-all-done.got = bf16[16,64,128]{2,1,0:T(8,128)(2,1)S(1)} async-done(((bf16[16,64,128]{2,1,0:T(8,128)(2,1)}), bf16[16,64,128]{2,1,0:T(8,128)(2,1)S(1)}, u32[]{:S(2)}, u32[]{:S(2)}) %all-to-all-start) | async-done | bytes 262176 | tf_op jit(solution)/shard_map/all_to_all | solution.py:37
  19.6 0.0 copy-start.2
  19.6 1.1 shard_map.78
  20.7 11.1 %all_to_all.60.got = bf16[4,512,128]{2,1,0:T(8,128)(2,1)S(1)} all-to-all(bf16[4,512,128]{2,1,0:T(8,128)(2,1)S(1)} %shard_map.78), channel_id=1, replica_groups=mesh['x_high'=2,'far'=8,'near'=2,'x_low'=2,'y'=4,'core'=2] {'x_high','ne..., dimensions={0} | all-to-all | bytes 1048576 | tf_op jit(solution)/shard_map/all_to_all | solution.py:37
  31.8 0.0 copy-done.2
  31.8 0.1 shard_map.79
  31.9 28.9 %all_to_all.61.got = bf16[8,128,128]{2,1,0:T(8,128)(2,1)S(1)} all-to-all(bf16[8,128,128]{2,1,0:T(8,128)(2,1)S(1)} %shard_map.79), channel_id=1, replica_groups=mesh['x_high'=2,'far'=8,'near'=2,'x_low'=2,'y'=4,'core'=2] {'far'}, dimensions={0} | all-to-all | bytes 524288 | tf_op jit(solution)/shard_map/all_to_all | solution.py:37
  60.8 0.1 shard_map.80
  60.9 10.7 %all_to_all.62.got = bf16[4,512,128]{2,1,0:T(8,128)(2,1)S(1)} all-to-all(bf16[4,512,128]{2,1,0:T(8,128)(2,1)S(1)} %get-tuple-element.21), channel_id=1, replica_groups=mesh['x_high'=2,'far'=8,'near'=2,'x_low'=2,'y'=4,'core'=2] {'x_high','ne..., dimensions={0} | all-to-all | bytes 1048576 | tf_op jit(solution)/shard_map/all_to_all | solution.py:37
  71.6 0.0 copy-start.3
  71.6 1.1 shard_map.81
  72.7 17.4 %all_to_all.63.got = bf16[16,64,128]{2,1,0:T(8,128)(2,1)S(1)} all-to-all(bf16[16,64,128]{2,1,0:T(8,128)(2,1)S(1)} %shard_map.81), channel_id=1, replica_groups=mesh['x_high'=2,'far'=8,'near'=2,'x_low'=2,'y'=4,'core'=2] {'x_low','y',..., dimensions={0} | all-to-all | bytes 524288 | tf_op jit(solution)/shard_map/all_to_all | solution.py:37
  90.1 0.0 copy-done.3
  90.1 0.8 shard_map.82
  91.0 11.2 %all_to_all.64.got = bf16[16,80,128]{2,1,0:T(8,128)(2,1)S(1)} all-to-all(bf16[16,80,128]{2,1,0:T(8,128)(2,1)S(1)} %get-tuple-element.24), channel_id=1, replica_groups=mesh['x_high'=2,'far'=8,'near'=2,'x_low'=2,'y'=4,'core'=2] {'x_low','y',..., dimensions={0} | all-to-all | bytes 655360 | tf_op jit(solution)/shard_map/all_to_all | solution.py:37
  102.1 1.1 shard_map.83
  103.3 11.5 %all_to_all.65.got = bf16[4,528,128]{2,1,0:T(8,128)(2,1)S(1)} all-to-all(bf16[4,528,128]{2,1,0:T(8,128)(2,1)S(1)} %shard_map.83), channel_id=1, replica_groups=mesh['x_high'=2,'far'=8,'near'=2,'x_low'=2,'y'=4,'core'=2] {'x_high','ne..., dimensions={0} | all-to-all | bytes 1081344 | tf_op jit(solution)/shard_map/all_to_all | solution.py:37
  114.7 0.1 shard_map.84
  114.9 22.8 %all_to_all.66.got = bf16[8,144,128]{2,1,0:T(8,128)(2,1)S(1)} all-to-all(bf16[8,144,128]{2,1,0:T(8,128)(2,1)S(1)} %shard_map.84), channel_id=1, replica_groups=mesh['x_high'=2,'far'=8,'near'=2,'x_low'=2,'y'=4,'core'=2] {'far'}, dimensions={0} | all-to-all | bytes 589824 | tf_op jit(solution)/shard_map/all_to_all | solution.py:37
  137.7 0.2 shard_map.85
  137.9 9.9 %all_to_all.67.got = bf16[4,512,128]{2,1,0:T(8,128)(2,1)S(1)} all-to-all(bf16[4,512,128]{2,1,0:T(8,128)(2,1)S(1)} %get-tuple-element.26), channel_id=1, replica_groups=mesh['x_high'=2,'far'=8,'near'=2,'x_low'=2,'y'=4,'core'=2] {'x_high','ne..., dimensions={0} | all-to-all | bytes 1048576 | tf_op jit(solution)/shard_map/all_to_all | solution.py:37
  147.8 1.1 shard_map.86
  148.9 17.5 %all_to_all.68.got = bf16[16,80,128]{2,1,0:T(8,128)(2,1)S(1)} all-to-all(bf16[16,80,128]{2,1,0:T(8,128)(2,1)S(1)} %shard_map.86), channel_id=1, replica_groups=mesh['x_high'=2,'far'=8,'near'=2,'x_low'=2,'y'=4,'core'=2] {'x_low','y',..., dimensions={0} | all-to-all | bytes 655360 | tf_op jit(solution)/shard_map/all_to_all | solution.py:37
  166.3 2.4 %shard_map.87 = (f32[64,128]{1,0:T(8,128)S(1)}, f32[64,128]{1,0:T(8,128)S(1)}, f32[32,32]{1,0:T(8,128)S(1)}, f32[32,32]{1,0:T(8,128)S(1)}, f32[32,1,1152]{2,1,0:T(1,128)S(1)}) custom-call(bf16[16,80,128]{2,1,0:T(8,128)(2,1)S(1)} %all_to_all.68.got, f32[64,128]{1,0:T(8,128)S(1)} %get-tuple-element.28.column_sums, f32[64,128]{1,0:T(8,128)S(1)} %bitcast.9, ...), custom_call_target="tpu_custom_call" | custom-call | tf_op jit(solution)/shard_map/pallas_call | solution.py:43
  168.8 12.1 %all_to_all.69.got = f32[32,1,1152]{2,1,0:T(1,128)S(1)} all-to-all(f32[32,1,1152]{2,1,0:T(1,128)S(1)} %get-tuple-element.29), channel_id=1, replica_groups=mesh['x_high'=2,'far'=8,'near'=2,'x_low'=2,'y'=4,'core'=2] {'x_high','x_..., dimensions={0} | all-to-all | bytes 294912 | tf_op jit(solution)/shard_map/all_to_all | solution.py:37
  181.0 15.7 %all_to_all.70.got = f32[16,1,1152]{2,1,0:T(1,128)S(1)} all-to-all(f32[16,1,1152]{2,1,0:T(1,128)S(1)} %shard_map.88), channel_id=1, replica_groups=mesh['x_high'=2,'far'=8,'near'=2,'x_low'=2,'y'=4,'core'=2] {'far','near'}, dimensions={0} | all-to-all | bytes 147456 | tf_op jit(solution)/shard_map/all_to_all | solution.py:37
  196.7 1.9 shard_map.89
  (1 shorter events, 0.0 us)
Async XLA Ops:
  0.6 13.6 %copy-start.4 = (s32[1,1,48]{2,1,0:T(1,128)S(1)}, s32[1,1,48]{2,1,0:T(1,128)}, u32[]{:S(2)}) copy-start(s32[1,1,48]{2,1,0:T(1,128)} %param.8) | copy-start | bytes 580
  0.6 13.6 %copy-start.5 = (s32[1,1,48]{2,1,0:T(1,128)S(1)}, s32[1,1,48]{2,1,0:T(1,128)}, u32[]{:S(2)}) copy-start(s32[1,1,48]{2,1,0:T(1,128)} %param.7) | copy-start | bytes 580
  0.7 0.8 copy-start.1
  2.1 17.4 %all-to-all-start = ((bf16[16,64,128]{2,1,0:T(8,128)(2,1)}), bf16[16,64,128]{2,1,0:T(8,128)(2,1)S(1)}, u32[]{:S(2)}, u32[]{:S(2)}) async-start(bf16[16,64,128]{2,1,0:T(8,128)(2,1)} %shard_map.76), calls=%async_computation | async-start | bytes 524288 | tf_op jit(solution)/shard_map/all_to_all | solution.py:37
  12.3 1.4 copy-start
  19.6 12.3 %copy-start.2 = (f32[2,32,128]{2,1,0:T(8,128)S(1)}, f32[2,32,128]{2,1,0:T(8,128)}, u32[]{:S(2)}) copy-start(f32[2,32,128]{2,1,0:T(8,128)} %param.5) | copy-start | bytes 98308
  71.6 18.5 %copy-start.3 = (bf16[2,128,128]{2,1,0:T(8,128)(2,1)S(1)}, bf16[2,128,128]{2,1,0:T(8,128)(2,1)}, u32[]{:S(2)}) copy-start(bf16[2,128,128]{2,1,0:T(8,128)(2,1)} %diagonal.3) | copy-start | bytes 196612

commit v10 on v9

--- a/solution.py
+++ b/solution.py
@@ -145,11 +145,6 @@
     return jnp.where(iota((K, K), 1) >= iota((K, K), 0), matrix, 0.0)
 
 
-def flip(matrix):
-    eye = jnp.where(iota((K, K), 0) == iota((K, K), 1), 1.0, 0.0)
-    return dot_t(eye, matrix)
-
-
 def fill(message, rows):
     for device in range(message.shape[0]):
         message[device, : rows.shape[0], :] = rows
@@ -180,7 +175,7 @@
     quarter = K // 4
     folded = jnp.concatenate([packed[:, 128 * line : 128 * (line + 1)] for line in range(quarter)])
     both = jnp.concatenate([lanes(folded, place) for place in range(4)])
-    other = flip(both)
+    other = both.T
     row, column = iota((K, K), 0), iota((K, K), 1)
     square = jnp.where(row >= column, both, other)
     middle = packed[:, 128 * quarter : 128 * quarter + K]
@@ -338,7 +333,7 @@
     alphas[0] = alpha_first[...]
     alphas[1] = alpha_last
     betas[0] = beta_first[...]
-    betas[1] = flip(upper)
+    betas[1] = upper.T
 
 
 def exchange(message, vectors, tiles, turned, lists):

time: 199 us -> 199 us (level)
  no operation moved by 1% of the time
where the time goes in v10:
time: 199 us
  blocking collectives  169 us (85%)
  Pallas kernels  11.3 us (6%)
  starting transfers between devices  10.2 us (5%)
  waiting for transfers between devices  5.21 us (3%)
  local copies, waits for them, and re-layouts  2.18 us (1%)
    all_to_all x11, blocking collectives, swap(): return lax.all_to_all(parts, axis, 0, 0, tiled=True)  169 us
    pallas_call x14, Pallas kernels, call(): pl.pallas_call(kernel, out_shape=outs, in_specs=specs, out_specs=jax.tree...  11.3 us
    all_to_all x1, starting transfers between devices, swap(): return lax.all_to_all(parts, axis, 0, 0, tiled=True)  10.2 us
    all_to_all x1, waiting for transfers between devices, swap(): return lax.all_to_all(parts, axis, 0, 0, tiled=True)  5.21 us
  transfers between devices with their start and end apart: 1, of which 1 were waited for; matrix products, arithmetic and copies ran while one was open for 0% of the time, Pallas kernels for 0%

profile of v10, /device:TPU:1, one launch (start us, length us, event | category | flops | bytes accessed | tf_op | source)
XLA Modules:
  0.0 198.5 jit_solution(11637391847833853291)
XLA Ops:
  0.6 0.0 copy-start.4
  0.6 0.0 copy-start.5
  0.7 0.0 copy-start.1
  0.7 0.8 copy-done.1
  1.4 0.7 shard_map.76
  2.1 10.2 %all-to-all-start = ((bf16[16,64,128]{2,1,0:T(8,128)(2,1)}), bf16[16,64,128]{2,1,0:T(8,128)(2,1)S(1)}, u32[]{:S(2)}, u32[]{:S(2)}) async-start(bf16[16,64,128]{2,1,0:T(8,128)(2,1)} %shard_map.76), calls=%async_computation | async-start | bytes 524288 | tf_op jit(solution)/shard_map/all_to_all | solution.py:37
  12.3 0.0 copy-start
  12.4 1.4 copy-done
  13.8 0.5 shard_map.77
  14.3 0.0 copy-done.4
  14.3 0.0 copy-done.5
  14.3 0.1 pad_add_fusion.lists
  14.4 5.2 %all-to-all-done.got = bf16[16,64,128]{2,1,0:T(8,128)(2,1)S(1)} async-done(((bf16[16,64,128]{2,1,0:T(8,128)(2,1)}), bf16[16,64,128]{2,1,0:T(8,128)(2,1)S(1)}, u32[]{:S(2)}, u32[]{:S(2)}) %all-to-all-start) | async-done | bytes 262176 | tf_op jit(solution)/shard_map/all_to_all | solution.py:37
  19.6 0.0 copy-start.2
  19.6 1.1 shard_map.78
  20.7 11.1 %all_to_all.60.got = bf16[4,512,128]{2,1,0:T(8,128)(2,1)S(1)} all-to-all(bf16[4,512,128]{2,1,0:T(8,128)(2,1)S(1)} %shard_map.78), channel_id=1, replica_groups=mesh['x_high'=2,'far'=8,'near'=2,'x_low'=2,'y'=4,'core'=2] {'x_high','ne..., dimensions={0} | all-to-all | bytes 1048576 | tf_op jit(solution)/shard_map/all_to_all | solution.py:37
  31.8 0.0 copy-done.2
  31.8 0.1 shard_map.79
  31.9 28.9 %all_to_all.61.got = bf16[8,128,128]{2,1,0:T(8,128)(2,1)S(1)} all-to-all(bf16[8,128,128]{2,1,0:T(8,128)(2,1)S(1)} %shard_map.79), channel_id=1, replica_groups=mesh['x_high'=2,'far'=8,'near'=2,'x_low'=2,'y'=4,'core'=2] {'far'}, dimensions={0} | all-to-all | bytes 524288 | tf_op jit(solution)/shard_map/all_to_all | solution.py:37
  60.8 0.1 shard_map.80
  60.9 10.7 %all_to_all.62.got = bf16[4,512,128]{2,1,0:T(8,128)(2,1)S(1)} all-to-all(bf16[4,512,128]{2,1,0:T(8,128)(2,1)S(1)} %get-tuple-element.21), channel_id=1, replica_groups=mesh['x_high'=2,'far'=8,'near'=2,'x_low'=2,'y'=4,'core'=2] {'x_high','ne..., dimensions={0} | all-to-all | bytes 1048576 | tf_op jit(solution)/shard_map/all_to_all | solution.py:37
  71.6 0.0 copy-start.3
  71.6 1.1 shard_map.81
  72.7 17.4 %all_to_all.63.got = bf16[16,64,128]{2,1,0:T(8,128)(2,1)S(1)} all-to-all(bf16[16,64,128]{2,1,0:T(8,128)(2,1)S(1)} %shard_map.81), channel_id=1, replica_groups=mesh['x_high'=2,'far'=8,'near'=2,'x_low'=2,'y'=4,'core'=2] {'x_low','y',..., dimensions={0} | all-to-all | bytes 524288 | tf_op jit(solution)/shard_map/all_to_all | solution.py:37
  90.1 0.0 copy-done.3
  90.1 0.8 shard_map.82
  90.9 11.2 %all_to_all.64.got = bf16[16,80,128]{2,1,0:T(8,128)(2,1)S(1)} all-to-all(bf16[16,80,128]{2,1,0:T(8,128)(2,1)S(1)} %get-tuple-element.24), channel_id=1, replica_groups=mesh['x_high'=2,'far'=8,'near'=2,'x_low'=2,'y'=4,'core'=2] {'x_low','y',..., dimensions={0} | all-to-all | bytes 655360 | tf_op jit(solution)/shard_map/all_to_all | solution.py:37
  102.1 1.1 shard_map.83
  103.2 11.5 %all_to_all.65.got = bf16[4,528,128]{2,1,0:T(8,128)(2,1)S(1)} all-to-all(bf16[4,528,128]{2,1,0:T(8,128)(2,1)S(1)} %shard_map.83), channel_id=1, replica_groups=mesh['x_high'=2,'far'=8,'near'=2,'x_low'=2,'y'=4,'core'=2] {'x_high','ne..., dimensions={0} | all-to-all | bytes 1081344 | tf_op jit(solution)/shard_map/all_to_all | solution.py:37
  114.7 0.1 shard_map.84
  114.9 22.8 %all_to_all.66.got = bf16[8,144,128]{2,1,0:T(8,128)(2,1)S(1)} all-to-all(bf16[8,144,128]{2,1,0:T(8,128)(2,1)S(1)} %shard_map.84), channel_id=1, replica_groups=mesh['x_high'=2,'far'=8,'near'=2,'x_low'=2,'y'=4,'core'=2] {'far'}, dimensions={0} | all-to-all | bytes 589824 | tf_op jit(solution)/shard_map/all_to_all | solution.py:37
  137.7 0.2 shard_map.85
  137.9 9.9 %all_to_all.67.got = bf16[4,512,128]{2,1,0:T(8,128)(2,1)S(1)} all-to-all(bf16[4,512,128]{2,1,0:T(8,128)(2,1)S(1)} %get-tuple-element.26), channel_id=1, replica_groups=mesh['x_high'=2,'far'=8,'near'=2,'x_low'=2,'y'=4,'core'=2] {'x_high','ne..., dimensions={0} | all-to-all | bytes 1048576 | tf_op jit(solution)/shard_map/all_to_all | solution.py:37
  147.8 1.1 shard_map.86
  148.9 17.5 %all_to_all.68.got = bf16[16,80,128]{2,1,0:T(8,128)(2,1)S(1)} all-to-all(bf16[16,80,128]{2,1,0:T(8,128)(2,1)S(1)} %shard_map.86), channel_id=1, replica_groups=mesh['x_high'=2,'far'=8,'near'=2,'x_low'=2,'y'=4,'core'=2] {'x_low','y',..., dimensions={0} | all-to-all | bytes 655360 | tf_op jit(solution)/shard_map/all_to_all | solution.py:37
  166.3 2.4 %shard_map.87 = (f32[64,128]{1,0:T(8,128)S(1)}, f32[64,128]{1,0:T(8,128)S(1)}, f32[32,32]{1,0:T(8,128)S(1)}, f32[32,32]{1,0:T(8,128)S(1)}, f32[32,1,1152]{2,1,0:T(1,128)S(1)}) custom-call(bf16[16,80,128]{2,1,0:T(8,128)(2,1)S(1)} %all_to_all.68.got, f32[64,128]{1,0:T(8,128)S(1)} %get-tuple-element.28.column_sums, f32[64,128]{1,0:T(8,128)S(1)} %bitcast.9, ...), custom_call_target="tpu_custom_call" | custom-call | tf_op jit(solution)/shard_map/pallas_call | solution.py:43
  168.8 12.2 %all_to_all.69.got = f32[32,1,1152]{2,1,0:T(1,128)S(1)} all-to-all(f32[32,1,1152]{2,1,0:T(1,128)S(1)} %get-tuple-element.29), channel_id=1, replica_groups=mesh['x_high'=2,'far'=8,'near'=2,'x_low'=2,'y'=4,'core'=2] {'x_high','x_..., dimensions={0} | all-to-all | bytes 294912 | tf_op jit(solution)/shard_map/all_to_all | solution.py:37
  181.0 15.7 %all_to_all.70.got = f32[16,1,1152]{2,1,0:T(1,128)S(1)} all-to-all(f32[16,1,1152]{2,1,0:T(1,128)S(1)} %shard_map.88), channel_id=1, replica_groups=mesh['x_high'=2,'far'=8,'near'=2,'x_low'=2,'y'=4,'core'=2] {'far','near'}, dimensions={0} | all-to-all | bytes 147456 | tf_op jit(solution)/shard_map/all_to_all | solution.py:37
  196.7 1.8 shard_map.89
  (1 shorter events, 0.0 us)
Async XLA Ops:
  0.6 13.6 %copy-start.4 = (s32[1,1,48]{2,1,0:T(1,128)S(1)}, s32[1,1,48]{2,1,0:T(1,128)}, u32[]{:S(2)}) copy-start(s32[1,1,48]{2,1,0:T(1,128)} %param.8) | copy-start | bytes 580
  0.6 13.6 %copy-start.5 = (s32[1,1,48]{2,1,0:T(1,128)S(1)}, s32[1,1,48]{2,1,0:T(1,128)}, u32[]{:S(2)}) copy-start(s32[1,1,48]{2,1,0:T(1,128)} %param.7) | copy-start | bytes 580
  0.7 0.8 copy-start.1
  2.1 17.4 %all-to-all-start = ((bf16[16,64,128]{2,1,0:T(8,128)(2,1)}), bf16[16,64,128]{2,1,0:T(8,128)(2,1)S(1)}, u32[]{:S(2)}, u32[]{:S(2)}) async-start(bf16[16,64,128]{2,1,0:T(8,128)(2,1)} %shard_map.76), calls=%async_computation | async-start | bytes 524288 | tf_op jit(solution)/shard_map/all_to_all | solution.py:37
  12.3 1.4 copy-start
  19.6 12.3 %copy-start.2 = (f32[2,32,128]{2,1,0:T(8,128)S(1)}, f32[2,32,128]{2,1,0:T(8,128)}, u32[]{:S(2)}) copy-start(f32[2,32,128]{2,1,0:T(8,128)} %param.5) | copy-start | bytes 98308
  71.6 18.5 %copy-start.3 = (bf16[2,128,128]{2,1,0:T(8,128)(2,1)S(1)}, bf16[2,128,128]{2,1,0:T(8,128)(2,1)}, u32[]{:S(2)}) copy-start(bf16[2,128,128]{2,1,0:T(8,128)(2,1)} %diagonal.3) | copy-start | bytes 196612

commit v11 on v10

--- a/solution.py
+++ b/solution.py
@@ -161,13 +161,15 @@
 
 
 def pack(square, cross):
-    row, column = iota((K, 128), 0), iota((K, 128), 1)
-    both = jnp.where(column < K, jnp.where(row >= column, square, cross), 0.0)
+    row, column = iota((K, K), 0), iota((K, K), 1)
+    wide = jnp.zeros((K, 128 - K), f32)
+    both = jnp.concatenate([jnp.where(row >= column, square, cross), wide], axis=1)
     quarter = K // 4
     folded = both[:quarter]
     for place in range(1, 4):
         folded += pltpu.roll(both[place * quarter : (place + 1) * quarter], K * place, 1)
-    middle = jnp.sum(jnp.where(row == column, cross, 0.0), axis=0, keepdims=True)
+    middle = jnp.concatenate([jnp.where(row == column, cross, 0.0), wide], axis=1)
+    middle = jnp.sum(middle, axis=0, keepdims=True)
     return jnp.concatenate([folded[line : line + 1] for line in range(quarter)] + [middle], axis=1)
 
 
@@ -267,16 +269,17 @@
 
 def middle_kernel(got, column_sums, start, diagonal, image, message):
     images = image_of(got, column_sums, start, diagonal)
-    grams = jnp.zeros((K, 128), f32)
-    empty = jnp.zeros((K, 128), f32)
+    upper = jnp.zeros((K, 2 * K), f32)
+    lower = jnp.zeros((K, 2 * K), f32)
     for block in range(OWN // K):
         where = slice(block * K, (block + 1) * K)
         vectors = start[where, :]
         image[where, :] = images[block]
-        pair = [vectors, images[block]]
-        grams += dot_t(vectors, jnp.concatenate(pair + [empty, empty]))
-        grams += dot_t(images[block], jnp.concatenate([empty, empty] + pair))
+        pair = jnp.concatenate([vectors, images[block]])
+        upper += dot_t(vectors, pair)
+        lower += dot_t(images[block], pair)
     fill(message, jnp.concatenate(images).astype(bf16))
+    grams = jnp.concatenate([upper, lower], axis=1)
     message[:, OWN:, :] = spread_slices(grams).reshape(COLUMNS, EXTRA, 128)
 
 
@@ -290,9 +293,8 @@
     inverse = lanes(work[:K], 2)
     weights = pltpu.roll(work[K:], 128 - 2 * K, 1)[:, : 2 * K]
     back = dot(dot_t(upper, inverse), inverse)
-    square = jnp.zeros((K, 128), f32)
-    cross = jnp.zeros((K, 128), f32)
-    empty = [jnp.zeros((K, 128), f32)] * 3
+    square = jnp.zeros((K, K), f32)
+    cross = jnp.zeros((K, K), f32)
     for block in range(OWN // K):
         where = slice(block * K, (block + 1) * K)
         current = dot(weights, jnp.concatenate([start[where, :], first[where, :]]))
@@ -300,9 +302,8 @@
         result -= dot(back, start[where, :])
         basis[where, :] = current
         image[where, :] = result
-        wide = jnp.concatenate([result] + empty)
-        square += dot_t(result, wide)
-        cross += dot_t(current, wide)
+        square += dot_t(result, result)
+        cross += dot_t(current, result)
     packed = pack(square, cross)
     for device in range(message.shape[0]):
         message[device] = packed

time: 199 us -> 199 us (level)
  no operation moved by 1% of the time
where the time goes in v11:
time: 199 us; the launch traced here: 198 us
  blocking collectives  169 us (85%)
  Pallas kernels  11.2 us (6%)
  starting transfers between devices  10.2 us (5%)
  waiting for transfers between devices  5.21 us (3%)
  local copies, waits for them, and re-layouts  2.18 us (1%)
    all_to_all x11, blocking collectives, swap(): return lax.all_to_all(parts, axis, 0, 0, tiled=True)  169 us
    pallas_call x14, Pallas kernels, call(): pl.pallas_call(kernel, out_shape=outs, in_specs=specs, out_specs=jax.tree...  11.2 us
    all_to_all x1, starting transfers between devices, swap(): return lax.all_to_all(parts, axis, 0, 0, tiled=True)  10.2 us
    all_to_all x1, waiting for transfers between devices, swap(): return lax.all_to_all(parts, axis, 0, 0, tiled=True)  5.21 us
  transfers between devices with their start and end apart: 1, of which 1 were waited for; matrix products, arithmetic and copies ran while one was open for 0% of the time, Pallas kernels for 0%

profile of v11, /device:TPU:1, one launch (start us, length us, event | category | flops | bytes accessed | tf_op | source)
XLA Modules:
  0.0 198.4 jit_solution(7095693359639000687)
XLA Ops:
  0.6 0.0 copy-start.4
  0.6 0.0 copy-start.5
  0.7 0.0 copy-start.1
  0.7 0.8 copy-done.1
  1.4 0.7 shard_map.76
  2.1 10.2 %all-to-all-start = ((bf16[16,64,128]{2,1,0:T(8,128)(2,1)}), bf16[16,64,128]{2,1,0:T(8,128)(2,1)S(1)}, u32[]{:S(2)}, u32[]{:S(2)}) async-start(bf16[16,64,128]{2,1,0:T(8,128)(2,1)} %shard_map.76), calls=%async_computation | async-start | bytes 524288 | tf_op jit(solution)/shard_map/all_to_all | solution.py:37
  12.3 0.0 copy-start
  12.4 1.4 copy-done
  13.8 0.5 shard_map.77
  14.3 0.0 copy-done.4
  14.3 0.0 copy-done.5
  14.3 0.1 pad_add_fusion.lists
  14.4 5.2 %all-to-all-done.got = bf16[16,64,128]{2,1,0:T(8,128)(2,1)S(1)} async-done(((bf16[16,64,128]{2,1,0:T(8,128)(2,1)}), bf16[16,64,128]{2,1,0:T(8,128)(2,1)S(1)}, u32[]{:S(2)}, u32[]{:S(2)}) %all-to-all-start) | async-done | bytes 262176 | tf_op jit(solution)/shard_map/all_to_all | solution.py:37
  19.6 0.0 copy-start.2
  19.6 1.1 shard_map.78
  20.7 11.1 %all_to_all.60.got = bf16[4,512,128]{2,1,0:T(8,128)(2,1)S(1)} all-to-all(bf16[4,512,128]{2,1,0:T(8,128)(2,1)S(1)} %shard_map.78), channel_id=1, replica_groups=mesh['x_high'=2,'far'=8,'near'=2,'x_low'=2,'y'=4,'core'=2] {'x_high','ne..., dimensions={0} | all-to-all | bytes 1048576 | tf_op jit(solution)/shard_map/all_to_all | solution.py:37
  31.8 0.0 copy-done.2
  31.8 0.1 shard_map.79
  31.9 28.9 %all_to_all.61.got = bf16[8,128,128]{2,1,0:T(8,128)(2,1)S(1)} all-to-all(bf16[8,128,128]{2,1,0:T(8,128)(2,1)S(1)} %shard_map.79), channel_id=1, replica_groups=mesh['x_high'=2,'far'=8,'near'=2,'x_low'=2,'y'=4,'core'=2] {'far'}, dimensions={0} | all-to-all | bytes 524288 | tf_op jit(solution)/shard_map/all_to_all | solution.py:37
  60.9 0.1 shard_map.80
  60.9 10.7 %all_to_all.62.got = bf16[4,512,128]{2,1,0:T(8,128)(2,1)S(1)} all-to-all(bf16[4,512,128]{2,1,0:T(8,128)(2,1)S(1)} %get-tuple-element.21), channel_id=1, replica_groups=mesh['x_high'=2,'far'=8,'near'=2,'x_low'=2,'y'=4,'core'=2] {'x_high','ne..., dimensions={0} | all-to-all | bytes 1048576 | tf_op jit(solution)/shard_map/all_to_all | solution.py:37
  71.6 0.0 copy-start.3
  71.6 1.1 shard_map.81
  72.7 17.4 %all_to_all.63.got = bf16[16,64,128]{2,1,0:T(8,128)(2,1)S(1)} all-to-all(bf16[16,64,128]{2,1,0:T(8,128)(2,1)S(1)} %shard_map.81), channel_id=1, replica_groups=mesh['x_high'=2,'far'=8,'near'=2,'x_low'=2,'y'=4,'core'=2] {'x_low','y',..., dimensions={0} | all-to-all | bytes 524288 | tf_op jit(solution)/shard_map/all_to_all | solution.py:37
  90.1 0.0 copy-done.3
  90.1 0.7 shard_map.82
  90.9 11.2 %all_to_all.64.got = bf16[16,80,128]{2,1,0:T(8,128)(2,1)S(1)} all-to-all(bf16[16,80,128]{2,1,0:T(8,128)(2,1)S(1)} %get-tuple-element.24), channel_id=1, replica_groups=mesh['x_high'=2,'far'=8,'near'=2,'x_low'=2,'y'=4,'core'=2] {'x_low','y',..., dimensions={0} | all-to-all | bytes 655360 | tf_op jit(solution)/shard_map/all_to_all | solution.py:37
  102.0 1.1 shard_map.83
  103.2 11.5 %all_to_all.65.got = bf16[4,528,128]{2,1,0:T(8,128)(2,1)S(1)} all-to-all(bf16[4,528,128]{2,1,0:T(8,128)(2,1)S(1)} %shard_map.83), channel_id=1, replica_groups=mesh['x_high'=2,'far'=8,'near'=2,'x_low'=2,'y'=4,'core'=2] {'x_high','ne..., dimensions={0} | all-to-all | bytes 1081344 | tf_op jit(solution)/shard_map/all_to_all | solution.py:37
  114.7 0.1 shard_map.84
  114.8 22.8 %all_to_all.66.got = bf16[8,144,128]{2,1,0:T(8,128)(2,1)S(1)} all-to-all(bf16[8,144,128]{2,1,0:T(8,128)(2,1)S(1)} %shard_map.84), channel_id=1, replica_groups=mesh['x_high'=2,'far'=8,'near'=2,'x_low'=2,'y'=4,'core'=2] {'far'}, dimensions={0} | all-to-all | bytes 589824 | tf_op jit(solution)/shard_map/all_to_all | solution.py:37
  137.6 0.2 shard_map.85
  137.8 9.9 %all_to_all.67.got = bf16[4,512,128]{2,1,0:T(8,128)(2,1)S(1)} all-to-all(bf16[4,512,128]{2,1,0:T(8,128)(2,1)S(1)} %get-tuple-element.26), channel_id=1, replica_groups=mesh['x_high'=2,'far'=8,'near'=2,'x_low'=2,'y'=4,'core'=2] {'x_high','ne..., dimensions={0} | all-to-all | bytes 1048576 | tf_op jit(solution)/shard_map/all_to_all | solution.py:37
  147.7 1.1 shard_map.86
  148.8 17.5 %all_to_all.68.got = bf16[16,80,128]{2,1,0:T(8,128)(2,1)S(1)} all-to-all(bf16[16,80,128]{2,1,0:T(8,128)(2,1)S(1)} %shard_map.86), channel_id=1, replica_groups=mesh['x_high'=2,'far'=8,'near'=2,'x_low'=2,'y'=4,'core'=2] {'x_low','y',..., dimensions={0} | all-to-all | bytes 655360 | tf_op jit(solution)/shard_map/all_to_all | solution.py:37
  166.3 2.4 %shard_map.87 = (f32[64,128]{1,0:T(8,128)S(1)}, f32[64,128]{1,0:T(8,128)S(1)}, f32[32,32]{1,0:T(8,128)S(1)}, f32[32,32]{1,0:T(8,128)S(1)}, f32[32,1,1152]{2,1,0:T(1,128)S(1)}) custom-call(bf16[16,80,128]{2,1,0:T(8,128)(2,1)S(1)} %all_to_all.68.got, f32[64,128]{1,0:T(8,128)S(1)} %get-tuple-element.28.column_sums, f32[64,128]{1,0:T(8,128)S(1)} %bitcast.9, ...), custom_call_target="tpu_custom_call" | custom-call | tf_op jit(solution)/shard_map/pallas_call | solution.py:43
  168.7 12.1 %all_to_all.69.got = f32[32,1,1152]{2,1,0:T(1,128)S(1)} all-to-all(f32[32,1,1152]{2,1,0:T(1,128)S(1)} %get-tuple-element.29), channel_id=1, replica_groups=mesh['x_high'=2,'far'=8,'near'=2,'x_low'=2,'y'=4,'core'=2] {'x_high','x_..., dimensions={0} | all-to-all | bytes 294912 | tf_op jit(solution)/shard_map/all_to_all | solution.py:37
  180.9 15.7 %all_to_all.70.got = f32[16,1,1152]{2,1,0:T(1,128)S(1)} all-to-all(f32[16,1,1152]{2,1,0:T(1,128)S(1)} %shard_map.88), channel_id=1, replica_groups=mesh['x_high'=2,'far'=8,'near'=2,'x_low'=2,'y'=4,'core'=2] {'far','near'}, dimensions={0} | all-to-all | bytes 147456 | tf_op jit(solution)/shard_map/all_to_all | solution.py:37
  196.6 1.8 shard_map.89
  (1 shorter events, 0.0 us)
Async XLA Ops:
  0.6 13.6 %copy-start.4 = (s32[1,1,48]{2,1,0:T(1,128)S(1)}, s32[1,1,48]{2,1,0:T(1,128)}, u32[]{:S(2)}) copy-start(s32[1,1,48]{2,1,0:T(1,128)} %param.8) | copy-start | bytes 580
  0.6 13.6 %copy-start.5 = (s32[1,1,48]{2,1,0:T(1,128)S(1)}, s32[1,1,48]{2,1,0:T(1,128)}, u32[]{:S(2)}) copy-start(s32[1,1,48]{2,1,0:T(1,128)} %param.7) | copy-start | bytes 580
  0.7 0.8 copy-start.1
  2.1 17.4 %all-to-all-start = ((bf16[16,64,128]{2,1,0:T(8,128)(2,1)}), bf16[16,64,128]{2,1,0:T(8,128)(2,1)S(1)}, u32[]{:S(2)}, u32[]{:S(2)}) async-start(bf16[16,64,128]{2,1,0:T(8,128)(2,1)} %shard_map.76), calls=%async_computation | async-start | bytes 524288 | tf_op jit(solution)/shard_map/all_to_all | solution.py:37
  12.3 1.4 copy-start
  19.6 12.3 %copy-start.2 = (f32[2,32,128]{2,1,0:T(8,128)S(1)}, f32[2,32,128]{2,1,0:T(8,128)}, u32[]{:S(2)}) copy-start(f32[2,32,128]{2,1,0:T(8,128)} %param.5) | copy-start | bytes 98308
  71.6 18.5 %copy-start.3 = (bf16[2,128,128]{2,1,0:T(8,128)(2,1)S(1)}, bf16[2,128,128]{2,1,0:T(8,128)(2,1)}, u32[]{:S(2)}) copy-start(bf16[2,128,128]{2,1,0:T(8,128)(2,1)} %diagonal.3) | copy-start | bytes 196612

commit v12 on v11

--- a/solution.py
+++ b/solution.py
@@ -150,10 +150,11 @@
         message[device, : rows.shape[0], :] = rows
 
 
-def stage_kernel(tiles, staged, turned):
+def stage_kernel(tiles, start, diagonal, staged, turned, part):
     for tile in range(tiles.shape[0]):
         staged[tile] = tiles[tile]
         turned[tile] = tiles[tile].T
+    part[...] = jnp.concatenate(own_part(start, diagonal))
 
 
 def prepare_kernel(start, message):
@@ -252,23 +253,30 @@
             message[device, OWN:, :] = piece[0][...]
 
 
-def image_of(got, column_sums, vectors, diagonal):
+def own_part(vectors, diagonal):
+    parts = []
+    for block in range(OWN // K):
+        narrow = vectors[block * K : (block + 1) * K, :].astype(bf16)
+        part = dot_t(narrow, diagonal[block], None)
+        part += jnp.dot(narrow, diagonal[block], preferred_element_type=f32)
+        parts.append(0.5 * part)
+    return parts
+
+
+def image_of(got, column_sums, parts):
     images = []
     for block in range(OWN // K):
         where = slice(block * K, (block + 1) * K)
-        narrow = vectors[where, :].astype(bf16)
-        image = dot_t(narrow, diagonal[block], None)
-        image += jnp.dot(narrow, diagonal[block], preferred_element_type=f32)
-        image = 0.5 * image + column_sums[where, :]
         total = got[0, where, :].astype(f32)
         for device in range(1, COLUMNS):
             total += got[device, where, :].astype(f32)
-        images.append(image + total)
+        images.append(parts[block] + column_sums[where, :] + total)
     return images
 
 
-def middle_kernel(got, column_sums, start, diagonal, image, message):
-    images = image_of(got, column_sums, start, diagonal)
+def middle_kernel(got, column_sums, start, part, image, message):
+    parts = [part[block * K : (block + 1) * K, :] for block in range(OWN // K)]
+    images = image_of(got, column_sums, parts)
     upper = jnp.zeros((K, 2 * K), f32)
     lower = jnp.zeros((K, 2 * K), f32)
     for block in range(OWN // K):
@@ -286,7 +294,7 @@
 def finish_kernel(
     got, column_sums, start, first, diagonal, basis, image, alpha, beta, message
 ):
-    images = image_of(got, column_sums, first, diagonal)
+    images = image_of(got, column_sums, own_part(first, diagonal))
     sums = join_slices(got[:, OWN:, :].reshape(COLUMNS * EXTRA, 128))
     work = eliminate(jnp.concatenate([sums, pltpu.roll(sums, 128 - 2 * K, 1)]))
     upper = upper_part(lanes(work[K:], 1))
@@ -368,10 +376,13 @@
 def local(start_block, tile_values, tile_rows, tile_columns, diagonal_blocks):
     start = start_block.reshape(OWN, 128)
     tiles = tile_values[0, 0]
-    matrix = (
-        *call(stage_kernel, (out(tiles.shape, bf16), out(tiles.shape, bf16)), (), (tiles,)),
-        jnp.concatenate([tile_rows[0, 0], tile_columns[0, 0]]),
-    )
+    *staged, part = call(
+        stage_kernel,
+        (out(tiles.shape, bf16), out(tiles.shape, bf16), out((OWN, 128), f32)),
+        (),
+        (tiles, start, diagonal_blocks),
+    )
+    matrix = (*staged, jnp.concatenate([tile_rows[0, 0], tile_columns[0, 0]]))
     vectors = out((OWN, 128), f32)
     square = out((K, K), f32)
     message = call(prepare_kernel, out((COLUMNS, OWN, 128), bf16), (), (start,))
@@ -380,7 +391,7 @@
         middle_kernel,
         (vectors, out((COLUMNS, OWN + EXTRA, 128), bf16)),
         (),
-        (got, column_sums, start, diagonal_blocks),
+        (got, column_sums, start, part),
     )
     got, column_sums = exchange(message, first, *matrix)
     planes, depths = lax.axis_size(PLANE), lax.axis_size(DEPTH)

time: 199 us -> 199 us (level)
  no operation moved by 1% of the time
where the time goes in v12:
time: 199 us; the launch traced here: 198 us
  blocking collectives  169 us (85%)
  Pallas kernels  11.1 us (6%)
  starting transfers between devices  10.2 us (5%)
  local copies, waits for them, and re-layouts  3.78 us (2%)
  waiting for transfers between devices  3.63 us (2%)
    all_to_all x11, blocking collectives, swap(): return lax.all_to_all(parts, axis, 0, 0, tiled=True)  169 us
    pallas_call x14, Pallas kernels, call(): pl.pallas_call(kernel, out_shape=outs, in_specs=specs, out_specs=jax.tree...  11.1 us
    all_to_all x1, starting transfers between devices, swap(): return lax.all_to_all(parts, axis, 0, 0, tiled=True)  10.2 us
  transfers between devices with their start and end apart: 1, of which 1 were waited for; matrix products, arithmetic and copies ran while one was open for 0% of the time, Pallas kernels for 0%

profile of v12, /device:TPU:1, one launch (start us, length us, event | category | flops | bytes accessed | tf_op | source)
XLA Modules:
  0.0 198.3 jit_solution(9244307511606366147)
XLA Ops:
  0.6 0.0 copy-start.6
  0.6 0.0 copy-start.7
  0.7 0.0 copy-start.1
  0.7 0.8 copy-done.1
  1.4 0.7 shard_map.76
  2.1 10.2 %all-to-all-start = ((bf16[16,64,128]{2,1,0:T(8,128)(2,1)}), bf16[16,64,128]{2,1,0:T(8,128)(2,1)S(1)}, u32[]{:S(2)}, u32[]{:S(2)}) async-start(bf16[16,64,128]{2,1,0:T(8,128)(2,1)} %shard_map.76), calls=%async_computation | async-start | bytes 524288 | tf_op jit(solution)/shard_map/all_to_all | solution.py:37
  12.3 0.0 copy-start
  12.4 1.4 copy-done
  13.8 0.0 copy-start.2
  13.8 0.8 copy-done.2
  14.5 0.0 copy-start.4
  14.5 0.8 copy-done.4
  15.4 0.5 shard_map.77
  15.9 0.0 copy-done.6
  15.9 0.0 copy-done.7
  15.9 0.1 pad_add_fusion.lists
  16.0 3.6 %all-to-all-done.got = bf16[16,64,128]{2,1,0:T(8,128)(2,1)S(1)} async-done(((bf16[16,64,128]{2,1,0:T(8,128)(2,1)}), bf16[16,64,128]{2,1,0:T(8,128)(2,1)S(1)}, u32[]{:S(2)}, u32[]{:S(2)}) %all-to-all-start) | async-done | bytes 262176 | tf_op jit(solution)/shard_map/all_to_all | solution.py:37
  19.6 0.0 copy-start.3
  19.6 1.1 shard_map.78
  20.7 11.1 %all_to_all.60.got = bf16[4,512,128]{2,1,0:T(8,128)(2,1)S(1)} all-to-all(bf16[4,512,128]{2,1,0:T(8,128)(2,1)S(1)} %shard_map.78), channel_id=1, replica_groups=mesh['x_high'=2,'far'=8,'near'=2,'x_low'=2,'y'=4,'core'=2] {'x_high','ne..., dimensions={0} | all-to-all | bytes 1048576 | tf_op jit(solution)/shard_map/all_to_all | solution.py:37
  31.8 0.0 copy-done.3
  31.8 0.1 shard_map.79
  31.9 28.9 %all_to_all.61.got = bf16[8,128,128]{2,1,0:T(8,128)(2,1)S(1)} all-to-all(bf16[8,128,128]{2,1,0:T(8,128)(2,1)S(1)} %shard_map.79), channel_id=1, replica_groups=mesh['x_high'=2,'far'=8,'near'=2,'x_low'=2,'y'=4,'core'=2] {'far'}, dimensions={0} | all-to-all | bytes 524288 | tf_op jit(solution)/shard_map/all_to_all | solution.py:37
  60.9 0.1 shard_map.80
  60.9 10.7 %all_to_all.62.got = bf16[4,512,128]{2,1,0:T(8,128)(2,1)S(1)} all-to-all(bf16[4,512,128]{2,1,0:T(8,128)(2,1)S(1)} %get-tuple-element.22), channel_id=1, replica_groups=mesh['x_high'=2,'far'=8,'near'=2,'x_low'=2,'y'=4,'core'=2] {'x_high','ne..., dimensions={0} | all-to-all | bytes 1048576 | tf_op jit(solution)/shard_map/all_to_all | solution.py:37
  71.6 1.1 shard_map.81
  72.7 17.4 %all_to_all.63.got = bf16[16,64,128]{2,1,0:T(8,128)(2,1)S(1)} all-to-all(bf16[16,64,128]{2,1,0:T(8,128)(2,1)S(1)} %shard_map.81), channel_id=1, replica_groups=mesh['x_high'=2,'far'=8,'near'=2,'x_low'=2,'y'=4,'core'=2] {'x_low','y',..., dimensions={0} | all-to-all | bytes 524288 | tf_op jit(solution)/shard_map/all_to_all | solution.py:37
  90.1 0.6 shard_map.82
  90.7 11.2 %all_to_all.64.got = bf16[16,80,128]{2,1,0:T(8,128)(2,1)S(1)} all-to-all(bf16[16,80,128]{2,1,0:T(8,128)(2,1)S(1)} %get-tuple-element.26), channel_id=1, replica_groups=mesh['x_high'=2,'far'=8,'near'=2,'x_low'=2,'y'=4,'core'=2] {'x_low','y',..., dimensions={0} | all-to-all | bytes 655360 | tf_op jit(solution)/shard_map/all_to_all | solution.py:37
  101.9 1.1 shard_map.83
  103.0 11.5 %all_to_all.65.got = bf16[4,528,128]{2,1,0:T(8,128)(2,1)S(1)} all-to-all(bf16[4,528,128]{2,1,0:T(8,128)(2,1)S(1)} %shard_map.83), channel_id=1, replica_groups=mesh['x_high'=2,'far'=8,'near'=2,'x_low'=2,'y'=4,'core'=2] {'x_high','ne..., dimensions={0} | all-to-all | bytes 1081344 | tf_op jit(solution)/shard_map/all_to_all | solution.py:37
  114.5 0.1 shard_map.84
  114.6 22.8 %all_to_all.66.got = bf16[8,144,128]{2,1,0:T(8,128)(2,1)S(1)} all-to-all(bf16[8,144,128]{2,1,0:T(8,128)(2,1)S(1)} %shard_map.84), channel_id=1, replica_groups=mesh['x_high'=2,'far'=8,'near'=2,'x_low'=2,'y'=4,'core'=2] {'far'}, dimensions={0} | all-to-all | bytes 589824 | tf_op jit(solution)/shard_map/all_to_all | solution.py:37
  137.5 0.2 shard_map.85
  137.7 9.9 %all_to_all.67.got = bf16[4,512,128]{2,1,0:T(8,128)(2,1)S(1)} all-to-all(bf16[4,512,128]{2,1,0:T(8,128)(2,1)S(1)} %get-tuple-element.28), channel_id=1, replica_groups=mesh['x_high'=2,'far'=8,'near'=2,'x_low'=2,'y'=4,'core'=2] {'x_high','ne..., dimensions={0} | all-to-all | bytes 1048576 | tf_op jit(solution)/shard_map/all_to_all | solution.py:37
  147.5 0.0 copy-start.5
  147.5 1.1 shard_map.86
  148.6 17.5 %all_to_all.68.got = bf16[16,80,128]{2,1,0:T(8,128)(2,1)S(1)} all-to-all(bf16[16,80,128]{2,1,0:T(8,128)(2,1)S(1)} %shard_map.86), channel_id=1, replica_groups=mesh['x_high'=2,'far'=8,'near'=2,'x_low'=2,'y'=4,'core'=2] {'x_low','y',..., dimensions={0} | all-to-all | bytes 655360 | tf_op jit(solution)/shard_map/all_to_all | solution.py:37
  166.1 0.0 copy-done.5
  166.1 2.4 %shard_map.87 = (f32[64,128]{1,0:T(8,128)S(1)}, f32[64,128]{1,0:T(8,128)S(1)}, f32[32,32]{1,0:T(8,128)S(1)}, f32[32,32]{1,0:T(8,128)S(1)}, f32[32,1,1152]{2,1,0:T(1,128)S(1)}) custom-call(bf16[16,80,128]{2,1,0:T(8,128)(2,1)S(1)} %all_to_all.68.got, f32[64,128]{1,0:T(8,128)S(1)} %get-tuple-element.30.column_sums, f32[64,128]{1,0:T(8,128)S(1)} %bitcast.10, ...), custom_call_target="tpu_custom_call" | custom-call | tf_op jit(solution)/shard_map/pallas_call | solution.py:43
  168.6 12.2 %all_to_all.69.got = f32[32,1,1152]{2,1,0:T(1,128)S(1)} all-to-all(f32[32,1,1152]{2,1,0:T(1,128)S(1)} %get-tuple-element.31), channel_id=1, replica_groups=mesh['x_high'=2,'far'=8,'near'=2,'x_low'=2,'y'=4,'core'=2] {'x_high','x_..., dimensions={0} | all-to-all | bytes 294912 | tf_op jit(solution)/shard_map/all_to_all | solution.py:37
  180.8 15.7 %all_to_all.70.got = f32[16,1,1152]{2,1,0:T(1,128)S(1)} all-to-all(f32[16,1,1152]{2,1,0:T(1,128)S(1)} %shard_map.88), channel_id=1, replica_groups=mesh['x_high'=2,'far'=8,'near'=2,'x_low'=2,'y'=4,'core'=2] {'far','near'}, dimensions={0} | all-to-all | bytes 147456 | tf_op jit(solution)/shard_map/all_to_all | solution.py:37
  196.5 1.8 shard_map.89
  (1 shorter events, 0.0 us)
Async XLA Ops:
  0.6 15.2 %copy-start.6 = (s32[1,1,48]{2,1,0:T(1,128)S(1)}, s32[1,1,48]{2,1,0:T(1,128)}, u32[]{:S(2)}) copy-start(s32[1,1,48]{2,1,0:T(1,128)} %param.8) | copy-start | bytes 580
  0.6 15.2 %copy-start.7 = (s32[1,1,48]{2,1,0:T(1,128)S(1)}, s32[1,1,48]{2,1,0:T(1,128)}, u32[]{:S(2)}) copy-start(s32[1,1,48]{2,1,0:T(1,128)} %param.7) | copy-start | bytes 580
  0.7 0.8 copy-start.1
  2.1 17.4 %all-to-all-start = ((bf16[16,64,128]{2,1,0:T(8,128)(2,1)}), bf16[16,64,128]{2,1,0:T(8,128)(2,1)S(1)}, u32[]{:S(2)}, u32[]{:S(2)}) async-start(bf16[16,64,128]{2,1,0:T(8,128)(2,1)} %shard_map.76), calls=%async_computation | async-start | bytes 524288 | tf_op jit(solution)/shard_map/all_to_all | solution.py:37
  12.3 1.4 copy-start
  13.8 0.8 copy-start.2
  14.5 0.8 copy-start.4
  19.6 12.3 %copy-start.3 = (f32[2,32,128]{2,1,0:T(8,128)S(1)}, f32[2,32,128]{2,1,0:T(8,128)}, u32[]{:S(2)}) copy-start(f32[2,32,128]{2,1,0:T(8,128)} %param.5) | copy-start | bytes 98308
  147.5 18.6 %copy-start.5 = (bf16[2,128,128]{2,1,0:T(8,128)(2,1)S(1)}, bf16[2,128,128]{2,1,0:T(8,128)(2,1)}, u32[]{:S(2)}) copy-start(bf16[2,128,128]{2,1,0:T(8,128)(2,1)} %diagonal.3) | copy-start | bytes 196612
